TPU v7x, 512 devices: a whole 4x8x8 slice. The times are simulated.
512 devices in a mesh: gx: 32 (over y, x), gy: 16 (over z, core).
Axes of the slice: x: 4, y: 8, z: 8, core: 2. Of those that a mesh axis runs over, the one named last changes fastest.
Arguments:
- source: float32 [4, 2048, 4096], P(None, 'gx', 'gy'), may hold values from -8 to 8
- reaction: float32 [2048, 4096], P('gx', 'gy'), may hold values from 0.001 to 0.06
- coupling: float32 [4, 4], replicated, may hold values from -0.025 to 0.015
- solid0: int32 [2048, 4096], P('gx', 'gy'), may hold values 0 or 1
- solid1: int32 [1024, 2048], P('gx', 'gy'), may hold values 0 or 1
- solid2: int32 [512, 1024], P('gx', 'gy'), may hold values 0 or 1
- solid3: int32 [256, 512], P('gx', 'gy'), may hold values 0 or 1
Outputs:
- displacement: float32 [4, 2048, 4096], P(None, 'gx', 'gy')
- residual: float32 [4, 2048, 4096], P(None, 'gx', 'gy')
All inputs are finite; a program needn't handle non-finite values. No bound on the sum of `solid0` or of `solid1` or of `solid2` or of `solid3` on one device may be relied on, other than what follows from the above.
Results may differ from a plain program's by a relative error of at most 0.0003.
Values sent between devices are 32-bit elements; how exact they have to be, the bound alone decides.
No kernel may reach another device: no remote copies, remote signals or barrier semaphores. Data moves between devices by JAX's collectives and lax.ppermute only.
A program may use at most 128 MiB of HBM per device.

v0:
```python
import jax
import jax.numpy as jnp
from jax import lax
from jax.sharding import PartitionSpec as P

CYCLES = 2
SWEEPS = 2
COARSE_SWEEPS = 6


OMEGA = 0.6


def extended(block, sides, width):
    for axis, dim in sides:
        count = lax.axis_size(axis)
        forward = [(i, i + 1) for i in range(count - 1)]
        backward = [(target, source) for source, target in forward]
        low = lax.ppermute(
            lax.slice_in_dim(block, block.shape[dim] - width, None, axis=dim), axis, forward
        )
        high = lax.ppermute(lax.slice_in_dim(block, 0, width, axis=dim), axis, backward)
        block = jnp.concatenate([low, block, high], axis=dim)
    return block


def combine_sides(padded):
    return padded[:, 2:, 1:-1] + padded[:, :-2, 1:-1] + padded[:, 1:-1, 2:] + padded[:, 1:-1, :-2]


def finish(field, sides, solid, react, coupling, scale):
    mixed = jnp.einsum("ab,bxy->axy", coupling, field, precision=lax.Precision.HIGHEST)
    return scale * (4.0 * field - solid * sides) + react * field + mixed


def apply_brick(field, solid, react, coupling, scale):
    padded = extended(solid * field, (("gx", 1), ("gy", 2)), 1)
    return finish(field, combine_sides(padded), solid, react, coupling, scale)


def apply_strip(field, solid, react, coupling, scale):
    sided = extended(solid * field, (("gy", 2),), 1)
    padded = jnp.pad(sided, ((0, 0), (1, 1), (0, 0)))
    return finish(field, combine_sides(padded), solid, react, coupling, scale)


def coarsen(values):
    lead, rows, cols = values.shape
    return values.reshape(lead, rows // 2, 2, cols // 2, 2).mean(axis=(2, 4))


def refine(values):
    return jnp.repeat(jnp.repeat(values, 2, axis=1), 2, axis=2)


def coarsest(rhs, levels, coupling, strip):
    solid, react, scale, divisor = levels[3]
    strip_solid, strip_react, strip_divisor = strip
    whole_rhs = lax.all_gather(rhs, "gx", axis=1, tiled=True)
    field = jnp.zeros_like(whole_rhs)
    for index in range(COARSE_SWEEPS):
        field = (
            field
            + OMEGA
            * (whole_rhs - apply_strip(field, strip_solid, strip_react, coupling, scale))
            / strip_divisor
        )
    leftover = whole_rhs - apply_strip(field, strip_solid, strip_react, coupling, scale)
    field = field + jnp.sum(leftover, axis=1, keepdims=True) / jnp.sum(
        strip_divisor, axis=1, keepdims=True
    )
    rows = rhs.shape[1]
    return lax.dynamic_slice_in_dim(field, lax.axis_index("gx") * rows, rows, 1)


def cycle(level, rhs, field, levels, coupling, strip):
    if level == 3:
        return coarsest(rhs, levels, coupling, strip)
    solid, react, scale, divisor = levels[level]

    def sweep(current):
        return (
            current + OMEGA * (rhs - apply_brick(current, solid, react, coupling, scale)) / divisor
        )

    for index in range(SWEEPS):
        field = sweep(field)
    error = rhs - apply_brick(field, solid, react, coupling, scale)
    coarse_rhs = coarsen(error)
    correction = cycle(level + 1, coarse_rhs, jnp.zeros_like(coarse_rhs), levels, coupling, strip)
    field = field + refine(correction)
    for index in range(SWEEPS):
        field = sweep(field)
    return field


def shards(source, reaction, coupling, solid0, solid1, solid2, solid3):
    masks = [solid0, solid1, solid2, solid3]
    react = reaction[None]
    diagonal = jnp.diagonal(coupling)[:, None, None]
    levels = []
    for level in range(4):
        solid = masks[level].astype(jnp.float32)[None]
        scale = 4.0 ** (-level)
        divisor = 4.0 * scale + react + diagonal
        levels.append((solid, react, scale, divisor))
        react = coarsen(react)
    strip = None
    stacked = jnp.concatenate([levels[3][0], levels[3][1]], axis=0)
    whole = lax.all_gather(stacked, "gx", axis=1, tiled=True)
    strip_solid = whole[0:1]
    strip_react = whole[1:2]
    strip_divisor = 4.0 * levels[3][2] + strip_react + diagonal
    strip = (strip_solid, strip_react, strip_divisor)
    field = jnp.zeros_like(source)
    for index in range(CYCLES):
        field = cycle(0, source, field, levels, coupling, strip)
    residual = source - apply_brick(field, levels[0][0], levels[0][1], coupling, 1.0)
    return (field, residual)


def solution(mesh):
    placed = (
        P(None, "gx", "gy"),
        P("gx", "gy"),
        P(),
        P("gx", "gy"),
        P("gx", "gy"),
        P("gx", "gy"),
        P("gx", "gy"),
    )
    return jax.shard_map(
        shards,
        mesh=mesh,
        in_specs=placed,
        out_specs=(P(None, "gx", "gy"), P(None, "gx", "gy")),
        check_vma=False,
    )
```

profile of v0, /device:TPU:225, one launch (start us, length us, event | category | flops | bytes accessed | tf_op | source)
XLA Modules:
  0.0 879.6 jit_solution(2154272678562209770)
XLA Ops:
  8.5 6.7 collective-permute-start.12
  17.8 6.7 collective-permute-start.24
  25.4 6.3 reshape_broadcast_in_dim.3
  61.0 6.3 collective-permute-start.7
  71.2 6.7 collective-permute-start.8
  105.3 9.5 %reduce_sum.112 = f32[4,32,128]{0,2,1:T(8,128)S(1)} reduce(f32[4,32,2,128,2]{0,4,3,2,1:T(2,128)} %bitcast.647, f32[]{:T(128)} %constant.17.clone.1), dimensions={2,4}, to_apply=%region_0.1 | reduce | flops 49152 | bytes 327684 | tf_op jit(solution)/shard_map/reduce_sum | solution.py:49
  121.1 30.7 %all_gather.10 = f32[2,256,32]{2,1,0:T(8,128)S(1)} all-gather(f32[2,8,32]{2,1,0:T(8,128)S(1)} %pad_maximum_fusion.287), channel_id=1, replica_groups=mesh['gx'=32,'gy'=16] {'gx'}, dimensions={1}, use_global_device_ids=true | all-gather | bytes 67584 | tf_op jit(solution)/shard_map/all_gather | solution.py:110
  151.9 7.0 collective-permute-start.18
  238.3 34.1 %all_gather.9 = f32[4,256,32]{2,0,1:T(4,128)S(1)} all-gather(f32[4,8,32]{2,0,1:T(4,128)S(1)} %copy.178), channel_id=1, replica_groups=mesh['gx'=32,'gy'=16] {'gx'}, dimensions={1}, use_global_device_ids=true | all-gather | bytes 135168 | tf_op jit(solution)/shard_map/all_gather | solution.py:59
  273.1 17.6 %collective-permute-start.38 = (f32[4,256,1]{1,0,2:T(4,128)S(1)}, f32[4,256,1]{1,0,2:T(4,128)S(1)}, u32[]{:S(2)}, u32[]{:S(2)}) collective-permute-start(f32[4,256,1]{1,0,2:T(4,128)S(1)} %get-tuple-element.96), channel_id=1, source_target_pairs={{0,1},{1,2},{2,3},{3,4},{4,5},{5,6},{6,7},{7,8},{8,9},{9,10},{10,1... | collective-permute-start | bytes 12296 | tf_op jit(solution)/shard_map/ppermute | solution.py:19
  373.9 6.8 collective-permute-start.57
  393.8 6.6 collective-permute-start.61
  413.8 6.6 collective-permute-start.65
  434.6 6.6 collective-permute-start.69
  456.1 6.7 collective-permute-start.73
  477.8 6.7 collective-permute-start.77
  499.4 6.7 collective-permute-start.81
  521.0 6.7 collective-permute-start.85
  535.5 9.5 %reduce_sum.120 = f32[4,32,128]{0,2,1:T(8,128)S(1)} reduce(f32[4,32,2,128,2]{0,4,3,2,1:T(2,128)} %bitcast.648, f32[]{:T(128)} %constant.17.clone.1), dimensions={2,4}, to_apply=%region_8.9 | reduce | flops 49152 | bytes 327684 | tf_op jit(solution)/shard_map/reduce_sum | solution.py:49
  557.6 6.9 collective-permute-start.89
  577.7 6.6 collective-permute-start.93
  600.3 6.6 collective-permute-start.97
  620.8 6.6 collective-permute-start.101
  629.4 34.9 %all_gather.11 = f32[4,256,32]{2,0,1:T(4,128)S(1)} all-gather(f32[4,8,32]{2,0,1:T(4,128)S(1)} %copy.211), channel_id=1, replica_groups=mesh['gx'=32,'gy'=16] {'gx'}, dimensions={1}, use_global_device_ids=true | all-gather | bytes 135168 | tf_op jit(solution)/shard_map/all_gather | solution.py:59
  664.7 16.8 %collective-permute-start.102 = (f32[4,256,1]{1,0,2:T(4,128)S(1)}, f32[4,256,1]{1,0,2:T(4,128)S(1)}, u32[]{:S(2)}, u32[]{:S(2)}) collective-permute-start(f32[4,256,1]{1,0,2:T(4,128)S(1)} %get-tuple-element.84), channel_id=1, source_target_pairs={{0,1},{1,2},{2,3},{3,4},{4,5},{5,6},{6,7},{7,8},{8,9},{9,10},{10,1... | collective-permute-start | bytes 12296 | tf_op jit(solution)/shard_map/ppermute | solution.py:19
  739.2 5.7 collective-permute-done.115
  764.7 6.6 collective-permute-start.121
  784.6 6.8 collective-permute-start.125
  804.8 6.6 collective-permute-start.129
  825.5 6.6 collective-permute-start.133
  847.0 6.7 collective-permute-start.137
  868.7 6.7 collective-permute-start.141
  (586 shorter events, 555.8 us)
Async XLA Ops:
  1.5 35.2 %collective-permute-start = (f32[4,1,256]{2,0,1:T(4,128)S(1)}, f32[4,1,256]{2,0,1:T(4,128)S(1)}, u32[]{:S(2)}, u32[]{:S(2)}) collective-permute-start(f32[4,1,256]{2,0,1:T(4,128)S(1)} %mul.527), channel_id=1, source_target_pairs={{16,0},{32,16},{48,32},{64,48},{80,64},{96,80},{112,96},{128,112},... | collective-permute-start | bytes 12296 | tf_op jit(solution)/shard_map/ppermute | solution.py:22
  5.8 30.9 %collective-permute-start.1 = (f32[4,1,256]{2,0,1:T(4,128)S(1)}, f32[4,1,256]{2,0,1:T(4,128)S(1)}, u32[]{:S(2)}, u32[]{:S(2)}) collective-permute-start(f32[4,1,256]{2,0,1:T(4,128)S(1)} %mul.528), channel_id=1, source_target_pairs={{0,16},{16,32},{32,48},{48,64},{64,80},{80,96},{96,112},{112,128},... | collective-permute-start | bytes 12296 | tf_op jit(solution)/shard_map/ppermute | solution.py:19
  8.5 69.4 %collective-permute-start.12 = (f32[4,1,128]{2,0,1:T(4,128)S(1)}, f32[4,1,128]{2,0,1:T(4,128)S(1)}, u32[]{:S(2)}, u32[]{:S(2)}) collective-permute-start(f32[4,1,128]{2,0,1:T(4,128)S(1)} %mul.546), channel_id=1, source_target_pairs={{16,0},{32,16},{48,32},{64,48},{80,64},{96,80},{112,96},{128,112},... | collective-permute-start | bytes 6152 | tf_op jit(solution)/shard_map/ppermute | solution.py:22
  15.2 64.6 %collective-permute-start.13 = (f32[4,1,128]{2,0,1:T(4,128)S(1)}, f32[4,1,128]{2,0,1:T(4,128)S(1)}, u32[]{:S(2)}, u32[]{:S(2)}) collective-permute-start(f32[4,1,128]{2,0,1:T(4,128)S(1)} %mul.547), channel_id=1, source_target_pairs={{0,16},{16,32},{32,48},{48,64},{64,80},{80,96},{96,112},{112,128},... | collective-permute-start | bytes 6152 | tf_op jit(solution)/shard_map/ppermute | solution.py:19
  17.8 153.5 %collective-permute-start.24 = (f32[4,1,64]{2,0,1:T(4,128)S(1)}, f32[4,1,64]{2,0,1:T(4,128)S(1)}, u32[]{:S(2)}, u32[]{:S(2)}) collective-permute-start(f32[4,1,64]{2,0,1:T(4,128)S(1)} %mul.568), channel_id=1, source_target_pairs={{16,0},{32,16},{48,32},{64,48},{80,64},{96,80},{112,96},{128,112},... | collective-permute-start | bytes 3080 | tf_op jit(solution)/shard_map/ppermute | solution.py:22
  37.0 9.9 %collective-permute-start.2 = (f32[4,66,1]{2,0,1:T(4,128)S(1)}, f32[4,66,1]{2,0,1:T(4,128)S(1)}, u32[]{:S(2)}, u32[]{:S(2)}) collective-permute-start(f32[4,66,1]{2,0,1:T(4,128)S(1)} %get-tuple-element.46), channel_id=1, source_target_pairs={{1,0},{2,1},{3,2},{4,3},{5,4},{6,5},{7,6},{8,7},{9,8},{10,9},{11,1... | collective-permute-start | bytes 3176 | tf_op jit(solution)/shard_map/ppermute | solution.py:22
  58.7 9.4 %collective-permute-start.6 = (f32[4,66,1]{2,0,1:T(4,128)S(1)}, f32[4,66,1]{2,0,1:T(4,128)S(1)}, u32[]{:S(2)}, u32[]{:S(2)}) collective-permute-start(f32[4,66,1]{2,0,1:T(4,128)S(1)} %get-tuple-element.44), channel_id=1, source_target_pairs={{1,0},{2,1},{3,2},{4,3},{5,4},{6,5},{7,6},{8,7},{9,8},{10,9},{11,1... | collective-permute-start | bytes 3176 | tf_op jit(solution)/shard_map/ppermute | solution.py:22
  61.0 9.0 %collective-permute-start.7 = (f32[4,66,1]{2,0,1:T(4,128)S(1)}, f32[4,66,1]{2,0,1:T(4,128)S(1)}, u32[]{:S(2)}, u32[]{:S(2)}) collective-permute-start(f32[4,66,1]{2,0,1:T(4,128)S(1)} %get-tuple-element.45), channel_id=1, source_target_pairs={{0,1},{1,2},{2,3},{3,4},{4,5},{5,6},{6,7},{7,8},{8,9},{9,10},{10,1... | collective-permute-start | bytes 3176 | tf_op jit(solution)/shard_map/ppermute | solution.py:19
  68.1 103.3 %collective-permute-start.25 = (f32[4,1,64]{2,0,1:T(4,128)S(1)}, f32[4,1,64]{2,0,1:T(4,128)S(1)}, u32[]{:S(2)}, u32[]{:S(2)}) collective-permute-start(f32[4,1,64]{2,0,1:T(4,128)S(1)} %mul.569), channel_id=1, source_target_pairs={{0,16},{16,32},{32,48},{48,64},{64,80},{80,96},{96,112},{112,128},... | collective-permute-start | bytes 3080 | tf_op jit(solution)/shard_map/ppermute | solution.py:19
  87.7 11.8 %collective-permute-start.11 = (f32[4,66,1]{2,0,1:T(4,128)S(1)}, f32[4,66,1]{2,0,1:T(4,128)S(1)}, u32[]{:S(2)}, u32[]{:S(2)}) collective-permute-start(f32[4,66,1]{2,0,1:T(4,128)S(1)} %get-tuple-element.43), channel_id=1, source_target_pairs={{0,1},{1,2},{2,3},{3,4},{4,5},{5,6},{6,7},{7,8},{8,9},{9,10},{10,1... | collective-permute-start | bytes 3176 | tf_op jit(solution)/shard_map/ppermute | solution.py:19
  92.6 22.8 %collective-permute-start.14 = (f32[4,34,1]{2,0,1:T(4,128)S(1)}, f32[4,34,1]{2,0,1:T(4,128)S(1)}, u32[]{:S(2)}, u32[]{:S(2)}) collective-permute-start(f32[4,34,1]{2,0,1:T(4,128)S(1)} %get-tuple-element.113), channel_id=1, source_target_pairs={{1,0},{2,1},{3,2},{4,3},{5,4},{6,5},{7,6},{8,7},{9,8},{10,9},{11,1... | collective-permute-start | bytes 1640 | tf_op jit(solution)/shard_map/ppermute | solution.py:22
  94.6 20.9 %collective-permute-start.15 = (f32[4,34,1]{2,0,1:T(4,128)S(1)}, f32[4,34,1]{2,0,1:T(4,128)S(1)}, u32[]{:S(2)}, u32[]{:S(2)}) collective-permute-start(f32[4,34,1]{2,0,1:T(4,128)S(1)} %get-tuple-element.114), channel_id=1, source_target_pairs={{0,1},{1,2},{2,3},{3,4},{4,5},{5,6},{6,7},{7,8},{8,9},{9,10},{10,1... | collective-permute-start | bytes 1640 | tf_op jit(solution)/shard_map/ppermute | solution.py:19
  115.8 36.0 %collective-permute-start.16 = (f32[4,1,128]{2,0,1:T(4,128)S(1)}, f32[4,1,128]{2,0,1:T(4,128)S(1)}, u32[]{:S(2)}, u32[]{:S(2)}) collective-permute-start(f32[4,1,128]{2,0,1:T(4,128)S(1)} %get-tuple-element.130), channel_id=1, source_target_pairs={{16,0},{32,16},{48,32},{64,48},{80,64},{96,80},{112,96},{128,112},... | collective-permute-start | bytes 6152 | tf_op jit(solution)/shard_map/ppermute | solution.py:22
  117.7 34.1 %collective-permute-start.17 = (f32[4,1,128]{2,0,1:T(4,128)S(1)}, f32[4,1,128]{2,0,1:T(4,128)S(1)}, u32[]{:S(2)}, u32[]{:S(2)}) collective-permute-start(f32[4,1,128]{2,0,1:T(4,128)S(1)} %get-tuple-element.129), channel_id=1, source_target_pairs={{0,16},{16,32},{32,48},{48,64},{64,80},{80,96},{96,112},{112,128},... | collective-permute-start | bytes 6152 | tf_op jit(solution)/shard_map/ppermute | solution.py:19
  151.9 11.5 %collective-permute-start.18 = (f32[4,34,1]{2,0,1:T(4,128)S(1)}, f32[4,34,1]{2,0,1:T(4,128)S(1)}, u32[]{:S(2)}, u32[]{:S(2)}) collective-permute-start(f32[4,34,1]{2,0,1:T(4,128)S(1)} %get-tuple-element.111), channel_id=1, source_target_pairs={{1,0},{2,1},{3,2},{4,3},{5,4},{6,5},{7,6},{8,7},{9,8},{10,9},{11,1... | collective-permute-start | bytes 1640 | tf_op jit(solution)/shard_map/ppermute | solution.py:22
  177.2 16.7 %collective-permute-start.22 = (f32[4,34,1]{2,0,1:T(4,128)S(1)}, f32[4,34,1]{2,0,1:T(4,128)S(1)}, u32[]{:S(2)}, u32[]{:S(2)}) collective-permute-start(f32[4,34,1]{2,0,1:T(4,128)S(1)} %get-tuple-element.109), channel_id=1, source_target_pairs={{1,0},{2,1},{3,2},{4,3},{5,4},{6,5},{7,6},{8,7},{9,8},{10,9},{11,1... | collective-permute-start | bytes 1640 | tf_op jit(solution)/shard_map/ppermute | solution.py:22
  180.5 13.5 %collective-permute-start.23 = (f32[4,34,1]{2,0,1:T(4,128)S(1)}, f32[4,34,1]{2,0,1:T(4,128)S(1)}, u32[]{:S(2)}, u32[]{:S(2)}) collective-permute-start(f32[4,34,1]{2,0,1:T(4,128)S(1)} %get-tuple-element.110), channel_id=1, source_target_pairs={{0,1},{1,2},{2,3},{3,4},{4,5},{5,6},{6,7},{7,8},{8,9},{9,10},{10,1... | collective-permute-start | bytes 1640 | tf_op jit(solution)/shard_map/ppermute | solution.py:19
  186.7 10.2 %collective-permute-start.26 = (f32[4,18,1]{2,0,1:T(4,128)}, f32[4,18,1]{2,0,1:T(4,128)}, u32[]{:S(2)}, u32[]{:S(2)}) collective-permute-start(f32[4,18,1]{2,0,1:T(4,128)} %get-tuple-element.151), channel_id=1, source_target_pairs={{1,0},{2,1},{3,2},{4,3},{5,4},{6,5},{7,6},{8,7},{9,8},{10,9},{11,1... | collective-permute-start | bytes 872 | tf_op jit(solution)/shard_map/ppermute | solution.py:22
  207.6 11.2 %collective-permute-start.30 = (f32[4,18,1]{2,0,1:T(4,128)S(1)}, f32[4,18,1]{2,0,1:T(4,128)S(1)}, u32[]{:S(2)}, u32[]{:S(2)}) collective-permute-start(f32[4,18,1]{2,0,1:T(4,128)S(1)} %get-tuple-element.149), channel_id=1, source_target_pairs={{1,0},{2,1},{3,2},{4,3},{5,4},{6,5},{7,6},{8,7},{9,8},{10,9},{11,1... | collective-permute-start | bytes 872 | tf_op jit(solution)/shard_map/ppermute | solution.py:22
  209.5 9.2 %collective-permute-start.31 = (f32[4,18,1]{2,0,1:T(4,128)S(1)}, f32[4,18,1]{2,0,1:T(4,128)S(1)}, u32[]{:S(2)}, u32[]{:S(2)}) collective-permute-start(f32[4,18,1]{2,0,1:T(4,128)S(1)} %get-tuple-element.150), channel_id=1, source_target_pairs={{0,1},{1,2},{2,3},{3,4},{4,5},{5,6},{6,7},{7,8},{8,9},{9,10},{10,1... | collective-permute-start | bytes 872 | tf_op jit(solution)/shard_map/ppermute | solution.py:19
  214.4 21.8 %collective-permute-start.36 = (f32[4,256,1]{1,0,2:T(4,128)S(1)}, f32[4,256,1]{1,0,2:T(4,128)S(1)}, u32[]{:S(2)}, u32[]{:S(2)}) collective-permute-start(f32[4,256,1]{1,0,2:T(4,128)S(1)} %mul.590), channel_id=1, source_target_pairs={{0,1},{1,2},{2,3},{3,4},{4,5},{5,6},{6,7},{7,8},{8,9},{9,10},{10,1... | collective-permute-start | bytes 12296 | tf_op jit(solution)/shard_map/ppermute | solution.py:19
  216.3 19.9 %collective-permute-start.37 = (f32[4,256,1]{1,0,2:T(4,128)S(1)}, f32[4,256,1]{1,0,2:T(4,128)S(1)}, u32[]{:S(2)}, u32[]{:S(2)}) collective-permute-start(f32[4,256,1]{1,0,2:T(4,128)S(1)} %mul.592), channel_id=1, source_target_pairs={{1,0},{2,1},{3,2},{4,3},{5,4},{6,5},{7,6},{8,7},{9,8},{10,9},{11,1... | collective-permute-start | bytes 12296 | tf_op jit(solution)/shard_map/ppermute | solution.py:22
  273.1 19.6 %collective-permute-start.38 = (f32[4,256,1]{1,0,2:T(4,128)S(1)}, f32[4,256,1]{1,0,2:T(4,128)S(1)}, u32[]{:S(2)}, u32[]{:S(2)}) collective-permute-start(f32[4,256,1]{1,0,2:T(4,128)S(1)} %get-tuple-element.96), channel_id=1, source_target_pairs={{0,1},{1,2},{2,3},{3,4},{4,5},{5,6},{6,7},{7,8},{8,9},{9,10},{10,1... | collective-permute-start | bytes 12296 | tf_op jit(solution)/shard_map/ppermute | solution.py:19
  432.7 9.3 %collective-permute-start.68 = (f32[4,66,1]{2,0,1:T(4,128)S(1)}, f32[4,66,1]{2,0,1:T(4,128)S(1)}, u32[]{:S(2)}, u32[]{:S(2)}) collective-permute-start(f32[4,66,1]{2,0,1:T(4,128)S(1)} %get-tuple-element.40), channel_id=1, source_target_pairs={{1,0},{2,1},{3,2},{4,3},{5,4},{6,5},{7,6},{8,7},{9,8},{10,9},{11,1... | collective-permute-start | bytes 3176 | tf_op jit(solution)/shard_map/ppermute | solution.py:22
  454.2 9.4 %collective-permute-start.72 = (f32[4,66,1]{2,0,1:T(4,128)S(1)}, f32[4,66,1]{2,0,1:T(4,128)S(1)}, u32[]{:S(2)}, u32[]{:S(2)}) collective-permute-start(f32[4,66,1]{2,0,1:T(4,128)S(1)} %get-tuple-element.38), channel_id=1, source_target_pairs={{1,0},{2,1},{3,2},{4,3},{5,4},{6,5},{7,6},{8,7},{9,8},{10,9},{11,1... | collective-permute-start | bytes 3176 | tf_op jit(solution)/shard_map/ppermute | solution.py:22
  475.8 9.4 %collective-permute-start.76 = (f32[4,66,1]{2,0,1:T(4,128)S(1)}, f32[4,66,1]{2,0,1:T(4,128)S(1)}, u32[]{:S(2)}, u32[]{:S(2)}) collective-permute-start(f32[4,66,1]{2,0,1:T(4,128)S(1)} %get-tuple-element.36), channel_id=1, source_target_pairs={{1,0},{2,1},{3,2},{4,3},{5,4},{6,5},{7,6},{8,7},{9,8},{10,9},{11,1... | collective-permute-start | bytes 3176 | tf_op jit(solution)/shard_map/ppermute | solution.py:22
  497.4 9.4 %collective-permute-start.80 = (f32[4,66,1]{2,0,1:T(4,128)S(1)}, f32[4,66,1]{2,0,1:T(4,128)S(1)}, u32[]{:S(2)}, u32[]{:S(2)}) collective-permute-start(f32[4,66,1]{2,0,1:T(4,128)S(1)} %get-tuple-element.34), channel_id=1, source_target_pairs={{1,0},{2,1},{3,2},{4,3},{5,4},{6,5},{7,6},{8,7},{9,8},{10,9},{11,1... | collective-permute-start | bytes 3176 | tf_op jit(solution)/shard_map/ppermute | solution.py:22
  519.0 9.4 %collective-permute-start.84 = (f32[4,66,1]{2,0,1:T(4,128)S(1)}, f32[4,66,1]{2,0,1:T(4,128)S(1)}, u32[]{:S(2)}, u32[]{:S(2)}) collective-permute-start(f32[4,66,1]{2,0,1:T(4,128)S(1)} %get-tuple-element.32), channel_id=1, source_target_pairs={{1,0},{2,1},{3,2},{4,3},{5,4},{6,5},{7,6},{8,7},{9,8},{10,9},{11,1... | collective-permute-start | bytes 3176 | tf_op jit(solution)/shard_map/ppermute | solution.py:22
  664.7 18.8 %collective-permute-start.102 = (f32[4,256,1]{1,0,2:T(4,128)S(1)}, f32[4,256,1]{1,0,2:T(4,128)S(1)}, u32[]{:S(2)}, u32[]{:S(2)}) collective-permute-start(f32[4,256,1]{1,0,2:T(4,128)S(1)} %get-tuple-element.84), channel_id=1, source_target_pairs={{0,1},{1,2},{2,3},{3,4},{4,5},{5,6},{6,7},{7,8},{8,9},{9,10},{10,1... | collective-permute-start | bytes 12296 | tf_op jit(solution)/shard_map/ppermute | solution.py:19
  823.6 9.3 %collective-permute-start.132 = (f32[4,66,1]{2,0,1:T(4,128)S(1)}, f32[4,66,1]{2,0,1:T(4,128)S(1)}, u32[]{:S(2)}, u32[]{:S(2)}) collective-permute-start(f32[4,66,1]{2,0,1:T(4,128)S(1)} %get-tuple-element.30), channel_id=1, source_target_pairs={{1,0},{2,1},{3,2},{4,3},{5,4},{6,5},{7,6},{8,7},{9,8},{10,9},{11,1... | collective-permute-start | bytes 3176 | tf_op jit(solution)/shard_map/ppermute | solution.py:22
  845.1 9.4 %collective-permute-start.136 = (f32[4,66,1]{2,0,1:T(4,128)S(1)}, f32[4,66,1]{2,0,1:T(4,128)S(1)}, u32[]{:S(2)}, u32[]{:S(2)}) collective-permute-start(f32[4,66,1]{2,0,1:T(4,128)S(1)} %get-tuple-element.28), channel_id=1, source_target_pairs={{1,0},{2,1},{3,2},{4,3},{5,4},{6,5},{7,6},{8,7},{9,8},{10,9},{11,1... | collective-permute-start | bytes 3176 | tf_op jit(solution)/shard_map/ppermute | solution.py:22
  866.7 9.4 %collective-permute-start.140 = (f32[4,66,1]{2,0,1:T(4,128)S(1)}, f32[4,66,1]{2,0,1:T(4,128)S(1)}, u32[]{:S(2)}, u32[]{:S(2)}) collective-permute-start(f32[4,66,1]{2,0,1:T(4,128)S(1)} %get-tuple-element.26), channel_id=1, source_target_pairs={{1,0},{2,1},{3,2},{4,3},{5,4},{6,5},{7,6},{8,7},{9,8},{10,9},{11,1... | collective-permute-start | bytes 3176 | tf_op jit(solution)/shard_map/ppermute | solution.py:22
  (144 other events, 1769.2 us)
where the time goes:
time: 893 us; the launch traced here: 880 us
  starting transfers between devices  494 us (55%)
  waiting for transfers between devices  191 us (21%)
  blocking collectives  99.8 us (11%)
  other arithmetic  34.5 us (4%)
  local copies, waits for them, and re-layouts  30.5 us (3%)
  matrix products  24.9 us (3%)
    ppermute x71, starting transfers between devices, extended(): lax.ppermute(lax.slice_in_dim(block, block.shape[dim] - width, None, axis...  319 us
    ppermute x71, starting transfers between devices, extended(): lax.ppermute(lax.slice_in_dim(block, 0, width, axis=dim), axis, backward)  175 us
    ppermute x71, waiting for transfers between devices, extended(): lax.ppermute(lax.slice_in_dim(block, block.shape[dim] - width, None, axis...  139 us
    all_gather x2, blocking collectives, coarsest(): whole_rhs = lax.all_gather(rhs, 'gx', axis=1, tiled=True)  69.1 us
    ppermute x71, waiting for transfers between devices, extended(): lax.ppermute(lax.slice_in_dim(block, 0, width, axis=dim), axis, backward)  52.1 us
    all_gather x1, blocking collectives, shards(): whole = lax.all_gather(stacked, 'gx', axis=1, tiled=True)  30.7 us
    reduce_sum x9, other arithmetic, coarsen(): return values.reshape(lead, rows // 2, 2, cols // 2, 2).mean(axis=(2, 4))  26.5 us
    dot_general x42, matrix products, finish(): jnp.einsum('ab,bxy->axy', coupling, field, precision=lax.Precision.HIGHEST)  24.9 us
  transfers between devices with their start and end apart: 142, of which 69 were waited for; matrix products, arithmetic and copies ran while one was open for 4% of the time, Pallas kernels for 0%

commit v1 on v0

v1 whole, which is shorter than its diff:
```python
import functools

import jax
import jax.numpy as jnp
from jax import lax
from jax.experimental import pallas as pl
from jax.experimental.pallas import tpu as pltpu
from jax.sharding import PartitionSpec as P


F = 4
ROWS = (8, 4, 2)
COLS = (4, 2, 1)
SCALE = (1.0, 0.25, 0.0625, 0.015625)
OMEGA = 0.6
TILES = 102
XTILES = 64
F32 = jnp.float32
BF16 = jnp.bfloat16


def lanes(shape):
    return lax.broadcasted_iota(jnp.int32, shape, len(shape) - 1)


def sublanes(shape):
    return lax.broadcasted_iota(jnp.int32, shape, len(shape) - 2)


def roll(value, shift, axis):
    size = value.shape[axis]
    shift = shift % size
    return value if shift == 0 else pltpu.roll(value, shift, axis)


def three(value):
    high = value.astype(BF16)
    rest = value - high.astype(F32)
    mid = rest.astype(BF16)
    low = (rest - mid.astype(F32)).astype(BF16)
    return high, mid, low


def exact_dot(value, matrix):
    parts = [jnp.dot(part, matrix, preferred_element_type=F32) for part in three(value)]
    return parts[0] + (parts[1] + parts[2])


def split_matrix(size, stride):
    c = lax.broadcasted_iota(jnp.int32, (size, size), 0)
    o = lax.broadcasted_iota(jnp.int32, (size, size), 1)
    return jnp.where(o == (c % stride) * (size // stride) + c // stride, 1.0, 0.0).astype(BF16)


def join_matrix(size, stride):
    o = lax.broadcasted_iota(jnp.int32, (size, size), 0)
    c = lax.broadcasted_iota(jnp.int32, (size, size), 1)
    return jnp.where(o == (c % stride) * (size // stride) + c // stride, 1.0, 0.0).astype(BF16)


def pack_rows(own, up, dn, count):
    low = sublanes((8, 128)) < 4

    def body(n, _):
        a = own[2 * n]
        b = own[2 * n + 1]
        up[n] = jnp.where(low, a, roll(b, 4, 0))
        dn[n] = jnp.where(low, roll(a, 4, 0), b)
        return _

    lax.fori_loop(0, count // 2, body, 0, unroll=3 if count % 6 == 0 else 4)


def outer_rows(up, dn, n, odd):
    low = sublanes((8, 128)) < 4
    if odd:
        return jnp.where(low, roll(up[n], 4, 0), dn[n])
    return jnp.where(low, up[n], roll(dn[n], 4, 0))


def pack_kernel(source, reaction, solid0, solid1, solid2, solid3, own, up, dn, stage, small):
    matrix = split_matrix(256, 4)
    for a in range(6):
        if a < 4:
            value = exact_dot(source[a], matrix)
        elif a == 4:
            value = exact_dot(reaction[...], matrix)
        else:
            value = jnp.dot(
                solid0[...].astype(F32).astype(BF16), matrix, preferred_element_type=F32
            )
        for h in range(2):
            stage[a, h] = value[:, 128 * h : 128 * h + 128]
    for a in range(6):
        for q in range(8):
            for h in range(2):
                own[a * 16 + q * 2 + h] = stage[a, h, pl.ds(q, 8, stride=8), :]
    small[...] = jnp.dot(
        solid1[...].astype(F32).astype(BF16),
        split_matrix(128, 2),
        preferred_element_type=F32,
    )
    for q in range(4):
        own[96 + q] = small[pl.ds(q, 8, stride=4), :]
    c = lax.broadcasted_iota(jnp.int32, (64, 128), 0)
    o = lax.broadcasted_iota(jnp.int32, (64, 128), 1)
    wide = jnp.where(o % 64 == c, 1.0, 0.0).astype(BF16)
    small[pl.ds(0, 16), :] = jnp.dot(
        solid2[...].astype(F32).astype(BF16), wide, preferred_element_type=F32
    )
    own[100] = jnp.where(
        lanes((8, 128)) < 64,
        small[pl.ds(0, 8, stride=2), :],
        small[pl.ds(1, 8, stride=2), :],
    )
    c = lax.broadcasted_iota(jnp.int32, (32, 128), 0)
    o = lax.broadcasted_iota(jnp.int32, (32, 128), 1)
    twice = jnp.where((o % 64) // 2 == c, 1.0, 0.0)
    own[101] = jnp.dot(
        solid3[...].astype(F32), twice, preferred_element_type=F32,
        precision=lax.Precision.HIGHEST,
    )
    pack_rows(own, up, dn, TILES)


def side_kernel(count, own, up, dn, right, left):
    lane = lanes((8, 128)) % 64

    def group(g, members):
        for v in range(2):
            tiles = []
            for t in range(members):
                index = 3 * g + t
                if v == 0:
                    tiles.append(own[index])
                else:
                    n = index // 2
                    low = sublanes((8, 128)) < 4
                    turn = lax.broadcast(index % 2, (8, 128)) == 1
                    a, b = up[n], dn[n]
                    even = jnp.where(low, a, roll(b, 4, 0))
                    odd = jnp.where(low, roll(a, 4, 0), b)
                    tiles.append(jnp.where(turn, odd, even))
            r, l = tiles[0], tiles[0]
            for t in range(1, members):
                r = jnp.where(lane < 64 - 20 * t, roll(tiles[t], -20 * t, 1), r)
                l = jnp.where(lane >= 20 * t, roll(tiles[t], 20 * t, 1), l)
            right[g, v] = r
            left[g, v] = l

    def body(g, _):
        group(g, 3)
        return _

    lax.fori_loop(0, count // 3, body, 0, unroll=2)
    if count % 3:
        group(jnp.int32(count // 3), count % 3)


def widen(own, up, dn, right, left, index):
    lane = lanes((8, 128))
    g, t = index // 3, index % 3
    out = [[], []]
    for v in range(2):
        mine = own[index] if v == 0 else outer_rows(up, dn, index // 2, index % 2)
        r, l = right[g, v], left[g, v]
        for h in range(2):
            centre = roll(mine, 64 * h, 1)
            before = roll(r, 64 + 20 * t + 64 * h, 1)
            after = roll(l, 64 - 20 * t + 64 * h, 1)
            tile = jnp.where(lane < 64, centre, jnp.where(lane < 84, after, 0.0))
            out[h].append(jnp.where(lane >= 108, before, tile))
    return [jnp.concatenate(pair, axis=0) for pair in out]


def fix_ends(masked, level):
    R, C = ROWS[level], COLS[level]
    for f in range(F):
        for p in range(C):
            masked[f, 0, p + 1] = roll(masked[f, R, p + 1], 1, 0)
            masked[f, R + 1, p + 1] = roll(masked[f, 1, p + 1], -1, 0)


def put_masked(masked, level, f, q, p, value):
    C = COLS[level]
    masked[f, q + 1, p + 1] = value
    if p == 0:
        masked[f, q + 1, C + 1] = roll(value, -1, 1)
    if p == C - 1:
        masked[f, q + 1, 0] = roll(value, 1, 1)


def each_row(count, body):
    if count > 4:
        def step(q, _):
            body(q)
            return _

        lax.fori_loop(0, count, step, 0)
    else:
        for q in range(count):
            body(q)


def drive(level, K, x, masked, rhs, solid, q, p, rows=slice(None)):
    xs = [x[f, q, p, rows] for f in range(F)]
    weight = solid[q, p, rows]
    if level:
        weight = weight * SCALE[level]
    out = []
    for f in range(F):
        near = (masked[f, q, p + 1, rows] + masked[f, q + 2, p + 1, rows]) + (
            masked[f, q + 1, p, rows] + masked[f, q + 1, p + 2, rows]
        )
        total = rhs[f, q, p, rows] + weight * near
        mixed = None
        for b in range(F):
            if b != f:
                term = K[f, b] * xs[b]
                mixed = term if mixed is None else mixed + term
        out.append(total - mixed)
    return out, xs


def sweep(level, K, x, masked, target, rhs, solid, inverse, last=False):
    R, C = ROWS[level], COLS[level]

    def body(q):
        for p in range(C):
            drives, xs = drive(level, K, x, masked, rhs, solid, q, p)
            m = solid[q, p]
            for f in range(F):
                new = (1.0 - OMEGA) * xs[f] + inverse[f, q, p] * drives[f]
                x[f, q, p] = new
                if not last:
                    put_masked(target, level, f, q, p, m * new)

    each_row(R, body)
    if not last:
        fix_ends(target, level)


def first(level, x, masked, rhs, solid, inverse):
    def body(q):
        for p in range(COLS[level]):
            m = solid[q, p]
            for f in range(F):
                new = inverse[f, q, p] * rhs[f, q, p]
                x[f, q, p] = new
                put_masked(masked, level, f, q, p, m * new)

    each_row(ROWS[level], body)
    fix_ends(masked, level)


def mask(level, x, masked, solid):
    def body(q):
        for p in range(COLS[level]):
            m = solid[q, p]
            for f in range(F):
                put_masked(masked, level, f, q, p, m * x[f, q, p])

    each_row(ROWS[level], body)
    fix_ends(masked, level)


def restrict(level, K, x, masked, rhs, solid, react, coarse):
    R, C = ROWS[level], COLS[level]
    wide = 2 if C > 1 else 1

    def body(half):
        for P_ in range(C // wide):
            sums = [None] * F
            for dq in range(2):
                for dp in range(wide):
                    q, p = 2 * half + dq, wide * P_ + dp
                    drives, xs = drive(level, K, x, masked, rhs, solid, q, p)
                    s = react[q, p]
                    for f in range(F):
                        e = drives[f] - (s + (4.0 * SCALE[level] + K[f, f])) * xs[f]
                        sums[f] = e if sums[f] is None else sums[f] + e
            for f in range(F):
                coarse[f, half, P_] = sums[f] * (0.5 / wide)

    each_row(R // 2, body)


def prolong(level, x, masked, solid, source):
    def body(half):
        for dq in range(2):
            q = 2 * half + dq
            for p in range(COLS[level]):
                m = solid[q, p]
                for f in range(F):
                    new = x[f, q, p] + source[f, half, p // 2]
                    x[f, q, p] = new
                    put_masked(masked, level, f, q, p, m * new)

    each_row(ROWS[level] // 2, body)
    fix_ends(masked, level)


def invert(level, K, react, inverse):
    def body(q):
        for p in range(COLS[level]):
            s = react[q, p]
            for f in range(F):
                inverse[f, q, p] = OMEGA / (s + (4.0 * SCALE[level] + K[f, f]))

    each_row(ROWS[level], body)


def decimate():
    k = lax.broadcasted_iota(jnp.int32, (128, 128), 0)
    o = lax.broadcasted_iota(jnp.int32, (128, 128), 1)
    return jnp.where(o == (k // 2 + 10) % 64, 0.5, 0.0).astype(BF16)


def spread(half):
    o = lax.broadcasted_iota(jnp.int32, (128, 128), 0)
    k = lax.broadcasted_iota(jnp.int32, (128, 128), 1)
    return jnp.where(o == (k // 2 + 10) % 64 + 64 * half, 1.0, 0.0).astype(BF16)


def half_pair(a, b):
    return jnp.where(lanes((8, 128)) < 64, a, roll(b, 64, 1))


def descend(K, X, M, RHS, SOLID, REACT, INV):
    for level in range(3):
        a, b = M[level]
        if level:
            first(level, X[level], a, RHS[level], SOLID[level], INV[level])
            sweep(level, K, X[level], a, b, RHS[level], SOLID[level], INV[level])
        if level < 2:
            restrict(
                level, K, X[level], b, RHS[level], SOLID[level], REACT[level], RHS[level + 1]
            )


def coarse_rhs(K, X, M, RHS, SOLID, REACT, three_rhs):
    restrict(2, K, X[2], M[2][1], RHS[2], SOLID[2], REACT[2], three_rhs)
    return [three_rhs[f, 0, 0, 0:8] for f in range(F)]


def down_one(
    K, own, up, dn, right, left,
    x0, r0, s0, m0, i0, x1, r1, s1, m1, i1, x2, r2, s2, m2, i2, payload,
    ma0, mb0, ma1, mb1, ma2, mb2, three_rhs,
):
    for a in range(6):
        for q in range(8):
            for h in range(2):
                pair = widen(own, up, dn, right, left, a * 16 + q * 2 + h)
                for e in range(2):
                    if a < 4:
                        r0[a, q, 2 * h + e] = pair[e]
                    elif a == 4:
                        s0[q, 2 * h + e] = pair[e]
                    else:
                        m0[q, 2 * h + e] = pair[e]
    for q in range(4):
        pair = widen(own, up, dn, right, left, 96 + q)
        m1[q, 0], m1[q, 1] = pair
    pair = widen(own, up, dn, right, left, 100)
    m2[0, 0], m2[1, 0] = pair
    m3 = widen(own, up, dn, right, left, 101)[0]
    for q in range(4):
        for p in range(2):
            s1[q, p] = 0.25 * (
                (s0[2 * q, 2 * p] + s0[2 * q, 2 * p + 1])
                + (s0[2 * q + 1, 2 * p] + s0[2 * q + 1, 2 * p + 1])
            )
    for q in range(2):
        s2[q, 0] = 0.25 * (
            (s1[2 * q, 0] + s1[2 * q, 1]) + (s1[2 * q + 1, 0] + s1[2 * q + 1, 1])
        )
    X, RHS, SOLID, REACT, INV = (x0, x1, x2), (r0, r1, r2), (m0, m1, m2), (s0, s1, s2), (i0, i1, i2)
    M = ((ma0, mb0), (ma1, mb1), (ma2, mb2))
    for level in range(3):
        invert(level, K, REACT[level], INV[level])
    first(0, x0, ma0, r0, m0, i0)
    sweep(0, K, x0, ma0, mb0, r0, m0, i0)
    descend(K, X, M, RHS, SOLID, REACT, INV)
    rest = coarse_rhs(K, X, M, RHS, SOLID, REACT, three_rhs)
    s3 = 0.5 * (s2[0, 0, 0:8] + s2[1, 0, 0:8])
    y = exact_dot(jnp.concatenate(rest + [m3[0:8], s3], axis=0), decimate())
    y = [y[8 * n : 8 * n + 8] for n in range(6)]
    tiles = [half_pair(y[0], y[1]), half_pair(y[2], y[3]), half_pair(y[4], y[5])]
    for d in range(payload.shape[0]):
        for n in range(3):
            payload[d, n] = tiles[n]


def down_two(
    K, own, up, dn, right, left, r0, s0, m0, i0, s1, m1, i1, s2, m2, i2,
    x0, x1, r1, x2, r2, payload,
    ma0, mb0, ma1, mb1, ma2, mb2, three_rhs,
):
    for a in range(F):
        for q in range(8):
            for h in range(2):
                pair = widen(own, up, dn, right, left, a * 16 + q * 2 + h)
                for e in range(2):
                    x0[a, q, 2 * h + e] = pair[e]
    X, RHS, SOLID, REACT, INV = (x0, x1, x2), (r0, r1, r2), (m0, m1, m2), (s0, s1, s2), (i0, i1, i2)
    M = ((ma0, mb0), (ma1, mb1), (ma2, mb2))
    mask(0, x0, mb0, m0)
    sweep(0, K, x0, mb0, ma0, r0, m0, i0)
    sweep(0, K, x0, ma0, mb0, r0, m0, i0)
    descend(K, X, M, RHS, SOLID, REACT, INV)
    rest = coarse_rhs(K, X, M, RHS, SOLID, REACT, three_rhs)
    y = exact_dot(jnp.concatenate(rest + rest[0:2], axis=0), decimate())
    y = [y[8 * n : 8 * n + 8] for n in range(4)]
    tiles = [half_pair(y[0], y[1]), half_pair(y[2], y[3])]
    for d in range(payload.shape[0]):
        for n in range(2):
            payload[d, n] = tiles[n]


def solve_coarsest(K, gathered, statics, natural, x, ma, mb, rhs, solid, react, inverse, wide, correct):
    low = lanes((8, 128)) < 64
    top = sublanes((8, 128)) == 0
    bottom = sublanes((8, 128)) == 7
    c = SCALE[3]
    blocks = gathered.shape[0]
    for d in range(blocks):
        natural[0, pl.ds(8 * d, 8), :] = gathered[d, 0]
        natural[1, pl.ds(8 * d, 8), :] = gathered[d, 1]
        natural[2, pl.ds(8 * d, 8), :] = statics[d, 2]
    diagonal = [jnp.where(low, 4.0 * c + K[2 * n, 2 * n], 4.0 * c + K[2 * n + 1, 2 * n + 1]) for n in range(2)]
    weights = [
        (jnp.where(low, K[0, 1], K[1, 0]), jnp.where(low, K[0, 2], K[1, 3]), jnp.where(low, K[0, 3], K[1, 2])),
        (jnp.where(low, K[2, 3], K[3, 2]), jnp.where(low, K[2, 0], K[3, 1]), jnp.where(low, K[2, 1], K[3, 0])),
    ]
    for t in range(blocks):
        pick = pl.ds(t, 8, stride=blocks)
        both = natural[2, pick, :]
        turned = roll(both, 64, 1)
        m = jnp.where(low, both, turned)
        s = jnp.where(low, turned, both)
        solid[t] = m
        react[t] = s
        for n in range(2):
            r = natural[n, pick, :]
            i = OMEGA / (s + diagonal[n])
            rhs[n, t] = r
            inverse[n, t] = i
            x[n, t] = i * r
            ma[n, t + 1] = m * (i * r)

    def ends(masked):
        for n in range(2):
            masked[n, 0] = jnp.where(top, 0.0, roll(masked[n, blocks], 1, 0))
            masked[n, blocks + 1] = jnp.where(bottom, 0.0, roll(masked[n, 1], -1, 0))

    def drives(t, masked):
        weight = c * solid[t]
        xs = [x[0, t], x[1, t]]
        turned = [roll(v, 64, 1) for v in xs]
        out = []
        for n in range(2):
            here = masked[n, t + 1]
            near = (masked[n, t] + masked[n, t + 2]) + (roll(here, 1, 1) + roll(here, -1, 1))
            u, v, w = weights[n]
            mixed = u * turned[n] + v * xs[1 - n] + w * turned[1 - n]
            out.append(rhs[n, t] + weight * near - mixed)
        return out, xs

    ends(ma)
    for index in range(5):
        source, target = (ma, mb) if index % 2 == 0 else (mb, ma)

        def body(t, _):
            out, xs = drives(t, source)
            m = solid[t]
            for n in range(2):
                new = (1.0 - OMEGA) * xs[n] + inverse[n, t] * out[n]
                x[n, t] = new
                target[n, t + 1] = m * new
            return _

        lax.fori_loop(0, blocks, body, 0, unroll=4)
        ends(target)

    def gather_sums(t, sums):
        out, xs = drives(t, mb)
        s = react[t]
        sums = list(sums)
        for n in range(2):
            g = s + diagonal[n]
            sums[n] = sums[n] + (out[n] - g * xs[n])
            sums[2 + n] = sums[2 + n] + g
        return tuple(sums)

    zero = jnp.zeros((8, 128), F32)
    sums = lax.fori_loop(0, blocks, gather_sums, (zero,) * 4, unroll=4)
    sums = [jnp.sum(v, axis=0, keepdims=True) for v in sums]
    for n in range(2):
        wide[n, pl.ds(0, 8), :] = zero
        wide[n, pl.ds(8 * blocks + 8, 8), :] = zero
        mean = sums[n] / sums[2 + n]
        for t in range(blocks):
            wide[n, pl.ds(8 + t, 8, stride=blocks), :] = x[n, t] + mean
    start = pl.multiple_of(lax.axis_index("gx") * 8, 8)
    rows = []
    for n in range(2):
        rows.append(wide[n, pl.ds(start + 8, 8), :])
        rows.append(
            jnp.where(
                sublanes((8, 128)) < 4,
                wide[n, pl.ds(start + 16, 8), :],
                wide[n, pl.ds(start, 8), :],
            )
        )
    rows = jnp.concatenate(rows, axis=0)
    for half in range(2):
        y = exact_dot(rows, spread(half))
        correct[half, 0, 0] = y[0:16]
        correct[2 + half, 0, 0] = y[16:32]


def ascend(K, X, M, RHS, SOLID, INV, correct, last):
    source = correct
    for level in (2, 1, 0):
        a, b = M[level]
        prolong(level, X[level], a, SOLID[level], source)
        sweep(level, K, X[level], a, b, RHS[level], SOLID[level], INV[level])
        sweep(
            level, K, X[level], b, a, RHS[level], SOLID[level], INV[level],
            last=level > 0 or not last,
        )
        source = X[level]


def copy_state(sources, targets):
    for source, target in zip(sources, targets):
        target[...] = source[...]


def up_one(
    K, gathered, x0i, r0, m0, i0, x1i, r1, m1, i1, x2i, r2, m2, i2,
    own, up, dn,
    x0, x1, x2, ma0, mb0, ma1, mb1, ma2, mb2,
    natural, x3, ma3, mb3, r3, m3, s3, i3, wide, correct,
):
    copy_state((x0i, x1i, x2i), (x0, x1, x2))
    solve_coarsest(K, gathered, gathered, natural, x3, ma3, mb3, r3, m3, s3, i3, wide, correct)
    M = ((ma0, mb0), (ma1, mb1), (ma2, mb2))
    ascend(K, (x0, x1, x2), M, (r0, r1, r2), (m0, m1, m2), (i0, i1, i2), correct, False)
    for f in range(F):
        for q in range(8):
            for h in range(2):
                own[f * 16 + q * 2 + h] = half_pair(
                    x0[f, q, 2 * h, 0:8], x0[f, q, 2 * h + 1, 0:8]
                )
    pack_rows(own, up, dn, XTILES)


def up_two(
    K, gathered, statics, x0i, r0, s0, m0, i0, x1i, r1, m1, i1, x2i, r2, m2, i2,
    displacement, residual,
    x0, x1, x2, ma0, mb0, ma1, mb1, ma2, mb2,
    natural, x3, ma3, mb3, r3, m3, s3, i3, wide, correct, stage,
):
    copy_state((x0i, x1i, x2i), (x0, x1, x2))
    solve_coarsest(K, gathered, statics, natural, x3, ma3, mb3, r3, m3, s3, i3, wide, correct)
    M = ((ma0, mb0), (ma1, mb1), (ma2, mb2))
    ascend(K, (x0, x1, x2), M, (r0, r1, r2), (m0, m1, m2), (i0, i1, i2), correct, True)
    mine = slice(0, 8)
    for q in range(8):
        for h in range(2):
            outs = []
            for p in (2 * h, 2 * h + 1):
                drives, xs = drive(0, K, x0, ma0, r0, m0, q, p, mine)
                s = s0[q, p, mine]
                rest = [drives[f] - (s + (4.0 + K[f, f])) * xs[f] for f in range(F)]
                outs.append(xs + rest)
            for a in range(2 * F):
                stage[a, h, pl.ds(q, 8, stride=8), :] = half_pair(outs[0][a], outs[1][a])
    matrix = join_matrix(256, 4)
    for f in range(F):
        for out, a in ((displacement, f), (residual, F + f)):
            out[f] = exact_dot(jnp.concatenate([stage[a, 0], stage[a, 1]], axis=1), matrix)


def sds(*shape):
    return jax.ShapeDtypeStruct(shape, F32)


def field(level):
    return (F, ROWS[level], COLS[level], 16, 128)


def plane(level):
    return (ROWS[level], COLS[level], 16, 128)


def masked_scratch():
    out = []
    for level in range(3):
        shape = (F, ROWS[level] + 2, COLS[level] + 2, 16, 128)
        out += [pltpu.VMEM(shape, F32), pltpu.VMEM(shape, F32)]
    return out


def coarsest_scratch(blocks):
    return [
        pltpu.VMEM((3, 8 * blocks, 128), F32),
        pltpu.VMEM((2, blocks, 8, 128), F32),
        pltpu.VMEM((2, blocks + 2, 8, 128), F32),
        pltpu.VMEM((2, blocks + 2, 8, 128), F32),
        pltpu.VMEM((2, blocks, 8, 128), F32),
        pltpu.VMEM((blocks, 8, 128), F32),
        pltpu.VMEM((blocks, 8, 128), F32),
        pltpu.VMEM((2, blocks, 8, 128), F32),
        pltpu.VMEM((2, 8 * blocks + 16, 128), F32),
        pltpu.VMEM((F, 1, 1, 16, 128), F32),
    ]


def call(body, outs, scratch, args, smem=True):
    specs = [pl.BlockSpec(memory_space=pltpu.VMEM)] * len(args)
    if smem:
        specs[0] = pl.BlockSpec(memory_space=pltpu.SMEM)
    return pl.pallas_call(
        body,
        out_shape=outs,
        in_specs=specs,
        out_specs=[pl.BlockSpec(memory_space=pltpu.VMEM)] * len(outs),
        scratch_shapes=scratch,
        compiler_params=pltpu.CompilerParams(vmem_limit_bytes=30 * 1024 * 1024),
    )(*args)


def along(axis, down_message, up_message):
    count = lax.axis_size(axis)
    forward = [(i, i + 1) for i in range(count - 1)]
    backward = [(target, source) for source, target in forward]
    return lax.ppermute(down_message, axis, forward), lax.ppermute(up_message, axis, backward)


def exchange(own, up, dn):
    count = own.shape[0]
    dn, up = along("gx", dn, up)
    groups = -(-count // 3)
    right, left = call(
        functools.partial(side_kernel, count),
        [sds(groups, 2, 8, 128)] * 2,
        [],
        (own, up, dn),
        smem=False,
    )
    right, left = along("gy", right, left)
    return own, up, dn, right, left


def shards(source, reaction, coupling, solid0, solid1, solid2, solid3):
    blocks = lax.axis_size("gx")
    packed = call(
        pack_kernel,
        [sds(TILES, 8, 128), sds(TILES // 2, 8, 128), sds(TILES // 2, 8, 128)],
        [pltpu.VMEM((6, 2, 64, 128), F32), pltpu.VMEM((32, 128), F32)],
        (source, reaction, solid0, solid1, solid2, solid3),
        smem=False,
    )
    halo = exchange(*packed)
    shapes = []
    for level in range(3):
        shapes += [sds(*field(level))] * 2 + [sds(*plane(level))] * 2 + [sds(*field(level))]
    state = call(
        down_one,
        shapes + [sds(blocks, 3, 8, 128)],
        masked_scratch() + [pltpu.VMEM((F, 1, 1, 16, 128), F32)],
        (coupling,) + halo,
    )
    x0, r0, s0, m0, i0, x1, r1, s1, m1, i1, x2, r2, s2, m2, i2, payload = state
    statics = lax.all_to_all(payload, "gx", 0, 0)
    inner = [pltpu.VMEM(field(level), F32) for level in range(3)]
    packed = call(
        up_one,
        [sds(XTILES, 8, 128), sds(XTILES // 2, 8, 128), sds(XTILES // 2, 8, 128)],
        inner + masked_scratch() + coarsest_scratch(blocks),
        (coupling, statics, x0, r0, m0, i0, x1, r1, m1, i1, x2, r2, m2, i2),
    )
    halo = exchange(*packed)
    x0, x1, r1, x2, r2, payload = call(
        down_two,
        [sds(*field(0)), sds(*field(1)), sds(*field(1)), sds(*field(2)), sds(*field(2)),
         sds(blocks, 2, 8, 128)],
        masked_scratch() + [pltpu.VMEM((F, 1, 1, 16, 128), F32)],
        (coupling,) + halo + (r0, s0, m0, i0, s1, m1, i1, s2, m2, i2),
    )
    gathered = lax.all_to_all(payload, "gx", 0, 0)
    displacement, residual = call(
        up_two,
        [sds(F, 64, 256), sds(F, 64, 256)],
        inner + masked_scratch() + coarsest_scratch(blocks)
        + [pltpu.VMEM((2 * F, 2, 64, 128), F32)],
        (coupling, gathered, statics, x0, r0, s0, m0, i0, x1, r1, m1, i1, x2, r2, m2, i2),
    )
    return displacement, residual


def solution(mesh):
    placed = (
        P(None, "gx", "gy"),
        P("gx", "gy"),
        P(),
        P("gx", "gy"),
        P("gx", "gy"),
        P("gx", "gy"),
        P("gx", "gy"),
    )
    return jax.shard_map(
        shards,
        mesh=mesh,
        in_specs=placed,
        out_specs=(P(None, "gx", "gy"), P(None, "gx", "gy")),
        check_vma=False,
    )
```

time: 893 us -> 134 us (0.15)
  the two profiles are of different devices: /device:TPU:225 before, /device:TPU:193 now
where the time goes in v1:
time: 134 us; the launch traced here: 133 us
  blocking collectives  46.1 us (34%)
  Pallas kernels  34.6 us (26%)
  starting transfers between devices  28.4 us (21%)
  waiting for transfers between devices  18.6 us (14%)
  local copies, waits for them, and re-layouts  4.72 us (4%)
    pallas_call x7, Pallas kernels, call(): pl.pallas_call(body, out_shape=outs, in_specs=specs, out_specs=[pl.BlockS...  34.6 us
    all_to_all x1, blocking collectives, shards(): statics = lax.all_to_all(payload, 'gx', 0, 0)  25.6 us
    ppermute x4, starting transfers between devices, along(): lax.ppermute(down_message, axis, forward)  22 us
    all_to_all x1, blocking collectives, shards(): gathered = lax.all_to_all(payload, 'gx', 0, 0)  20.5 us
    ppermute x4, waiting for transfers between devices, along(): lax.ppermute(up_message, axis, backward)  14.2 us
    ppermute x4, starting transfers between devices, along(): lax.ppermute(up_message, axis, backward)  6.43 us
    unnamed x14, local copies, waits for them, and re-layouts  4.72 us
    ppermute x4, waiting for transfers between devices, along(): lax.ppermute(down_message, axis, forward)  4.41 us
  transfers between devices with their start and end apart: 8, of which 8 were waited for; matrix products, arithmetic and copies ran while one was open for 0% of the time, Pallas kernels for 0%

profile of v1, /device:TPU:193, one launch (start us, length us, event | category | flops | bytes accessed | tf_op | source)
XLA Modules:
  0.0 133.2 jit_solution(16415971856146882468)
XLA Ops:
  0.6 0.9 copy-done
  1.6 0.8 copy-done.1
  2.4 0.8 copy-done.2
  3.3 0.7 copy-done.4
  4.0 0.7 copy-done.5
  4.7 0.7 copy-done.6
  5.4 0.7 shard_map.86
  6.0 1.3 collective-permute-start
  7.3 4.0 %collective-permute-start.1 = (f32[51,8,128]{2,1,0:T(8,128)S(1)}, f32[51,8,128]{2,1,0:T(8,128)S(1)}, u32[]{:S(2)}, u32[]{:S(2)}) collective-permute-start(f32[51,8,128]{2,1,0:T(8,128)S(1)} %get-tuple-element.36), channel_id=1, source_target_pairs={{0,16},{16,32},{32,48},{48,64},{64,80},{80,96},{96,112},{112,128},... | collective-permute-start | bytes 626696 | tf_op jit(solution)/shard_map/ppermute | solution.py:640
  11.3 2.6 %collective-permute-done.up = f32[51,8,128]{2,1,0:T(8,128)S(1)} collective-permute-done((f32[51,8,128]{2,1,0:T(8,128)S(1)}, f32[51,8,128]{2,1,0:T(8,128)S(1)}, u32[]{:S(2)}, u32[]{:S(2)}) %collective-permute-start) | collective-permute-done | bytes 208928 | tf_op jit(solution)/shard_map/ppermute | solution.py:640
  14.0 0.9 collective-permute-done.1.dn
  14.8 1.7 %shard_map.87 = (f32[34,2,8,128]{3,2,1,0:T(8,128)S(1)}, f32[34,2,8,128]{3,2,1,0:T(8,128)S(1)}) custom-call(f32[102,8,128]{2,1,0:T(8,128)S(1)} %get-tuple-element.34.own, f32[51,8,128]{2,1,0:T(8,128)S(1)} %collective-permute-done.up, f32[51,8,128]{2,1,0:T(8,128)S(1)} %collective-permute-done.1.dn), custom_call_target="tpu_custom_call" | custom-call | tf_op jit(solution)/shard_map/pallas_call | solution.py:626
  16.5 7.0 %collective-permute-start.2 = (f32[34,2,8,128]{3,2,1,0:T(8,128)S(1)}, f32[34,2,8,128]{3,2,1,0:T(8,128)S(1)}, u32[]{:S(2)}, u32[]{:S(2)}) collective-permute-start(f32[34,2,8,128]{3,2,1,0:T(8,128)S(1)} %get-tuple-element.37), channel_id=1, source_target_pairs={{0,1},{1,2},{2,3},{3,4},{4,5},{5,6},{6,7},{7,8},{8,9},{9,10},{10,1... | collective-permute-start | bytes 835592 | tf_op jit(solution)/shard_map/ppermute | solution.py:640
  23.4 1.9 %collective-permute-start.3 = (f32[34,2,8,128]{3,2,1,0:T(8,128)S(1)}, f32[34,2,8,128]{3,2,1,0:T(8,128)S(1)}, u32[]{:S(2)}, u32[]{:S(2)}) collective-permute-start(f32[34,2,8,128]{3,2,1,0:T(8,128)S(1)} %get-tuple-element.38), channel_id=1, source_target_pairs={{1,0},{2,1},{3,2},{4,3},{5,4},{6,5},{7,6},{8,7},{9,8},{10,9},{11,1... | collective-permute-start | bytes 835592 | tf_op jit(solution)/shard_map/ppermute | solution.py:640
  25.4 1.5 %collective-permute-done.2.right = f32[34,2,8,128]{3,2,1,0:T(8,128)S(1)} collective-permute-done((f32[34,2,8,128]{3,2,1,0:T(8,128)S(1)}, f32[34,2,8,128]{3,2,1,0:T(8,128)S(1)}, u32[]{:S(2)}, u32[]{:S(2)}) %collective-permute-start.2) | collective-permute-done | bytes 278560 | tf_op jit(solution)/shard_map/ppermute | solution.py:640
  26.9 5.6 %collective-permute-done.3.left = f32[34,2,8,128]{3,2,1,0:T(8,128)S(1)} collective-permute-done((f32[34,2,8,128]{3,2,1,0:T(8,128)S(1)}, f32[34,2,8,128]{3,2,1,0:T(8,128)S(1)}, u32[]{:S(2)}, u32[]{:S(2)}) %collective-permute-start.3) | collective-permute-done | bytes 278560 | tf_op jit(solution)/shard_map/ppermute | solution.py:640
  32.5 0.0 copy-done.3
  32.5 5.1 %shard_map.88 = (f32[4,8,4,16,128]{4,3,2,1,0:T(8,128)S(1)}, f32[4,8,4,16,128]{4,3,2,1,0:T(8,128)S(1)}, f32[8,4,16,128]{3,2,1,0:T(8,128)S(1)}, f32[8,4,16,128]{3,...) custom-call(f32[4,4]{1,0:T(4,128)S(1)} %copy-done.3, ...), custom_call_target="tpu_custom_call" | custom-call | tf_op jit(solution)/shard_map/pallas_call | solution.py:626
  37.7 25.6 %all_to_all.10.gathered.statics = f32[32,3,8,128]{3,2,1,0:T(8,128)S(1)} all-to-all(f32[32,3,8,128]{3,2,1,0:T(8,128)S(1)} %get-tuple-element.39), channel_id=1, replica_groups=mesh['gx'=32,'gy'=16] {'gx'}, dimensions={0} | all-to-all | bytes 786432 | tf_op jit(solution)/shard_map/all_to_all | solution.py:678
  63.3 9.2 %shard_map.89 = (f32[64,8,128]{2,1,0:T(8,128)S(1)}, f32[32,8,128]{2,1,0:T(8,128)S(1)}, f32[32,8,128]{2,1,0:T(8,128)S(1)}) custom-call(f32[4,4]{1,0:T(4,128)S(1)} %copy-done.3, f32[32,3,8,128]{3,2,1,0:T(8,128)S(1)} %all_to_all.10.gathered.statics, f32[4,8,4,16,128]{4,3,2,1,0:T(8,128)S(1)} %get-tuple-element.40.x0i, ...), custom_call_target="tpu_custom_call" | custom-call | tf_op jit(solution)/shard_map/pallas_call | solution.py:626
  72.4 1.3 collective-permute-start.4
  73.7 4.0 %collective-permute-start.5 = (f32[32,8,128]{2,1,0:T(8,128)S(1)}, f32[32,8,128]{2,1,0:T(8,128)S(1)}, u32[]{:S(2)}, u32[]{:S(2)}) collective-permute-start(f32[32,8,128]{2,1,0:T(8,128)S(1)} %get-tuple-element.54), channel_id=1, source_target_pairs={{0,16},{16,32},{32,48},{48,64},{64,80},{80,96},{96,112},{112,128},... | collective-permute-start | bytes 393224 | tf_op jit(solution)/shard_map/ppermute | solution.py:640
  77.7 0.4 collective-permute-done.4.up
  78.1 1.5 %collective-permute-done.5.dn = f32[32,8,128]{2,1,0:T(8,128)S(1)} collective-permute-done((f32[32,8,128]{2,1,0:T(8,128)S(1)}, f32[32,8,128]{2,1,0:T(8,128)S(1)}, u32[]{:S(2)}, u32[]{:S(2)}) %collective-permute-start.5) | collective-permute-done | bytes 131104 | tf_op jit(solution)/shard_map/ppermute | solution.py:640
  79.6 1.0 shard_map.90
  80.7 7.0 %collective-permute-start.6 = (f32[22,2,8,128]{3,2,1,0:T(8,128)S(1)}, f32[22,2,8,128]{3,2,1,0:T(8,128)S(1)}, u32[]{:S(2)}, u32[]{:S(2)}) collective-permute-start(f32[22,2,8,128]{3,2,1,0:T(8,128)S(1)} %get-tuple-element.55), channel_id=1, source_target_pairs={{0,1},{1,2},{2,3},{3,4},{4,5},{5,6},{6,7},{7,8},{8,9},{9,10},{10,1... | collective-permute-start | bytes 540680 | tf_op jit(solution)/shard_map/ppermute | solution.py:640
  87.7 1.9 %collective-permute-start.7 = (f32[22,2,8,128]{3,2,1,0:T(8,128)S(1)}, f32[22,2,8,128]{3,2,1,0:T(8,128)S(1)}, u32[]{:S(2)}, u32[]{:S(2)}) collective-permute-start(f32[22,2,8,128]{3,2,1,0:T(8,128)S(1)} %get-tuple-element.56), channel_id=1, source_target_pairs={{1,0},{2,1},{3,2},{4,3},{5,4},{6,5},{7,6},{8,7},{9,8},{10,9},{11,1... | collective-permute-start | bytes 540680 | tf_op jit(solution)/shard_map/ppermute | solution.py:640
  89.7 0.5 collective-permute-done.6.right
  90.2 5.6 %collective-permute-done.7.left = f32[22,2,8,128]{3,2,1,0:T(8,128)S(1)} collective-permute-done((f32[22,2,8,128]{3,2,1,0:T(8,128)S(1)}, f32[22,2,8,128]{3,2,1,0:T(8,128)S(1)}, u32[]{:S(2)}, u32[]{:S(2)}) %collective-permute-start.7) | collective-permute-done | bytes 180256 | tf_op jit(solution)/shard_map/ppermute | solution.py:640
  95.8 5.7 %shard_map.91 = (f32[4,8,4,16,128]{4,3,2,1,0:T(8,128)S(1)}, f32[4,4,2,16,128]{4,3,2,1,0:T(8,128)S(1)}, f32[4,4,2,16,128]{4,3,2,1,0:T(8,128)S(1)}, f32[4,2,1,16,1...) custom-call(f32[4,4]{1,0:T(4,128)S(1)} %copy-done.3, ...), custom_call_target="tpu_custom_call" | custom-call | tf_op jit(solution)/shard_map/pallas_call | solution.py:626
  101.5 20.5 %all_to_all.11.gathered = f32[32,2,8,128]{3,2,1,0:T(8,128)S(1)} all-to-all(f32[32,2,8,128]{3,2,1,0:T(8,128)S(1)} %get-tuple-element.60), channel_id=1, replica_groups=mesh['gx'=32,'gy'=16] {'gx'}, dimensions={0} | all-to-all | bytes 524288 | tf_op jit(solution)/shard_map/all_to_all | solution.py:694
  122.0 11.2 %shard_map.92 = (f32[4,64,256]{2,1,0:T(8,128)}, f32[4,64,256]{2,1,0:T(8,128)}) custom-call(f32[4,4]{1,0:T(4,128)S(1)} %copy-done.3, f32[32,2,8,128]{3,2,1,0:T(8,128)S(1)} %all_to_all.11.gathered, f32[32,3,8,128]{3,2,1,0:T(8,128)S(1)} %all_to_all.10.gathered.statics, f32[4,8,4,16,128]{4,3,2,1,0:T(8,128)S(1)} %get-tuple-element.61.x0i, ...), custom_call_target="tpu_custom_call" | custom-call | tf_op jit(solution)/shard_map/pallas_call | solution.py:626
  (7 shorter events, 0.0 us)
Async XLA Ops:
  0.6 1.0 copy-start
  1.6 0.8 copy-start.1
  2.4 0.8 copy-start.2
  3.3 0.7 copy-start.4
  4.0 0.7 copy-start.5
  4.7 0.7 copy-start.6
  6.0 7.9 %collective-permute-start = (f32[51,8,128]{2,1,0:T(8,128)S(1)}, f32[51,8,128]{2,1,0:T(8,128)S(1)}, u32[]{:S(2)}, u32[]{:S(2)}) collective-permute-start(f32[51,8,128]{2,1,0:T(8,128)S(1)} %get-tuple-element.35), channel_id=1, source_target_pairs={{16,0},{32,16},{48,32},{64,48},{80,64},{96,80},{112,96},{128,112},... | collective-permute-start | bytes 626696 | tf_op jit(solution)/shard_map/ppermute | solution.py:640
  7.3 7.5 %collective-permute-start.1 = (f32[51,8,128]{2,1,0:T(8,128)S(1)}, f32[51,8,128]{2,1,0:T(8,128)S(1)}, u32[]{:S(2)}, u32[]{:S(2)}) collective-permute-start(f32[51,8,128]{2,1,0:T(8,128)S(1)} %get-tuple-element.36), channel_id=1, source_target_pairs={{0,16},{16,32},{32,48},{48,64},{64,80},{80,96},{96,112},{112,128},... | collective-permute-start | bytes 626696 | tf_op jit(solution)/shard_map/ppermute | solution.py:640
  16.5 16.1 %copy-start.3 = (f32[4,4]{1,0:T(4,128)S(1)}, f32[4,4]{1,0:T(4,128)}, u32[]{:S(2)}) copy-start(f32[4,4]{1,0:T(4,128)} %K.7) | copy-start | bytes 196
  16.5 10.4 %collective-permute-start.2 = (f32[34,2,8,128]{3,2,1,0:T(8,128)S(1)}, f32[34,2,8,128]{3,2,1,0:T(8,128)S(1)}, u32[]{:S(2)}, u32[]{:S(2)}) collective-permute-start(f32[34,2,8,128]{3,2,1,0:T(8,128)S(1)} %get-tuple-element.37), channel_id=1, source_target_pairs={{0,1},{1,2},{2,3},{3,4},{4,5},{5,6},{6,7},{7,8},{8,9},{9,10},{10,1... | collective-permute-start | bytes 835592 | tf_op jit(solution)/shard_map/ppermute | solution.py:640
  23.4 9.1 %collective-permute-start.3 = (f32[34,2,8,128]{3,2,1,0:T(8,128)S(1)}, f32[34,2,8,128]{3,2,1,0:T(8,128)S(1)}, u32[]{:S(2)}, u32[]{:S(2)}) collective-permute-start(f32[34,2,8,128]{3,2,1,0:T(8,128)S(1)} %get-tuple-element.38), channel_id=1, source_target_pairs={{1,0},{2,1},{3,2},{4,3},{5,4},{6,5},{7,6},{8,7},{9,8},{10,9},{11,1... | collective-permute-start | bytes 835592 | tf_op jit(solution)/shard_map/ppermute | solution.py:640
  72.4 5.7 %collective-permute-start.4 = (f32[32,8,128]{2,1,0:T(8,128)S(1)}, f32[32,8,128]{2,1,0:T(8,128)S(1)}, u32[]{:S(2)}, u32[]{:S(2)}) collective-permute-start(f32[32,8,128]{2,1,0:T(8,128)S(1)} %get-tuple-element.53), channel_id=1, source_target_pairs={{16,0},{32,16},{48,32},{64,48},{80,64},{96,80},{112,96},{128,112},... | collective-permute-start | bytes 393224 | tf_op jit(solution)/shard_map/ppermute | solution.py:640
  73.7 5.9 %collective-permute-start.5 = (f32[32,8,128]{2,1,0:T(8,128)S(1)}, f32[32,8,128]{2,1,0:T(8,128)S(1)}, u32[]{:S(2)}, u32[]{:S(2)}) collective-permute-start(f32[32,8,128]{2,1,0:T(8,128)S(1)} %get-tuple-element.54), channel_id=1, source_target_pairs={{0,16},{16,32},{32,48},{48,64},{64,80},{80,96},{96,112},{112,128},... | collective-permute-start | bytes 393224 | tf_op jit(solution)/shard_map/ppermute | solution.py:640
  80.7 9.5 %collective-permute-start.6 = (f32[22,2,8,128]{3,2,1,0:T(8,128)S(1)}, f32[22,2,8,128]{3,2,1,0:T(8,128)S(1)}, u32[]{:S(2)}, u32[]{:S(2)}) collective-permute-start(f32[22,2,8,128]{3,2,1,0:T(8,128)S(1)} %get-tuple-element.55), channel_id=1, source_target_pairs={{0,1},{1,2},{2,3},{3,4},{4,5},{5,6},{6,7},{7,8},{8,9},{9,10},{10,1... | collective-permute-start | bytes 540680 | tf_op jit(solution)/shard_map/ppermute | solution.py:640
  87.7 8.0 %collective-permute-start.7 = (f32[22,2,8,128]{3,2,1,0:T(8,128)S(1)}, f32[22,2,8,128]{3,2,1,0:T(8,128)S(1)}, u32[]{:S(2)}, u32[]{:S(2)}) collective-permute-start(f32[22,2,8,128]{3,2,1,0:T(8,128)S(1)} %get-tuple-element.56), channel_id=1, source_target_pairs={{1,0},{2,1},{3,2},{4,3},{5,4},{6,5},{7,6},{8,7},{9,8},{10,9},{11,1... | collective-permute-start | bytes 540680 | tf_op jit(solution)/shard_map/ppermute | solution.py:640

commit v2 on v1

--- a/solution.py
+++ b/solution.py
@@ -78,8 +78,28 @@
     return jnp.where(low, up[n], roll(dn[n], 4, 0))
 
 
-def pack_kernel(source, reaction, solid0, solid1, solid2, solid3, own, up, dn, stage, small):
+def pack_kernel(
+    source_in, reaction_in, solid0_in, solid1_in, solid2_in, solid3_in, own, up, dn,
+    source, reaction, solid0, solid1, solid2, solid3, stage, small, arrived,
+):
+    moves = [
+        pltpu.make_async_copy(there, here, arrived.at[n])
+        for n, (there, here) in enumerate(
+            (
+                (source_in, source),
+                (reaction_in, reaction),
+                (solid0_in, solid0),
+                (solid1_in, solid1),
+                (solid2_in, solid2),
+                (solid3_in, solid3),
+            )
+        )
+    ]
+    for move in moves:
+        move.start()
     matrix = split_matrix(256, 4)
+    for move in moves:
+        move.wait()
     for a in range(6):
         if a < 4:
             value = exact_dot(source[a], matrix)
@@ -179,15 +199,13 @@
         for p in range(C):
             masked[f, 0, p + 1] = roll(masked[f, R, p + 1], 1, 0)
             masked[f, R + 1, p + 1] = roll(masked[f, 1, p + 1], -1, 0)
+        for q in range(R):
+            masked[f, q + 1, 0] = roll(masked[f, q + 1, C], 1, 1)
+            masked[f, q + 1, C + 1] = roll(masked[f, q + 1, 1], -1, 1)
 
 
 def put_masked(masked, level, f, q, p, value):
-    C = COLS[level]
     masked[f, q + 1, p + 1] = value
-    if p == 0:
-        masked[f, q + 1, C + 1] = roll(value, -1, 1)
-    if p == C - 1:
-        masked[f, q + 1, 0] = roll(value, 1, 1)
 
 
 def each_row(count, body):
@@ -196,7 +214,7 @@
             body(q)
             return _
 
-        lax.fori_loop(0, count, step, 0)
+        lax.fori_loop(0, count, step, 0, unroll=count)
     else:
         for q in range(count):
             body(q)
@@ -226,14 +244,18 @@
     R, C = ROWS[level], COLS[level]
 
     def body(q):
+        news = []
         for p in range(C):
             drives, xs = drive(level, K, x, masked, rhs, solid, q, p)
-            m = solid[q, p]
+            news.append(
+                [(1.0 - OMEGA) * xs[f] + inverse[f, q, p] * drives[f] for f in range(F)]
+            )
+        for p in range(C):
+            m = None if last else solid[q, p]
             for f in range(F):
-                new = (1.0 - OMEGA) * xs[f] + inverse[f, q, p] * drives[f]
-                x[f, q, p] = new
+                x[f, q, p] = news[p][f]
                 if not last:
-                    put_masked(target, level, f, q, p, m * new)
+                    put_masked(target, level, f, q, p, m * news[p][f])
 
     each_row(R, body)
     if not last:
@@ -480,7 +502,7 @@
                 target[n, t + 1] = m * new
             return _
 
-        lax.fori_loop(0, blocks, body, 0, unroll=4)
+        lax.fori_loop(0, blocks, body, 0, unroll=blocks)
         ends(target)
 
     def gather_sums(t, sums):
@@ -494,7 +516,7 @@
         return tuple(sums)
 
     zero = jnp.zeros((8, 128), F32)
-    sums = lax.fori_loop(0, blocks, gather_sums, (zero,) * 4, unroll=4)
+    sums = lax.fori_loop(0, blocks, gather_sums, (zero,) * 4, unroll=blocks)
     sums = [jnp.sum(v, axis=0, keepdims=True) for v in sums]
     for n in range(2):
         wide[n, pl.ds(0, 8), :] = zero
@@ -619,8 +641,8 @@
     ]
 
 
-def call(body, outs, scratch, args, smem=True):
-    specs = [pl.BlockSpec(memory_space=pltpu.VMEM)] * len(args)
+def call(body, outs, scratch, args, smem=True, space=pltpu.VMEM):
+    specs = [pl.BlockSpec(memory_space=space)] * len(args)
     if smem:
         specs[0] = pl.BlockSpec(memory_space=pltpu.SMEM)
     return pl.pallas_call(
@@ -657,12 +679,19 @@
 
 def shards(source, reaction, coupling, solid0, solid1, solid2, solid3):
     blocks = lax.axis_size("gx")
+    arrays = (source, reaction, solid0, solid1, solid2, solid3)
     packed = call(
         pack_kernel,
         [sds(TILES, 8, 128), sds(TILES // 2, 8, 128), sds(TILES // 2, 8, 128)],
-        [pltpu.VMEM((6, 2, 64, 128), F32), pltpu.VMEM((32, 128), F32)],
-        (source, reaction, solid0, solid1, solid2, solid3),
+        [pltpu.VMEM(array.shape, array.dtype) for array in arrays]
+        + [
+            pltpu.VMEM((6, 2, 64, 128), F32),
+            pltpu.VMEM((32, 128), F32),
+            pltpu.SemaphoreType.DMA((6,)),
+        ],
+        tuple(pltpu.with_memory_space_constraint(array, pltpu.HBM) for array in arrays),
         smem=False,
+        space=pltpu.HBM,
     )
     halo = exchange(*packed)
     shapes = []

time: 134 us -> 116 us (0.87)
  Pallas kernels: 34.6 us -> 21.9 us
  local copies, waits for them, and re-layouts: 4.72 us -> 0.01 us
    pallas_call x7, Pallas kernels: 34.6 us -> 21.9 us  [call(): pl.pallas_call(body, out_shape=outs, in_specs=specs, out_specs=[pl.BlockS...]
    unnamed x14 -> x2, local copies, waits for them, and re-layouts: 4.72 us -> 0.01 us
where the time goes in v2:
time: 116 us
  blocking collectives  46.1 us (40%)
  starting transfers between devices  28.4 us (24%)
  Pallas kernels  21.9 us (19%)
  waiting for transfers between devices  18.6 us (16%)
    all_to_all x1, blocking collectives, shards(): statics = lax.all_to_all(payload, 'gx', 0, 0)  25.6 us
    ppermute x4, starting transfers between devices, along(): lax.ppermute(down_message, axis, forward)  22 us
    pallas_call x7, Pallas kernels, call(): pl.pallas_call(body, out_shape=outs, in_specs=specs, out_specs=[pl.BlockS...  21.9 us
    all_to_all x1, blocking collectives, shards(): gathered = lax.all_to_all(payload, 'gx', 0, 0)  20.5 us
    ppermute x4, waiting for transfers between devices, along(): lax.ppermute(up_message, axis, backward)  14.2 us
    ppermute x4, starting transfers between devices, along(): lax.ppermute(up_message, axis, backward)  6.43 us
    ppermute x4, waiting for transfers between devices, along(): lax.ppermute(down_message, axis, forward)  4.41 us
  transfers between devices with their start and end apart: 8, of which 8 were waited for; matrix products, arithmetic and copies ran while one was open for 0% of the time, Pallas kernels for 0%

profile of v2, /device:TPU:193, one launch (start us, length us, event | category | flops | bytes accessed | tf_op | source)
XLA Modules:
  0.0 115.8 jit_solution(12736014846349994485)
XLA Ops:
  0.6 1.7 %shard_map.86 = (f32[102,8,128]{2,1,0:T(8,128)S(1)}, f32[51,8,128]{2,1,0:T(8,128)S(1)}, f32[51,8,128]{2,1,0:T(8,128)S(1)}) custom-call(f32[4,64,256]{2,1,0:T(8,128)} %source_in.1, f32[64,256]{1,0:T(8,128)} %reaction_in.1, s32[64,256]{1,0:T(8,128)} %solid0_in.1, s32[32,128]{1,0:T(8,128)} %solid1_in.1, s32[16,64]{1,0:T(8,128)} %solid2_in.1, s32[8,32]{1,0:T(8,128)} %solid3_in.1), custom_call_target="tpu_custom_call" | custom-call | tf_op jit(solution)/shard_map/pallas_call | solution.py:648
  2.3 1.3 %collective-permute-start = (f32[51,8,128]{2,1,0:T(8,128)S(1)}, f32[51,8,128]{2,1,0:T(8,128)S(1)}, u32[]{:S(2)}, u32[]{:S(2)}) collective-permute-start(f32[51,8,128]{2,1,0:T(8,128)S(1)} %get-tuple-element.35), channel_id=1, source_target_pairs={{16,0},{32,16},{48,32},{64,48},{80,64},{96,80},{112,96},{128,112},... | collective-permute-start | bytes 626696 | tf_op jit(solution)/shard_map/ppermute | solution.py:662
  3.6 4.0 %collective-permute-start.1 = (f32[51,8,128]{2,1,0:T(8,128)S(1)}, f32[51,8,128]{2,1,0:T(8,128)S(1)}, u32[]{:S(2)}, u32[]{:S(2)}) collective-permute-start(f32[51,8,128]{2,1,0:T(8,128)S(1)} %get-tuple-element.36), channel_id=1, source_target_pairs={{0,16},{16,32},{32,48},{48,64},{64,80},{80,96},{96,112},{112,128},... | collective-permute-start | bytes 626696 | tf_op jit(solution)/shard_map/ppermute | solution.py:662
  7.6 2.6 %collective-permute-done.up = f32[51,8,128]{2,1,0:T(8,128)S(1)} collective-permute-done((f32[51,8,128]{2,1,0:T(8,128)S(1)}, f32[51,8,128]{2,1,0:T(8,128)S(1)}, u32[]{:S(2)}, u32[]{:S(2)}) %collective-permute-start) | collective-permute-done | bytes 208928 | tf_op jit(solution)/shard_map/ppermute | solution.py:662
  10.2 0.9 collective-permute-done.1.dn
  11.1 1.7 %shard_map.87 = (f32[34,2,8,128]{3,2,1,0:T(8,128)S(1)}, f32[34,2,8,128]{3,2,1,0:T(8,128)S(1)}) custom-call(f32[102,8,128]{2,1,0:T(8,128)S(1)} %get-tuple-element.34.own, f32[51,8,128]{2,1,0:T(8,128)S(1)} %collective-permute-done.up, f32[51,8,128]{2,1,0:T(8,128)S(1)} %collective-permute-done.1.dn), custom_call_target="tpu_custom_call" | custom-call | tf_op jit(solution)/shard_map/pallas_call | solution.py:648
  12.7 0.0 copy-start
  12.7 7.0 %collective-permute-start.2 = (f32[34,2,8,128]{3,2,1,0:T(8,128)S(1)}, f32[34,2,8,128]{3,2,1,0:T(8,128)S(1)}, u32[]{:S(2)}, u32[]{:S(2)}) collective-permute-start(f32[34,2,8,128]{3,2,1,0:T(8,128)S(1)} %get-tuple-element.37), channel_id=1, source_target_pairs={{0,1},{1,2},{2,3},{3,4},{4,5},{5,6},{6,7},{7,8},{8,9},{9,10},{10,1... | collective-permute-start | bytes 835592 | tf_op jit(solution)/shard_map/ppermute | solution.py:662
  19.7 1.9 %collective-permute-start.3 = (f32[34,2,8,128]{3,2,1,0:T(8,128)S(1)}, f32[34,2,8,128]{3,2,1,0:T(8,128)S(1)}, u32[]{:S(2)}, u32[]{:S(2)}) collective-permute-start(f32[34,2,8,128]{3,2,1,0:T(8,128)S(1)} %get-tuple-element.38), channel_id=1, source_target_pairs={{1,0},{2,1},{3,2},{4,3},{5,4},{6,5},{7,6},{8,7},{9,8},{10,9},{11,1... | collective-permute-start | bytes 835592 | tf_op jit(solution)/shard_map/ppermute | solution.py:662
  21.6 1.5 %collective-permute-done.2.right = f32[34,2,8,128]{3,2,1,0:T(8,128)S(1)} collective-permute-done((f32[34,2,8,128]{3,2,1,0:T(8,128)S(1)}, f32[34,2,8,128]{3,2,1,0:T(8,128)S(1)}, u32[]{:S(2)}, u32[]{:S(2)}) %collective-permute-start.2) | collective-permute-done | bytes 278560 | tf_op jit(solution)/shard_map/ppermute | solution.py:662
  23.2 5.6 %collective-permute-done.3.left = f32[34,2,8,128]{3,2,1,0:T(8,128)S(1)} collective-permute-done((f32[34,2,8,128]{3,2,1,0:T(8,128)S(1)}, f32[34,2,8,128]{3,2,1,0:T(8,128)S(1)}, u32[]{:S(2)}, u32[]{:S(2)}) %collective-permute-start.3) | collective-permute-done | bytes 278560 | tf_op jit(solution)/shard_map/ppermute | solution.py:662
  28.8 0.0 copy-done
  28.8 3.9 %shard_map.88 = (f32[4,8,4,16,128]{4,3,2,1,0:T(8,128)S(1)}, f32[4,8,4,16,128]{4,3,2,1,0:T(8,128)S(1)}, f32[8,4,16,128]{3,2,1,0:T(8,128)S(1)}, f32[8,4,16,128]{3,...) custom-call(f32[4,4]{1,0:T(4,128)S(1)} %copy-done, ...), custom_call_target="tpu_custom_call" | custom-call | tf_op jit(solution)/shard_map/pallas_call | solution.py:648
  32.7 25.6 %all_to_all.10.gathered.statics = f32[32,3,8,128]{3,2,1,0:T(8,128)S(1)} all-to-all(f32[32,3,8,128]{3,2,1,0:T(8,128)S(1)} %get-tuple-element.39), channel_id=1, replica_groups=mesh['gx'=32,'gy'=16] {'gx'}, dimensions={0} | all-to-all | bytes 786432 | tf_op jit(solution)/shard_map/all_to_all | solution.py:707
  58.3 3.8 %shard_map.89 = (f32[64,8,128]{2,1,0:T(8,128)S(1)}, f32[32,8,128]{2,1,0:T(8,128)S(1)}, f32[32,8,128]{2,1,0:T(8,128)S(1)}) custom-call(f32[4,4]{1,0:T(4,128)S(1)} %copy-done, f32[32,3,8,128]{3,2,1,0:T(8,128)S(1)} %all_to_all.10.gathered.statics, f32[4,8,4,16,128]{4,3,2,1,0:T(8,128)S(1)} %get-tuple-element.40.x0i, ...), custom_call_target="tpu_custom_call" | custom-call | tf_op jit(solution)/shard_map/pallas_call | solution.py:648
  62.1 1.3 %collective-permute-start.4 = (f32[32,8,128]{2,1,0:T(8,128)S(1)}, f32[32,8,128]{2,1,0:T(8,128)S(1)}, u32[]{:S(2)}, u32[]{:S(2)}) collective-permute-start(f32[32,8,128]{2,1,0:T(8,128)S(1)} %get-tuple-element.53), channel_id=1, source_target_pairs={{16,0},{32,16},{48,32},{64,48},{80,64},{96,80},{112,96},{128,112},... | collective-permute-start | bytes 393224 | tf_op jit(solution)/shard_map/ppermute | solution.py:662
  63.4 4.0 %collective-permute-start.5 = (f32[32,8,128]{2,1,0:T(8,128)S(1)}, f32[32,8,128]{2,1,0:T(8,128)S(1)}, u32[]{:S(2)}, u32[]{:S(2)}) collective-permute-start(f32[32,8,128]{2,1,0:T(8,128)S(1)} %get-tuple-element.54), channel_id=1, source_target_pairs={{0,16},{16,32},{32,48},{48,64},{64,80},{80,96},{96,112},{112,128},... | collective-permute-start | bytes 393224 | tf_op jit(solution)/shard_map/ppermute | solution.py:662
  67.4 0.4 collective-permute-done.4.up
  67.8 1.5 %collective-permute-done.5.dn = f32[32,8,128]{2,1,0:T(8,128)S(1)} collective-permute-done((f32[32,8,128]{2,1,0:T(8,128)S(1)}, f32[32,8,128]{2,1,0:T(8,128)S(1)}, u32[]{:S(2)}, u32[]{:S(2)}) %collective-permute-start.5) | collective-permute-done | bytes 131104 | tf_op jit(solution)/shard_map/ppermute | solution.py:662
  69.3 1.0 shard_map.90
  70.4 7.0 %collective-permute-start.6 = (f32[22,2,8,128]{3,2,1,0:T(8,128)S(1)}, f32[22,2,8,128]{3,2,1,0:T(8,128)S(1)}, u32[]{:S(2)}, u32[]{:S(2)}) collective-permute-start(f32[22,2,8,128]{3,2,1,0:T(8,128)S(1)} %get-tuple-element.55), channel_id=1, source_target_pairs={{0,1},{1,2},{2,3},{3,4},{4,5},{5,6},{6,7},{7,8},{8,9},{9,10},{10,1... | collective-permute-start | bytes 540680 | tf_op jit(solution)/shard_map/ppermute | solution.py:662
  77.4 1.9 %collective-permute-start.7 = (f32[22,2,8,128]{3,2,1,0:T(8,128)S(1)}, f32[22,2,8,128]{3,2,1,0:T(8,128)S(1)}, u32[]{:S(2)}, u32[]{:S(2)}) collective-permute-start(f32[22,2,8,128]{3,2,1,0:T(8,128)S(1)} %get-tuple-element.56), channel_id=1, source_target_pairs={{1,0},{2,1},{3,2},{4,3},{5,4},{6,5},{7,6},{8,7},{9,8},{10,9},{11,1... | collective-permute-start | bytes 540680 | tf_op jit(solution)/shard_map/ppermute | solution.py:662
  79.4 0.5 collective-permute-done.6.right
  79.8 5.6 %collective-permute-done.7.left = f32[22,2,8,128]{3,2,1,0:T(8,128)S(1)} collective-permute-done((f32[22,2,8,128]{3,2,1,0:T(8,128)S(1)}, f32[22,2,8,128]{3,2,1,0:T(8,128)S(1)}, u32[]{:S(2)}, u32[]{:S(2)}) %collective-permute-start.7) | collective-permute-done | bytes 180256 | tf_op jit(solution)/shard_map/ppermute | solution.py:662
  85.4 4.2 %shard_map.91 = (f32[4,8,4,16,128]{4,3,2,1,0:T(8,128)S(1)}, f32[4,4,2,16,128]{4,3,2,1,0:T(8,128)S(1)}, f32[4,4,2,16,128]{4,3,2,1,0:T(8,128)S(1)}, f32[4,2,1,16,1...) custom-call(f32[4,4]{1,0:T(4,128)S(1)} %copy-done, ...), custom_call_target="tpu_custom_call" | custom-call | tf_op jit(solution)/shard_map/pallas_call | solution.py:648
  89.6 20.5 %all_to_all.11.gathered = f32[32,2,8,128]{3,2,1,0:T(8,128)S(1)} all-to-all(f32[32,2,8,128]{3,2,1,0:T(8,128)S(1)} %get-tuple-element.60), channel_id=1, replica_groups=mesh['gx'=32,'gy'=16] {'gx'}, dimensions={0} | all-to-all | bytes 524288 | tf_op jit(solution)/shard_map/all_to_all | solution.py:723
  110.1 5.6 %shard_map.92 = (f32[4,64,256]{2,1,0:T(8,128)}, f32[4,64,256]{2,1,0:T(8,128)}) custom-call(f32[4,4]{1,0:T(4,128)S(1)} %copy-done, f32[32,2,8,128]{3,2,1,0:T(8,128)S(1)} %all_to_all.11.gathered, f32[32,3,8,128]{3,2,1,0:T(8,128)S(1)} %all_to_all.10.gathered.statics, f32[4,8,4,16,128]{4,3,2,1,0:T(8,128)S(1)} %get-tuple-element.61.x0i, ...), custom_call_target="tpu_custom_call" | custom-call | tf_op jit(solution)/shard_map/pallas_call | solution.py:648
Async XLA Ops:
  2.3 7.9 %collective-permute-start = (f32[51,8,128]{2,1,0:T(8,128)S(1)}, f32[51,8,128]{2,1,0:T(8,128)S(1)}, u32[]{:S(2)}, u32[]{:S(2)}) collective-permute-start(f32[51,8,128]{2,1,0:T(8,128)S(1)} %get-tuple-element.35), channel_id=1, source_target_pairs={{16,0},{32,16},{48,32},{64,48},{80,64},{96,80},{112,96},{128,112},... | collective-permute-start | bytes 626696 | tf_op jit(solution)/shard_map/ppermute | solution.py:662
  3.6 7.5 %collective-permute-start.1 = (f32[51,8,128]{2,1,0:T(8,128)S(1)}, f32[51,8,128]{2,1,0:T(8,128)S(1)}, u32[]{:S(2)}, u32[]{:S(2)}) collective-permute-start(f32[51,8,128]{2,1,0:T(8,128)S(1)} %get-tuple-element.36), channel_id=1, source_target_pairs={{0,16},{16,32},{32,48},{48,64},{64,80},{80,96},{96,112},{112,128},... | collective-permute-start | bytes 626696 | tf_op jit(solution)/shard_map/ppermute | solution.py:662
  12.7 16.1 %copy-start = (f32[4,4]{1,0:T(4,128)S(1)}, f32[4,4]{1,0:T(4,128)}, u32[]{:S(2)}) copy-start(f32[4,4]{1,0:T(4,128)} %K.7) | copy-start | bytes 196
  12.7 10.4 %collective-permute-start.2 = (f32[34,2,8,128]{3,2,1,0:T(8,128)S(1)}, f32[34,2,8,128]{3,2,1,0:T(8,128)S(1)}, u32[]{:S(2)}, u32[]{:S(2)}) collective-permute-start(f32[34,2,8,128]{3,2,1,0:T(8,128)S(1)} %get-tuple-element.37), channel_id=1, source_target_pairs={{0,1},{1,2},{2,3},{3,4},{4,5},{5,6},{6,7},{7,8},{8,9},{9,10},{10,1... | collective-permute-start | bytes 835592 | tf_op jit(solution)/shard_map/ppermute | solution.py:662
  19.7 9.1 %collective-permute-start.3 = (f32[34,2,8,128]{3,2,1,0:T(8,128)S(1)}, f32[34,2,8,128]{3,2,1,0:T(8,128)S(1)}, u32[]{:S(2)}, u32[]{:S(2)}) collective-permute-start(f32[34,2,8,128]{3,2,1,0:T(8,128)S(1)} %get-tuple-element.38), channel_id=1, source_target_pairs={{1,0},{2,1},{3,2},{4,3},{5,4},{6,5},{7,6},{8,7},{9,8},{10,9},{11,1... | collective-permute-start | bytes 835592 | tf_op jit(solution)/shard_map/ppermute | solution.py:662
  62.1 5.7 %collective-permute-start.4 = (f32[32,8,128]{2,1,0:T(8,128)S(1)}, f32[32,8,128]{2,1,0:T(8,128)S(1)}, u32[]{:S(2)}, u32[]{:S(2)}) collective-permute-start(f32[32,8,128]{2,1,0:T(8,128)S(1)} %get-tuple-element.53), channel_id=1, source_target_pairs={{16,0},{32,16},{48,32},{64,48},{80,64},{96,80},{112,96},{128,112},... | collective-permute-start | bytes 393224 | tf_op jit(solution)/shard_map/ppermute | solution.py:662
  63.4 5.9 %collective-permute-start.5 = (f32[32,8,128]{2,1,0:T(8,128)S(1)}, f32[32,8,128]{2,1,0:T(8,128)S(1)}, u32[]{:S(2)}, u32[]{:S(2)}) collective-permute-start(f32[32,8,128]{2,1,0:T(8,128)S(1)} %get-tuple-element.54), channel_id=1, source_target_pairs={{0,16},{16,32},{32,48},{48,64},{64,80},{80,96},{96,112},{112,128},... | collective-permute-start | bytes 393224 | tf_op jit(solution)/shard_map/ppermute | solution.py:662
  70.4 9.5 %collective-permute-start.6 = (f32[22,2,8,128]{3,2,1,0:T(8,128)S(1)}, f32[22,2,8,128]{3,2,1,0:T(8,128)S(1)}, u32[]{:S(2)}, u32[]{:S(2)}) collective-permute-start(f32[22,2,8,128]{3,2,1,0:T(8,128)S(1)} %get-tuple-element.55), channel_id=1, source_target_pairs={{0,1},{1,2},{2,3},{3,4},{4,5},{5,6},{6,7},{7,8},{8,9},{9,10},{10,1... | collective-permute-start | bytes 540680 | tf_op jit(solution)/shard_map/ppermute | solution.py:662
  77.4 8.0 %collective-permute-start.7 = (f32[22,2,8,128]{3,2,1,0:T(8,128)S(1)}, f32[22,2,8,128]{3,2,1,0:T(8,128)S(1)}, u32[]{:S(2)}, u32[]{:S(2)}) collective-permute-start(f32[22,2,8,128]{3,2,1,0:T(8,128)S(1)} %get-tuple-element.56), channel_id=1, source_target_pairs={{1,0},{2,1},{3,2},{4,3},{5,4},{6,5},{7,6},{8,7},{9,8},{10,9},{11,1... | collective-permute-start | bytes 540680 | tf_op jit(solution)/shard_map/ppermute | solution.py:662

commit v3 on v2

--- a/solution.py
+++ b/solution.py
@@ -15,6 +15,7 @@
 OMEGA = 0.6
 TILES = 102
 XTILES = 64
+MIDDLE = 100
 F32 = jnp.float32
 BF16 = jnp.bfloat16
 
@@ -58,28 +59,39 @@
     return jnp.where(o == (c % stride) * (size // stride) + c // stride, 1.0, 0.0).astype(BF16)
 
 
-def pack_rows(own, up, dn, count):
+def is_even(axis):
+    return lax.broadcast(lax.rem(lax.axis_index(axis), 2), (8, 128)) == 0
+
+
+def meet(after, before, even):
+    return jnp.where(even, after, before), jnp.where(even, before, after)
+
+
+def pack_rows(own, one, two, count):
     low = sublanes((8, 128)) < 4
+    even = is_even("gx")
 
     def body(n, _):
         a = own[2 * n]
         b = own[2 * n + 1]
-        up[n] = jnp.where(low, a, roll(b, 4, 0))
-        dn[n] = jnp.where(low, roll(a, 4, 0), b)
+        up = jnp.where(low, a, roll(b, 4, 0))
+        dn = jnp.where(low, roll(a, 4, 0), b)
+        one[n], two[n] = meet(dn, up, even)
         return _
 
-    lax.fori_loop(0, count // 2, body, 0, unroll=3 if count % 6 == 0 else 4)
-
-
-def outer_rows(up, dn, n, odd):
+    lax.fori_loop(0, count // 2, body, 0, unroll=3)
+
+
+def outer_rows(one, two, n, odd, even):
     low = sublanes((8, 128)) < 4
+    up, dn = meet(one[n], two[n], even)
     if odd:
-        return jnp.where(low, roll(up[n], 4, 0), dn[n])
-    return jnp.where(low, up[n], roll(dn[n], 4, 0))
+        return jnp.where(low, roll(up, 4, 0), dn)
+    return jnp.where(low, up, roll(dn, 4, 0))
 
 
 def pack_kernel(
-    source_in, reaction_in, solid0_in, solid1_in, solid2_in, solid3_in, own, up, dn,
+    source_in, reaction_in, solid0_in, solid1_in, solid2_in, solid3_in, own, one, two,
     source, reaction, solid0, solid1, solid2, solid3, stage, small, arrived,
 ):
     moves = [
@@ -140,56 +152,57 @@
         solid3[...].astype(F32), twice, preferred_element_type=F32,
         precision=lax.Precision.HIGHEST,
     )
-    pack_rows(own, up, dn, TILES)
-
-
-def side_kernel(count, own, up, dn, right, left):
+    pack_rows(own, one, two, TILES)
+
+
+def pack_sides(pick, count, one, two, even):
     lane = lanes((8, 128)) % 64
-
-    def group(g, members):
+    for g in range(-(-count // 3)):
+        members = min(3, count - 3 * g)
         for v in range(2):
-            tiles = []
-            for t in range(members):
-                index = 3 * g + t
-                if v == 0:
-                    tiles.append(own[index])
-                else:
-                    n = index // 2
-                    low = sublanes((8, 128)) < 4
-                    turn = lax.broadcast(index % 2, (8, 128)) == 1
-                    a, b = up[n], dn[n]
-                    even = jnp.where(low, a, roll(b, 4, 0))
-                    odd = jnp.where(low, roll(a, 4, 0), b)
-                    tiles.append(jnp.where(turn, odd, even))
+            tiles = [pick(3 * g + t, v) for t in range(members)]
             r, l = tiles[0], tiles[0]
             for t in range(1, members):
                 r = jnp.where(lane < 64 - 20 * t, roll(tiles[t], -20 * t, 1), r)
                 l = jnp.where(lane >= 20 * t, roll(tiles[t], 20 * t, 1), l)
-            right[g, v] = r
-            left[g, v] = l
-
-    def body(g, _):
-        group(g, 3)
-        return _
-
-    lax.fori_loop(0, count // 3, body, 0, unroll=2)
-    if count % 3:
-        group(jnp.int32(count // 3), count % 3)
-
-
-def widen(own, up, dn, right, left, index):
+            one[g, v], two[g, v] = meet(r, l, even)
+
+
+def side_kernel(count, own, up_one, up_two, one, two):
+    even = is_even("gx")
+
+    def pick(index, v):
+        if v == 0:
+            return own[index]
+        return outer_rows(up_one, up_two, index // 2, index % 2, even)
+
+    pack_sides(pick, count, one, two, is_even("gy"))
+
+
+def sides(one, two, index, v, even):
+    g, t = index // 3, index % 3
+    l, r = meet(one[g, v], two[g, v], even)
+    return [
+        (roll(r, 64 + 20 * t + 64 * h, 1), roll(l, 64 - 20 * t + 64 * h, 1)) for h in range(2)
+    ]
+
+
+def with_sides(centre, before, after):
     lane = lanes((8, 128))
-    g, t = index // 3, index % 3
+    tile = jnp.where(lane < 64, centre, jnp.where(lane < 84, after, 0.0))
+    return jnp.where(lane >= 108, before, tile)
+
+
+def widen(own, row_one, row_two, one, two, index, even_x, even_y):
     out = [[], []]
     for v in range(2):
-        mine = own[index] if v == 0 else outer_rows(up, dn, index // 2, index % 2)
-        r, l = right[g, v], left[g, v]
+        if v == 0:
+            mine = own[index]
+        else:
+            mine = outer_rows(row_one, row_two, index // 2, index % 2, even_x)
+        halo = sides(one, two, index, v, even_y)
         for h in range(2):
-            centre = roll(mine, 64 * h, 1)
-            before = roll(r, 64 + 20 * t + 64 * h, 1)
-            after = roll(l, 64 - 20 * t + 64 * h, 1)
-            tile = jnp.where(lane < 64, centre, jnp.where(lane < 84, after, 0.0))
-            out[h].append(jnp.where(lane >= 108, before, tile))
+            out[h].append(with_sides(roll(mine, 64 * h, 1), *halo[h]))
     return [jnp.concatenate(pair, axis=0) for pair in out]
 
 
@@ -307,6 +320,11 @@
     each_row(R // 2, body)
 
 
+def near_rows(value):
+    outer = jnp.where(sublanes((8, 128)) < 4, value[8:16], value[16:24])
+    return jnp.concatenate([value[0:8], outer], axis=0)
+
+
 def prolong(level, x, masked, solid, source):
     def body(half):
         for dq in range(2):
@@ -314,7 +332,10 @@
             for p in range(COLS[level]):
                 m = solid[q, p]
                 for f in range(F):
-                    new = x[f, q, p] + source[f, half, p // 2]
+                    fix = source[f, half, p // 2]
+                    if fix.shape[0] == 24 and m.shape[0] == 16:
+                        fix = near_rows(fix)
+                    new = x[f, q, p] + fix
                     x[f, q, p] = new
                     put_masked(masked, level, f, q, p, m * new)
 
@@ -365,15 +386,28 @@
     return [three_rhs[f, 0, 0, 0:8] for f in range(F)]
 
 
+def middle_tiles(x1, r1, s1, m1, x2, r2, s2, m2):
+    for level, (x, r, s, m) in ((1, (x1, r1, s1, m1)), (2, (x2, r2, s2, m2))):
+        for q in range(ROWS[level]):
+            for p in range(COLS[level]):
+                for f in range(F):
+                    yield x[f, q, p]
+                    yield r[f, q, p]
+                yield s[q, p]
+                yield m[q, p]
+
+
 def down_one(
-    K, own, up, dn, right, left,
-    x0, r0, s0, m0, i0, x1, r1, s1, m1, i1, x2, r2, s2, m2, i2, payload,
+    K, own, row_one, row_two, one, two,
+    x0, r0, s0, m0, i0, x1, r1, s1, m1, i1, x2, r2, s2, m2, i2, middle, payload,
     ma0, mb0, ma1, mb1, ma2, mb2, three_rhs,
 ):
+    halo = (own, row_one, row_two, one, two)
+    even = (is_even("gx"), is_even("gy"))
     for a in range(6):
         for q in range(8):
             for h in range(2):
-                pair = widen(own, up, dn, right, left, a * 16 + q * 2 + h)
+                pair = widen(*halo, a * 16 + q * 2 + h, *even)
                 for e in range(2):
                     if a < 4:
                         r0[a, q, 2 * h + e] = pair[e]
@@ -382,11 +416,11 @@
                     else:
                         m0[q, 2 * h + e] = pair[e]
     for q in range(4):
-        pair = widen(own, up, dn, right, left, 96 + q)
+        pair = widen(*halo, 96 + q, *even)
         m1[q, 0], m1[q, 1] = pair
-    pair = widen(own, up, dn, right, left, 100)
+    pair = widen(*halo, 100, *even)
     m2[0, 0], m2[1, 0] = pair
-    m3 = widen(own, up, dn, right, left, 101)[0]
+    m3 = widen(*halo, 101, *even)[0]
     for q in range(4):
         for p in range(2):
             s1[q, p] = 0.25 * (
@@ -404,6 +438,8 @@
     first(0, x0, ma0, r0, m0, i0)
     sweep(0, K, x0, ma0, mb0, r0, m0, i0)
     descend(K, X, M, RHS, SOLID, REACT, INV)
+    for n, tile in enumerate(middle_tiles(x1, r1, s1, m1, x2, r2, s2, m2)):
+        middle[n] = tile[0:8]
     rest = coarse_rhs(K, X, M, RHS, SOLID, REACT, three_rhs)
     s3 = 0.5 * (s2[0, 0, 0:8] + s2[1, 0, 0:8])
     y = exact_dot(jnp.concatenate(rest + [m3[0:8], s3], axis=0), decimate())
@@ -415,16 +451,21 @@
 
 
 def down_two(
-    K, own, up, dn, right, left, r0, s0, m0, i0, s1, m1, i1, s2, m2, i2,
+    K, x0i, one, two, r0, s0, m0, i0, s1, m1, i1, s2, m2, i2,
     x0, x1, r1, x2, r2, payload,
     ma0, mb0, ma1, mb1, ma2, mb2, three_rhs,
 ):
+    even = is_even("gy")
     for a in range(F):
         for q in range(8):
             for h in range(2):
-                pair = widen(own, up, dn, right, left, a * 16 + q * 2 + h)
+                halo = [sides(one, two, a * 16 + q * 2 + h, v, even) for v in range(2)]
                 for e in range(2):
-                    x0[a, q, 2 * h + e] = pair[e]
+                    mine = x0i[a, q, 2 * h + e]
+                    x0[a, q, 2 * h + e] = jnp.concatenate(
+                        [with_sides(mine[8 * v : 8 * v + 8], *halo[v][e]) for v in range(2)],
+                        axis=0,
+                    )
     X, RHS, SOLID, REACT, INV = (x0, x1, x2), (r0, r1, r2), (m0, m1, m2), (s0, s1, s2), (i0, i1, i2)
     M = ((ma0, mb0), (ma1, mb1), (ma2, mb2))
     mask(0, x0, mb0, m0)
@@ -525,21 +566,19 @@
         for t in range(blocks):
             wide[n, pl.ds(8 + t, 8, stride=blocks), :] = x[n, t] + mean
     start = pl.multiple_of(lax.axis_index("gx") * 8, 8)
+    low = sublanes((8, 128)) < 4
+    height = correct.shape[-2]
     rows = []
     for n in range(2):
-        rows.append(wide[n, pl.ds(start + 8, 8), :])
-        rows.append(
-            jnp.where(
-                sublanes((8, 128)) < 4,
-                wide[n, pl.ds(start + 16, 8), :],
-                wide[n, pl.ds(start, 8), :],
-            )
-        )
+        mine = wide[n, pl.ds(start + 8, 8), :]
+        after = wide[n, pl.ds(start + 16, 8), :]
+        before = wide[n, pl.ds(start, 8), :]
+        rows += [mine, after, before] if height == 24 else [mine, jnp.where(low, after, before)]
     rows = jnp.concatenate(rows, axis=0)
     for half in range(2):
         y = exact_dot(rows, spread(half))
-        correct[half, 0, 0] = y[0:16]
-        correct[2 + half, 0, 0] = y[16:32]
+        correct[half, 0, 0] = y[0:height]
+        correct[2 + half, 0, 0] = y[height : 2 * height]
 
 
 def ascend(K, X, M, RHS, SOLID, INV, correct, last):
@@ -561,22 +600,42 @@
 
 
 def up_one(
-    K, gathered, x0i, r0, m0, i0, x1i, r1, m1, i1, x2i, r2, m2, i2,
-    own, up, dn,
-    x0, x1, x2, ma0, mb0, ma1, mb1, ma2, mb2,
+    K, gathered, mine, from_one, from_two, x0i, r0, m0, i0,
+    x0, one, two,
+    x1, r1, s1, m1, i1, x2, r2, s2, m2, i2, ma0, mb0, ma1, mb1, ma2, mb2,
     natural, x3, ma3, mb3, r3, m3, s3, i3, wide, correct,
 ):
-    copy_state((x0i, x1i, x2i), (x0, x1, x2))
+    even = is_even("gx")
+    n = 0
+
+    def tall():
+        nonlocal n
+        after, before = meet(from_one[n], from_two[n], even)
+        tile = jnp.concatenate([mine[n], after, before], axis=0)
+        n += 1
+        return tile
+
+    for level, (x, r, s, m) in ((1, (x1, r1, s1, m1)), (2, (x2, r2, s2, m2))):
+        for q in range(ROWS[level]):
+            for p in range(COLS[level]):
+                for f in range(F):
+                    x[f, q, p] = tall()
+                    r[f, q, p] = tall()
+                s[q, p] = tall()
+                m[q, p] = tall()
+    invert(1, K, s1, i1)
+    invert(2, K, s2, i2)
+    x0[...] = x0i[...]
     solve_coarsest(K, gathered, gathered, natural, x3, ma3, mb3, r3, m3, s3, i3, wide, correct)
     M = ((ma0, mb0), (ma1, mb1), (ma2, mb2))
     ascend(K, (x0, x1, x2), M, (r0, r1, r2), (m0, m1, m2), (i0, i1, i2), correct, False)
-    for f in range(F):
-        for q in range(8):
-            for h in range(2):
-                own[f * 16 + q * 2 + h] = half_pair(
-                    x0[f, q, 2 * h, 0:8], x0[f, q, 2 * h + 1, 0:8]
-                )
-    pack_rows(own, up, dn, XTILES)
+
+    def pick(index, v):
+        f, q, h = index // 16, index // 2 % 8, index % 2
+        part = slice(8 * v, 8 * v + 8)
+        return half_pair(x0[f, q, 2 * h, part], x0[f, q, 2 * h + 1, part])
+
+    pack_sides(pick, XTILES, one, two, is_even("gy"))
 
 
 def up_two(
@@ -610,23 +669,24 @@
     return jax.ShapeDtypeStruct(shape, F32)
 
 
-def field(level):
-    return (F, ROWS[level], COLS[level], 16, 128)
-
-
-def plane(level):
-    return (ROWS[level], COLS[level], 16, 128)
-
-
-def masked_scratch():
+def field(level, height=16):
+    return (F, ROWS[level], COLS[level], height, 128)
+
+
+def plane(level, height=16):
+    return (ROWS[level], COLS[level], height, 128)
+
+
+def masked_scratch(height=16):
     out = []
     for level in range(3):
-        shape = (F, ROWS[level] + 2, COLS[level] + 2, 16, 128)
+        tall = height if level else 16
+        shape = (F, ROWS[level] + 2, COLS[level] + 2, tall, 128)
         out += [pltpu.VMEM(shape, F32), pltpu.VMEM(shape, F32)]
     return out
 
 
-def coarsest_scratch(blocks):
+def coarsest_scratch(blocks, height=16):
     return [
         pltpu.VMEM((3, 8 * blocks, 128), F32),
         pltpu.VMEM((2, blocks, 8, 128), F32),
@@ -637,7 +697,7 @@
         pltpu.VMEM((blocks, 8, 128), F32),
         pltpu.VMEM((2, blocks, 8, 128), F32),
         pltpu.VMEM((2, 8 * blocks + 16, 128), F32),
-        pltpu.VMEM((F, 1, 1, 16, 128), F32),
+        pltpu.VMEM((F, 1, 1, height, 128), F32),
     ]
 
 
@@ -655,26 +715,11 @@
     )(*args)
 
 
-def along(axis, down_message, up_message):
+def swap(axis, first, second):
     count = lax.axis_size(axis)
-    forward = [(i, i + 1) for i in range(count - 1)]
-    backward = [(target, source) for source, target in forward]
-    return lax.ppermute(down_message, axis, forward), lax.ppermute(up_message, axis, backward)
-
-
-def exchange(own, up, dn):
-    count = own.shape[0]
-    dn, up = along("gx", dn, up)
-    groups = -(-count // 3)
-    right, left = call(
-        functools.partial(side_kernel, count),
-        [sds(groups, 2, 8, 128)] * 2,
-        [],
-        (own, up, dn),
-        smem=False,
-    )
-    right, left = along("gy", right, left)
-    return own, up, dn, right, left
+    near = [(i, i ^ 1) for i in range(count) if i ^ 1 < count]
+    far = [(i, ((i - 1) ^ 1) + 1) for i in range(1, count) if ((i - 1) ^ 1) + 1 < count]
+    return lax.ppermute(first, axis, near), lax.ppermute(second, axis, far)
 
 
 def shards(source, reaction, coupling, solid0, solid1, solid2, solid3):
@@ -693,32 +738,46 @@
         smem=False,
         space=pltpu.HBM,
     )
-    halo = exchange(*packed)
+    own, one, two = packed
+    rows = swap("gx", one, two)
+    side = call(
+        functools.partial(side_kernel, TILES),
+        [sds(TILES // 3, 2, 8, 128)] * 2,
+        [],
+        (own,) + rows,
+        smem=False,
+    )
+    halo = (own,) + rows + swap("gy", *side)
     shapes = []
     for level in range(3):
         shapes += [sds(*field(level))] * 2 + [sds(*plane(level))] * 2 + [sds(*field(level))]
     state = call(
         down_one,
-        shapes + [sds(blocks, 3, 8, 128)],
+        shapes + [sds(MIDDLE, 8, 128), sds(blocks, 3, 8, 128)],
         masked_scratch() + [pltpu.VMEM((F, 1, 1, 16, 128), F32)],
         (coupling,) + halo,
     )
-    x0, r0, s0, m0, i0, x1, r1, s1, m1, i1, x2, r2, s2, m2, i2, payload = state
+    x0, r0, s0, m0, i0, x1, r1, s1, m1, i1, x2, r2, s2, m2, i2, middle, payload = state
+    near, far = swap("gx", middle, middle)
     statics = lax.all_to_all(payload, "gx", 0, 0)
     inner = [pltpu.VMEM(field(level), F32) for level in range(3)]
-    packed = call(
+    tall = []
+    for level in (1, 2):
+        tall += [pltpu.VMEM(field(level, 24), F32)] * 2
+        tall += [pltpu.VMEM(plane(level, 24), F32)] * 2
+        tall += [pltpu.VMEM(field(level, 24), F32)]
+    x0, one, two = call(
         up_one,
-        [sds(XTILES, 8, 128), sds(XTILES // 2, 8, 128), sds(XTILES // 2, 8, 128)],
-        inner + masked_scratch() + coarsest_scratch(blocks),
-        (coupling, statics, x0, r0, m0, i0, x1, r1, m1, i1, x2, r2, m2, i2),
-    )
-    halo = exchange(*packed)
+        [sds(*field(0))] + [sds(-(-XTILES // 3), 2, 8, 128)] * 2,
+        tall + masked_scratch(24) + coarsest_scratch(blocks, 24),
+        (coupling, statics, middle, near, far, x0, r0, m0, i0),
+    )
     x0, x1, r1, x2, r2, payload = call(
         down_two,
         [sds(*field(0)), sds(*field(1)), sds(*field(1)), sds(*field(2)), sds(*field(2)),
          sds(blocks, 2, 8, 128)],
         masked_scratch() + [pltpu.VMEM((F, 1, 1, 16, 128), F32)],
-        (coupling,) + halo + (r0, s0, m0, i0, s1, m1, i1, s2, m2, i2),
+        (coupling, x0) + swap("gy", one, two) + (r0, s0, m0, i0, s1, m1, i1, s2, m2, i2),
     )
     gathered = lax.all_to_all(payload, "gx", 0, 0)
     displacement, residual = call(

time: 116 us -> 116 us (level)
  blocking collectives: 46.1 us -> 22.4 us
  starting transfers between devices: 28.4 us -> 40.1 us
  local copies, waits for them, and re-layouts: 0.01 us -> 8.26 us
  waiting for transfers between devices: 18.6 us -> 21.9 us
    all_to_all x1 -> x0, blocking collectives: 25.6 us -> none  [shards(): statics = lax.all_to_all(payload, 'gx', 0, 0)]
    all_to_all x0 -> x1, starting transfers between devices: none -> 14 us  [shards(): statics = lax.all_to_all(payload, 'gx', 0, 0)]
    unnamed x2 -> x20, local copies, waits for them, and re-layouts: 0.01 us -> 8.26 us
    ppermute x8, waiting for transfers between devices: 18.6 us -> 21.9 us  [swap(): return (lax.ppermute(first, axis, near), lax.ppermute(second, axis, far))]
    ppermute x8, starting transfers between devices: 28.4 us -> 26.1 us  [swap(): return (lax.ppermute(first, axis, near), lax.ppermute(second, axis, far))]
    all_to_all x1, blocking collectives: 20.5 us -> 22.4 us  [shards(): gathered = lax.all_to_all(payload, 'gx', 0, 0)]
    pallas_call x7 -> x6, Pallas kernels: 21.9 us -> 21.9 us  [call(): pl.pallas_call(body, out_shape=outs, in_specs=specs, out_specs=[pl.BlockS...]
  transfers between devices with their start and end apart: 8 -> 9, of which waited for: 8 -> 4; matrix products, arithmetic and copies ran while one was open for 0% -> 0% of each run, Pallas kernels for 0% -> 0%
where the time goes in v3:
time: 116 us; the launch traced here: 115 us
  starting transfers between devices  40.1 us (35%)
  blocking collectives  22.4 us (19%)
  Pallas kernels  21.9 us (19%)
  waiting for transfers between devices  21.9 us (19%)
  local copies, waits for them, and re-layouts  8.26 us (7%)
    ppermute x8, starting transfers between devices, swap(): return (lax.ppermute(first, axis, near), lax.ppermute(second, axis, far))  26.1 us
    all_to_all x1, blocking collectives, shards(): gathered = lax.all_to_all(payload, 'gx', 0, 0)  22.4 us
    ppermute x8, waiting for transfers between devices, swap(): return (lax.ppermute(first, axis, near), lax.ppermute(second, axis, far))  21.9 us
    pallas_call x6, Pallas kernels, call(): pl.pallas_call(body, out_shape=outs, in_specs=specs, out_specs=[pl.BlockS...  21.9 us
    all_to_all x1, starting transfers between devices, shards(): statics = lax.all_to_all(payload, 'gx', 0, 0)  14 us
    unnamed x20, local copies, waits for them, and re-layouts  8.26 us
  transfers between devices with their start and end apart: 9, of which 4 were waited for; matrix products, arithmetic and copies ran while one was open for 0% of the time, Pallas kernels for 0%

profile of v3, /device:TPU:193, one launch (start us, length us, event | category | flops | bytes accessed | tf_op | source)
XLA Modules:
  0.0 115.3 jit_solution(11107645801152286728)
XLA Ops:
  0.6 1.7 %shard_map.86 = (f32[102,8,128]{2,1,0:T(8,128)S(1)}, f32[51,8,128]{2,1,0:T(8,128)S(1)}, f32[51,8,128]{2,1,0:T(8,128)S(1)}) custom-call(f32[4,64,256]{2,1,0:T(8,128)} %source_in.1, f32[64,256]{1,0:T(8,128)} %reaction_in.1, s32[64,256]{1,0:T(8,128)} %solid0_in.1, s32[32,128]{1,0:T(8,128)} %solid1_in.1, s32[16,64]{1,0:T(8,128)} %solid2_in.1, s32[8,32]{1,0:T(8,128)} %solid3_in.1), custom_call_target="tpu_custom_call" | custom-call | tf_op jit(solution)/shard_map/pallas_call | solution.py:708
  2.3 3.1 %collective-permute-start = (f32[51,8,128]{2,1,0:T(8,128)S(1)}, f32[51,8,128]{2,1,0:T(8,128)S(1)}, u32[]{:S(2)}, u32[]{:S(2)}) collective-permute-start(f32[51,8,128]{2,1,0:T(8,128)S(1)} %get-tuple-element.30), channel_id=1, source_target_pairs={{0,16},{16,0},{32,48},{48,32},{64,80},{80,64},{96,112},{112,96},{1... | collective-permute-start | bytes 626696 | tf_op jit(solution)/shard_map/ppermute | solution.py:722
  5.4 0.7 collective-permute-start.1
  6.1 4.1 %collective-permute-done.up_one.row_one = f32[51,8,128]{2,1,0:T(8,128)S(1)} collective-permute-done((f32[51,8,128]{2,1,0:T(8,128)S(1)}, f32[51,8,128]{2,1,0:T(8,128)S(1)}, u32[]{:S(2)}, u32[]{:S(2)}) %collective-permute-start) | collective-permute-done | bytes 208928 | tf_op jit(solution)/shard_map/ppermute | solution.py:722
  10.2 0.0 collective-permute-done.1.up_two.row_two
  10.2 0.4 shard_map.87
  10.6 0.0 copy-start.9
  10.6 3.5 %collective-permute-start.2 = (f32[34,2,8,128]{3,2,1,0:T(8,128)S(1)}, f32[34,2,8,128]{3,2,1,0:T(8,128)S(1)}, u32[]{:S(2)}, u32[]{:S(2)}) collective-permute-start(f32[34,2,8,128]{3,2,1,0:T(8,128)S(1)} %get-tuple-element.32), channel_id=1, source_target_pairs={{0,1},{1,0},{2,3},{3,2},{4,5},{5,4},{6,7},{7,6},{8,9},{9,8},{10,11... | collective-permute-start | bytes 835592 | tf_op jit(solution)/shard_map/ppermute | solution.py:722
  14.1 5.1 %collective-permute-start.3 = (f32[34,2,8,128]{3,2,1,0:T(8,128)S(1)}, f32[34,2,8,128]{3,2,1,0:T(8,128)S(1)}, u32[]{:S(2)}, u32[]{:S(2)}) collective-permute-start(f32[34,2,8,128]{3,2,1,0:T(8,128)S(1)} %get-tuple-element.33), channel_id=1, source_target_pairs={{1,2},{2,1},{3,4},{4,3},{5,6},{6,5},{7,8},{8,7},{9,10},{10,9},{11,... | collective-permute-start | bytes 835592 | tf_op jit(solution)/shard_map/ppermute | solution.py:722
  19.2 4.2 %collective-permute-done.3.two = f32[34,2,8,128]{3,2,1,0:T(8,128)S(1)} collective-permute-done((f32[34,2,8,128]{3,2,1,0:T(8,128)S(1)}, f32[34,2,8,128]{3,2,1,0:T(8,128)S(1)}, u32[]{:S(2)}, u32[]{:S(2)}) %collective-permute-start.3) | collective-permute-done | bytes 278560 | tf_op jit(solution)/shard_map/ppermute | solution.py:722
  23.4 4.3 %shard_map.88 = (f32[4,8,4,16,128]{4,3,2,1,0:T(8,128)S(1)}, f32[4,8,4,16,128]{4,3,2,1,0:T(8,128)S(1)}, f32[8,4,16,128]{3,2,1,0:T(8,128)S(1)}, f32[8,4,16,128]{3,...) custom-call(f32[4,4]{1,0:T(4,128)S(1)} %copy-done.9, ...), custom_call_target="tpu_custom_call" | custom-call | tf_op jit(solution)/shard_map/pallas_call | solution.py:708
  27.7 1.0 copy-done
  28.7 0.8 copy-done.2
  29.5 0.8 copy-done.8
  30.2 14.0 %all-to-all-start = ((f32[32,3,8,128]{3,2,1,0:T(8,128)}), f32[32,3,8,128]{3,2,1,0:T(8,128)S(1)}, u32[]{:S(2)}, u32[]{:S(2)}) async-start(f32[32,3,8,128]{3,2,1,0:T(8,128)} %copy-done.8), calls=%async_computation | async-start | bytes 786432 | tf_op jit(solution)/shard_map/all_to_all | solution.py:762
  44.2 0.7 collective-permute-start.5
  44.9 5.5 %collective-permute-start.4 = (f32[100,8,128]{2,1,0:T(8,128)}, f32[100,8,128]{2,1,0:T(8,128)S(1)}, u32[]{:S(2)}, u32[]{:S(2)}) collective-permute-start(f32[100,8,128]{2,1,0:T(8,128)} %copy-done.2), channel_id=1, source_target_pairs={{0,16},{16,0},{32,48},{48,32},{64,80},{80,64},{96,112},{112,96},{1... | collective-permute-start | bytes 1228808 | tf_op jit(solution)/shard_map/ppermute | solution.py:722
  50.4 0.0 collective-permute-done.5.from_two
  50.5 0.7 copy-done.4
  51.2 10.6 %collective-permute-done.4.from_one = f32[100,8,128]{2,1,0:T(8,128)S(1)} collective-permute-done((f32[100,8,128]{2,1,0:T(8,128)}, f32[100,8,128]{2,1,0:T(8,128)S(1)}, u32[]{:S(2)}, u32[]{:S(2)}) %collective-permute-start.4) | collective-permute-done | bytes 409632 | tf_op jit(solution)/shard_map/ppermute | solution.py:722
  61.8 0.8 copy-done.6
  62.6 1.2 %copy-done.1 = f32[4,8,4,16,128]{4,3,2,1,0:T(8,128)S(1)} copy-done((f32[4,8,4,16,128]{4,3,2,1,0:T(8,128)S(1)}, f32[4,8,4,16,128]{4,3,2,1,0:T(8,128)}, u32[]{:S(2)}) %copy-start.1) | copy-done | bytes 1048600
  63.8 1.0 copy-done.3
  64.8 1.0 copy-done.5
  65.8 1.0 copy-done.7
  66.8 6.7 %shard_map.89 = (f32[4,8,4,16,128]{4,3,2,1,0:T(8,128)S(1)}, f32[22,2,8,128]{3,2,1,0:T(8,128)S(1)}, f32[22,2,8,128]{3,2,1,0:T(8,128)S(1)}) custom-call(f32[4,4]{1,0:T(4,128)S(1)} %copy-done.9, f32[32,3,8,128]{3,2,1,0:T(8,128)S(1)} %all-to-all-done.gathered.statics, f32[100,8,128]{2,1,0:T(8,128)S(1)} %copy-done.3, f32[100,8,128]{2,1,0:T(8,128)S(1)} %copy-done.7, ...), custom_call_target="tpu_custom_call" | custom-call | tf_op jit(solution)/shard_map/pallas_call | solution.py:708
  73.5 2.3 %collective-permute-start.6 = (f32[22,2,8,128]{3,2,1,0:T(8,128)S(1)}, f32[22,2,8,128]{3,2,1,0:T(8,128)S(1)}, u32[]{:S(2)}, u32[]{:S(2)}) collective-permute-start(f32[22,2,8,128]{3,2,1,0:T(8,128)S(1)} %get-tuple-element.41), channel_id=1, source_target_pairs={{0,1},{1,0},{2,3},{3,2},{4,5},{5,4},{6,7},{7,6},{8,9},{9,8},{10,11... | collective-permute-start | bytes 540680 | tf_op jit(solution)/shard_map/ppermute | solution.py:722
  75.8 5.2 %collective-permute-start.7 = (f32[22,2,8,128]{3,2,1,0:T(8,128)S(1)}, f32[22,2,8,128]{3,2,1,0:T(8,128)S(1)}, u32[]{:S(2)}, u32[]{:S(2)}) collective-permute-start(f32[22,2,8,128]{3,2,1,0:T(8,128)S(1)} %get-tuple-element.42), channel_id=1, source_target_pairs={{1,2},{2,1},{3,4},{4,3},{5,6},{6,5},{7,8},{8,7},{9,10},{10,9},{11,... | collective-permute-start | bytes 540680 | tf_op jit(solution)/shard_map/ppermute | solution.py:722
  81.1 3.0 %collective-permute-done.7.two = f32[22,2,8,128]{3,2,1,0:T(8,128)S(1)} collective-permute-done((f32[22,2,8,128]{3,2,1,0:T(8,128)S(1)}, f32[22,2,8,128]{3,2,1,0:T(8,128)S(1)}, u32[]{:S(2)}, u32[]{:S(2)}) %collective-permute-start.7) | collective-permute-done | bytes 180256 | tf_op jit(solution)/shard_map/ppermute | solution.py:722
  84.0 3.6 %shard_map.90 = (f32[4,8,4,16,128]{4,3,2,1,0:T(8,128)S(1)}, f32[4,4,2,16,128]{4,3,2,1,0:T(8,128)S(1)}, f32[4,4,2,16,128]{4,3,2,1,0:T(8,128)S(1)}, f32[4,2,1,16,1...) custom-call(f32[4,4]{1,0:T(4,128)S(1)} %copy-done.9, ...), custom_call_target="tpu_custom_call" | custom-call | tf_op jit(solution)/shard_map/pallas_call | solution.py:708
  87.6 22.4 %all_to_all.10.gathered = f32[32,2,8,128]{3,2,1,0:T(8,128)S(1)} all-to-all(f32[32,2,8,128]{3,2,1,0:T(8,128)S(1)} %get-tuple-element.50), channel_id=1, replica_groups=mesh['gx'=32,'gy'=16] {'gx'}, dimensions={0} | all-to-all | bytes 524288 | tf_op jit(solution)/shard_map/all_to_all | solution.py:782
  110.0 5.3 %shard_map.91 = (f32[4,64,256]{2,1,0:T(8,128)}, f32[4,64,256]{2,1,0:T(8,128)}) custom-call(f32[4,4]{1,0:T(4,128)S(1)} %copy-done.9, f32[32,2,8,128]{3,2,1,0:T(8,128)S(1)} %all_to_all.10.gathered, f32[32,3,8,128]{3,2,1,0:T(8,128)S(1)} %all-to-all-done.gathered.statics, f32[4,8,4,16,128]{4,3,2,1,0:T(8,128)S(1)} %get-tuple-element.51.x0i, ...), custom_call_target="tpu_custom_call" | custom-call | tf_op jit(solution)/shard_map/pallas_call | solution.py:708
  (13 shorter events, 0.0 us)
Async XLA Ops:
  2.3 7.9 %collective-permute-start = (f32[51,8,128]{2,1,0:T(8,128)S(1)}, f32[51,8,128]{2,1,0:T(8,128)S(1)}, u32[]{:S(2)}, u32[]{:S(2)}) collective-permute-start(f32[51,8,128]{2,1,0:T(8,128)S(1)} %get-tuple-element.30), channel_id=1, source_target_pairs={{0,16},{16,0},{32,48},{48,32},{64,80},{80,64},{96,112},{112,96},{1... | collective-permute-start | bytes 626696 | tf_op jit(solution)/shard_map/ppermute | solution.py:722
  5.4 4.8 %collective-permute-start.1 = (f32[51,8,128]{2,1,0:T(8,128)S(1)}, f32[51,8,128]{2,1,0:T(8,128)S(1)}, u32[]{:S(2)}, u32[]{:S(2)}) collective-permute-start(f32[51,8,128]{2,1,0:T(8,128)S(1)} %get-tuple-element.31), channel_id=1, source_target_pairs={{16,32},{32,16},{48,64},{64,48},{80,96},{96,80},{112,128},{128,112... | collective-permute-start | bytes 626696 | tf_op jit(solution)/shard_map/ppermute | solution.py:722
  10.6 12.8 %copy-start.9 = (f32[4,4]{1,0:T(4,128)S(1)}, f32[4,4]{1,0:T(4,128)}, u32[]{:S(2)}) copy-start(f32[4,4]{1,0:T(4,128)} %K.7) | copy-start | bytes 196
  10.6 8.6 %collective-permute-start.2 = (f32[34,2,8,128]{3,2,1,0:T(8,128)S(1)}, f32[34,2,8,128]{3,2,1,0:T(8,128)S(1)}, u32[]{:S(2)}, u32[]{:S(2)}) collective-permute-start(f32[34,2,8,128]{3,2,1,0:T(8,128)S(1)} %get-tuple-element.32), channel_id=1, source_target_pairs={{0,1},{1,0},{2,3},{3,2},{4,5},{5,4},{6,7},{7,6},{8,9},{9,8},{10,11... | collective-permute-start | bytes 835592 | tf_op jit(solution)/shard_map/ppermute | solution.py:722
  14.1 9.3 %collective-permute-start.3 = (f32[34,2,8,128]{3,2,1,0:T(8,128)S(1)}, f32[34,2,8,128]{3,2,1,0:T(8,128)S(1)}, u32[]{:S(2)}, u32[]{:S(2)}) collective-permute-start(f32[34,2,8,128]{3,2,1,0:T(8,128)S(1)} %get-tuple-element.33), channel_id=1, source_target_pairs={{1,2},{2,1},{3,4},{4,3},{5,6},{6,5},{7,8},{8,7},{9,10},{10,9},{11,... | collective-permute-start | bytes 835592 | tf_op jit(solution)/shard_map/ppermute | solution.py:722
  27.7 1.0 copy-start
  28.7 0.8 copy-start.2
  29.5 0.8 copy-start.8
  30.2 32.3 %all-to-all-start = ((f32[32,3,8,128]{3,2,1,0:T(8,128)}), f32[32,3,8,128]{3,2,1,0:T(8,128)S(1)}, u32[]{:S(2)}, u32[]{:S(2)}) async-start(f32[32,3,8,128]{3,2,1,0:T(8,128)} %copy-done.8), calls=%async_computation | async-start | bytes 786432 | tf_op jit(solution)/shard_map/all_to_all | solution.py:762
  44.2 6.2 %collective-permute-start.5 = (f32[100,8,128]{2,1,0:T(8,128)}, f32[100,8,128]{2,1,0:T(8,128)S(1)}, u32[]{:S(2)}, u32[]{:S(2)}) collective-permute-start(f32[100,8,128]{2,1,0:T(8,128)} %copy-done.2), channel_id=1, source_target_pairs={{16,32},{32,16},{48,64},{64,48},{80,96},{96,80},{112,128},{128,112... | collective-permute-start | bytes 1228808 | tf_op jit(solution)/shard_map/ppermute | solution.py:722
  44.9 16.9 %collective-permute-start.4 = (f32[100,8,128]{2,1,0:T(8,128)}, f32[100,8,128]{2,1,0:T(8,128)S(1)}, u32[]{:S(2)}, u32[]{:S(2)}) collective-permute-start(f32[100,8,128]{2,1,0:T(8,128)} %copy-done.2), channel_id=1, source_target_pairs={{0,16},{16,0},{32,48},{48,32},{64,80},{80,64},{96,112},{112,96},{1... | collective-permute-start | bytes 1228808 | tf_op jit(solution)/shard_map/ppermute | solution.py:722
  50.5 0.8 copy-start.4
  61.8 0.8 copy-start.6
  62.6 1.2 %copy-start.1 = (f32[4,8,4,16,128]{4,3,2,1,0:T(8,128)S(1)}, f32[4,8,4,16,128]{4,3,2,1,0:T(8,128)}, u32[]{:S(2)}) copy-start(f32[4,8,4,16,128]{4,3,2,1,0:T(8,128)} %copy-done) | copy-start | bytes 3145732
  63.8 1.0 copy-start.3
  64.8 1.0 copy-start.5
  65.8 1.0 copy-start.7
  73.5 7.5 %collective-permute-start.6 = (f32[22,2,8,128]{3,2,1,0:T(8,128)S(1)}, f32[22,2,8,128]{3,2,1,0:T(8,128)S(1)}, u32[]{:S(2)}, u32[]{:S(2)}) collective-permute-start(f32[22,2,8,128]{3,2,1,0:T(8,128)S(1)} %get-tuple-element.41), channel_id=1, source_target_pairs={{0,1},{1,0},{2,3},{3,2},{4,5},{5,4},{6,7},{7,6},{8,9},{9,8},{10,11... | collective-permute-start | bytes 540680 | tf_op jit(solution)/shard_map/ppermute | solution.py:722
  75.8 8.2 %collective-permute-start.7 = (f32[22,2,8,128]{3,2,1,0:T(8,128)S(1)}, f32[22,2,8,128]{3,2,1,0:T(8,128)S(1)}, u32[]{:S(2)}, u32[]{:S(2)}) collective-permute-start(f32[22,2,8,128]{3,2,1,0:T(8,128)S(1)} %get-tuple-element.42), channel_id=1, source_target_pairs={{1,2},{2,1},{3,4},{4,3},{5,6},{6,5},{7,8},{8,7},{9,10},{10,9},{11,... | collective-permute-start | bytes 540680 | tf_op jit(solution)/shard_map/ppermute | solution.py:722

commit v4 on v3

--- a/solution.py
+++ b/solution.py
@@ -15,7 +15,8 @@
 OMEGA = 0.6
 TILES = 102
 XTILES = 64
-MIDDLE = 100
+MIDDLE = 30
+STATE = 15
 F32 = jnp.float32
 BF16 = jnp.bfloat16
 
@@ -386,22 +387,74 @@
     return [three_rhs[f, 0, 0, 0:8] for f in range(F)]
 
 
-def middle_tiles(x1, r1, s1, m1, x2, r2, s2, m2):
-    for level, (x, r, s, m) in ((1, (x1, r1, s1, m1)), (2, (x2, r2, s2, m2))):
+def levels_one_two(state_one, state_two):
+    out = []
+    for level, (x, r, s, m) in ((1, state_one), (2, state_two)):
+        keys = []
         for q in range(ROWS[level]):
             for p in range(COLS[level]):
                 for f in range(F):
-                    yield x[f, q, p]
-                    yield r[f, q, p]
-                yield s[q, p]
-                yield m[q, p]
-
-
-def down_one(
-    K, own, row_one, row_two, one, two,
-    x0, r0, s0, m0, i0, x1, r1, s1, m1, i1, x2, r2, s2, m2, i2, middle, payload,
-    ma0, mb0, ma1, mb1, ma2, mb2, three_rhs,
-):
+                    keys.append((x, (f, q, p)))
+                    keys.append((r, (f, q, p)))
+                keys.append((s, (q, p)))
+                keys.append((m, (q, p)))
+        out.append(keys)
+    return out
+
+
+TAKE = ((3, 2), (2, 4))
+
+
+def pack_middle(keys, middle):
+    sub = sublanes((8, 128))
+    place = 0
+    for (start, size), members in zip(TAKE, keys):
+        each = 8 // size
+        for g in range(0, len(members), each):
+            tile = None
+            for u in range(each):
+                ref, index = members[g + u]
+                part = roll(ref[index][0:8], size * u - start, 0)
+                tile = part if tile is None else jnp.where(sub >= size * u, part, tile)
+            middle[place] = tile
+            place += 1
+
+
+def grow(keys, tall_keys, near, far, even):
+    sub = sublanes((8, 128))
+    place = 0
+    for (start, size), members, targets in zip(TAKE, keys, tall_keys):
+        each = 8 // size
+        for g in range(0, len(members), each):
+            after, before = meet(near[place], far[place], even)
+            for u in range(each):
+                ref, index = members[g + u]
+                tile = ref[index]
+                inner, outer = tile[0:8], tile[8:16]
+                later = roll(after, start - size * u, 0)
+                sooner = roll(before, start - size * u, 0)
+                later = jnp.where(sub < start, outer, jnp.where(sub < start + size, later, 0.0))
+                sooner = jnp.where(
+                    sub >= start + size, outer, jnp.where(sub >= start, sooner, 0.0)
+                )
+                target, index = targets[g + u]
+                target[index] = jnp.concatenate([inner, later, sooner], axis=0)
+            place += 1
+
+
+def down_one(K, own, row_one, row_two, one, two, *refs):
+    there, payload = refs[: STATE + 1], refs[STATE + 1]
+    here = refs[STATE + 2 : 2 * STATE + 3]
+    ma0, mb0, ma1, mb1, ma2, mb2, three_rhs, tile, sent, spread_sent = refs[2 * STATE + 3 :]
+    x0, r0, s0, m0, i0, x1, r1, s1, m1, i1, x2, r2, s2, m2, i2, middle = here
+    moves = []
+
+    def send(*which):
+        for n in which:
+            move = pltpu.make_async_copy(here[n], there[n], sent.at[n])
+            move.start()
+            moves.append(move)
+
     halo = (own, row_one, row_two, one, two)
     even = (is_even("gx"), is_even("gy"))
     for a in range(6):
@@ -415,11 +468,10 @@
                         s0[q, 2 * h + e] = pair[e]
                     else:
                         m0[q, 2 * h + e] = pair[e]
+    send(1, 2, 3)
     for q in range(4):
-        pair = widen(*halo, 96 + q, *even)
-        m1[q, 0], m1[q, 1] = pair
-    pair = widen(*halo, 100, *even)
-    m2[0, 0], m2[1, 0] = pair
+        m1[q, 0], m1[q, 1] = widen(*halo, 96 + q, *even)
+    m2[0, 0], m2[1, 0] = widen(*halo, 100, *even)
     m3 = widen(*halo, 101, *even)[0]
     for q in range(4):
         for p in range(2):
@@ -435,19 +487,25 @@
     M = ((ma0, mb0), (ma1, mb1), (ma2, mb2))
     for level in range(3):
         invert(level, K, REACT[level], INV[level])
+    send(4, 7, 8, 9, 12, 13, 14)
     first(0, x0, ma0, r0, m0, i0)
     sweep(0, K, x0, ma0, mb0, r0, m0, i0)
+    send(0)
     descend(K, X, M, RHS, SOLID, REACT, INV)
-    for n, tile in enumerate(middle_tiles(x1, r1, s1, m1, x2, r2, s2, m2)):
-        middle[n] = tile[0:8]
+    pack_middle(levels_one_two((x1, r1, s1, m1), (x2, r2, s2, m2)), middle)
+    send(15, 5, 6, 10, 11)
     rest = coarse_rhs(K, X, M, RHS, SOLID, REACT, three_rhs)
     s3 = 0.5 * (s2[0, 0, 0:8] + s2[1, 0, 0:8])
     y = exact_dot(jnp.concatenate(rest + [m3[0:8], s3], axis=0), decimate())
     y = [y[8 * n : 8 * n + 8] for n in range(6)]
-    tiles = [half_pair(y[0], y[1]), half_pair(y[2], y[3]), half_pair(y[4], y[5])]
+    for n in range(3):
+        tile[n] = half_pair(y[2 * n], y[2 * n + 1])
     for d in range(payload.shape[0]):
-        for n in range(3):
-            payload[d, n] = tiles[n]
+        move = pltpu.make_async_copy(tile, payload.at[d], spread_sent.at[d])
+        move.start()
+        moves.append(move)
+    for move in moves:
+        move.wait()
 
 
 def down_two(
@@ -599,34 +657,28 @@
         target[...] = source[...]
 
 
-def up_one(
-    K, gathered, mine, from_one, from_two, x0i, r0, m0, i0,
-    x0, one, two,
-    x1, r1, s1, m1, i1, x2, r2, s2, m2, i2, ma0, mb0, ma1, mb1, ma2, mb2,
-    natural, x3, ma3, mb3, r3, m3, s3, i3, wide, correct,
-):
-    even = is_even("gx")
-    n = 0
-
-    def tall():
-        nonlocal n
-        after, before = meet(from_one[n], from_two[n], even)
-        tile = jnp.concatenate([mine[n], after, before], axis=0)
-        n += 1
-        return tile
-
-    for level, (x, r, s, m) in ((1, (x1, r1, s1, m1)), (2, (x2, r2, s2, m2))):
-        for q in range(ROWS[level]):
-            for p in range(COLS[level]):
-                for f in range(F):
-                    x[f, q, p] = tall()
-                    r[f, q, p] = tall()
-                s[q, p] = tall()
-                m[q, p] = tall()
+def up_one(K, gathered, *refs):
+    there = refs[:14]
+    x0, one, two = refs[14:17]
+    here = (x0,) + refs[17:30]
+    x1, r1, s1, m1, i1, x2, r2, s2, m2, i2, ma0, mb0, ma1, mb1, ma2, mb2 = refs[30:46]
+    natural, x3, ma3, mb3, r3, m3, s3, i3, wide, correct, arrived = refs[46:]
+    moves = [
+        pltpu.make_async_copy(there[n], here[n], arrived.at[n]) for n in range(len(there))
+    ]
+    for move in moves:
+        move.start()
+    x0, r0, m0, i0, x1s, r1s, s1s, m1s, x2s, r2s, s2s, m2s, near, far = here
+    solve_coarsest(K, gathered, gathered, natural, x3, ma3, mb3, r3, m3, s3, i3, wide, correct)
+    for move in moves:
+        move.wait()
+    grow(
+        levels_one_two((x1s, r1s, s1s, m1s), (x2s, r2s, s2s, m2s)),
+        levels_one_two((x1, r1, s1, m1), (x2, r2, s2, m2)),
+        near, far, is_even("gx"),
+    )
     invert(1, K, s1, i1)
     invert(2, K, s2, i2)
-    x0[...] = x0i[...]
-    solve_coarsest(K, gathered, gathered, natural, x3, ma3, mb3, r3, m3, s3, i3, wide, correct)
     M = ((ma0, mb0), (ma1, mb1), (ma2, mb2))
     ascend(K, (x0, x1, x2), M, (r0, r1, r2), (m0, m1, m2), (i0, i1, i2), correct, False)
 
@@ -701,15 +753,22 @@
     ]
 
 
-def call(body, outs, scratch, args, smem=True, space=pltpu.VMEM):
-    specs = [pl.BlockSpec(memory_space=space)] * len(args)
+def call(body, outs, scratch, args, smem=True, hbm=0):
+    specs = [pl.BlockSpec(memory_space=pltpu.VMEM)] * (len(args) - hbm)
+    specs += [pl.BlockSpec(memory_space=pltpu.HBM)] * hbm
     if smem:
         specs[0] = pl.BlockSpec(memory_space=pltpu.SMEM)
+    args = args[: len(args) - hbm] + tuple(
+        pltpu.with_memory_space_constraint(array, pltpu.HBM) for array in args[len(args) - hbm :]
+    )
+    kept = [isinstance(out, jax.ShapeDtypeStruct) for out in outs]
     return pl.pallas_call(
         body,
         out_shape=outs,
         in_specs=specs,
-        out_specs=[pl.BlockSpec(memory_space=pltpu.VMEM)] * len(outs),
+        out_specs=[
+            pl.BlockSpec(memory_space=pltpu.VMEM if inside else pltpu.HBM) for inside in kept
+        ],
         scratch_shapes=scratch,
         compiler_params=pltpu.CompilerParams(vmem_limit_bytes=30 * 1024 * 1024),
     )(*args)
@@ -734,9 +793,9 @@
             pltpu.VMEM((32, 128), F32),
             pltpu.SemaphoreType.DMA((6,)),
         ],
-        tuple(pltpu.with_memory_space_constraint(array, pltpu.HBM) for array in arrays),
+        arrays,
         smem=False,
-        space=pltpu.HBM,
+        hbm=6,
     )
     own, one, two = packed
     rows = swap("gx", one, two)
@@ -750,11 +809,19 @@
     halo = (own,) + rows + swap("gy", *side)
     shapes = []
     for level in range(3):
-        shapes += [sds(*field(level))] * 2 + [sds(*plane(level))] * 2 + [sds(*field(level))]
+        shapes += [field(level)] * 2 + [plane(level)] * 2 + [field(level)]
+    shapes.append((MIDDLE, 8, 128))
     state = call(
         down_one,
-        shapes + [sds(MIDDLE, 8, 128), sds(blocks, 3, 8, 128)],
-        masked_scratch() + [pltpu.VMEM((F, 1, 1, 16, 128), F32)],
+        [pltpu.HBM(shape, F32) for shape in shapes + [(blocks, 3, 8, 128)]],
+        [pltpu.VMEM(shape, F32) for shape in shapes]
+        + masked_scratch()
+        + [
+            pltpu.VMEM((F, 1, 1, 16, 128), F32),
+            pltpu.VMEM((3, 8, 128), F32),
+            pltpu.SemaphoreType.DMA((STATE + 1,)),
+            pltpu.SemaphoreType.DMA((blocks,)),
+        ],
         (coupling,) + halo,
     )
     x0, r0, s0, m0, i0, x1, r1, s1, m1, i1, x2, r2, s2, m2, i2, middle, payload = state
@@ -766,11 +833,17 @@
         tall += [pltpu.VMEM(field(level, 24), F32)] * 2
         tall += [pltpu.VMEM(plane(level, 24), F32)] * 2
         tall += [pltpu.VMEM(field(level, 24), F32)]
+    given = (x0, r0, m0, i0, x1, r1, s1, m1, x2, r2, s2, m2, near, far)
     x0, one, two = call(
         up_one,
         [sds(*field(0))] + [sds(-(-XTILES // 3), 2, 8, 128)] * 2,
-        tall + masked_scratch(24) + coarsest_scratch(blocks, 24),
-        (coupling, statics, middle, near, far, x0, r0, m0, i0),
+        [pltpu.VMEM(array.shape, F32) for array in given[1:]]
+        + tall
+        + masked_scratch(24)
+        + coarsest_scratch(blocks, 24)
+        + [pltpu.SemaphoreType.DMA((len(given),))],
+        (coupling, statics) + given,
+        hbm=len(given),
     )
     x0, x1, r1, x2, r2, payload = call(
         down_two,

time: 116 us -> 107 us (0.922)
  local copies, waits for them, and re-layouts: 8.26 us -> 0.06 us
  blocking collectives: 22.4 us -> 17.9 us
  Pallas kernels: 21.9 us -> 26.2 us
  waiting for transfers between devices: 21.9 us -> 20 us
    unnamed x20 -> x28, local copies, waits for them, and re-layouts: 8.26 us -> 0.06 us
    ppermute x8, waiting for transfers between devices: 21.9 us -> 16.3 us  [swap(): return (lax.ppermute(first, axis, near), lax.ppermute(second, axis, far))]
    all_to_all x1, blocking collectives: 22.4 us -> 17.9 us  [shards(): gathered = lax.all_to_all(payload, 'gx', 0, 0)]
    pallas_call x6, Pallas kernels: 21.9 us -> 26.2 us  [call(): pl.pallas_call(body, out_shape=outs, in_specs=specs, out_specs=[pl.BlockS...]
    all_to_all x1, waiting for transfers between devices: 0.01 us -> 3.77 us  [shards(): statics = lax.all_to_all(payload, 'gx', 0, 0)]
  transfers between devices with their start and end apart: 9 -> 9, of which waited for: 4 -> 5; matrix products, arithmetic and copies ran while one was open for 0% -> 0% of each run, Pallas kernels for 0% -> 0%
where the time goes in v4:
time: 107 us; the launch traced here: 106 us
  starting transfers between devices  41 us (38%)
  Pallas kernels  26.2 us (24%)
  waiting for transfers between devices  20 us (19%)
  blocking collectives  17.9 us (17%)
    ppermute x8, starting transfers between devices, swap(): return (lax.ppermute(first, axis, near), lax.ppermute(second, axis, far))  26.9 us
    pallas_call x6, Pallas kernels, call(): pl.pallas_call(body, out_shape=outs, in_specs=specs, out_specs=[pl.BlockS...  26.2 us
    all_to_all x1, blocking collectives, shards(): gathered = lax.all_to_all(payload, 'gx', 0, 0)  17.9 us
    ppermute x8, waiting for transfers between devices, swap(): return (lax.ppermute(first, axis, near), lax.ppermute(second, axis, far))  16.3 us
    all_to_all x1, starting transfers between devices, shards(): statics = lax.all_to_all(payload, 'gx', 0, 0)  14.1 us
    all_to_all x1, waiting for transfers between devices, shards(): statics = lax.all_to_all(payload, 'gx', 0, 0)  3.77 us
  transfers between devices with their start and end apart: 9, of which 5 were waited for; matrix products, arithmetic and copies ran while one was open for 0% of the time, Pallas kernels for 0%

profile of v4, /device:TPU:193, one launch (start us, length us, event | category | flops | bytes accessed | tf_op | source)
XLA Modules:
  0.0 106.1 jit_solution(2173039098991436672)
XLA Ops:
  0.6 1.7 %shard_map.86 = (f32[102,8,128]{2,1,0:T(8,128)S(1)}, f32[51,8,128]{2,1,0:T(8,128)S(1)}, f32[51,8,128]{2,1,0:T(8,128)S(1)}) custom-call(f32[4,64,256]{2,1,0:T(8,128)} %source_in.1, f32[64,256]{1,0:T(8,128)} %reaction_in.1, s32[64,256]{1,0:T(8,128)} %solid0_in.1, s32[32,128]{1,0:T(8,128)} %solid1_in.1, s32[16,64]{1,0:T(8,128)} %solid2_in.1, s32[8,32]{1,0:T(8,128)} %solid3_in.1), custom_call_target="tpu_custom_call" | custom-call | tf_op jit(solution)/shard_map/pallas_call | solution.py:765
  2.3 3.1 %collective-permute-start = (f32[51,8,128]{2,1,0:T(8,128)S(1)}, f32[51,8,128]{2,1,0:T(8,128)S(1)}, u32[]{:S(2)}, u32[]{:S(2)}) collective-permute-start(f32[51,8,128]{2,1,0:T(8,128)S(1)} %get-tuple-element.34), channel_id=1, source_target_pairs={{0,16},{16,0},{32,48},{48,32},{64,80},{80,64},{96,112},{112,96},{1... | collective-permute-start | bytes 626696 | tf_op jit(solution)/shard_map/ppermute | solution.py:781
  5.4 0.7 collective-permute-start.1
  6.1 4.1 %collective-permute-done.up_one.row_one = f32[51,8,128]{2,1,0:T(8,128)S(1)} collective-permute-done((f32[51,8,128]{2,1,0:T(8,128)S(1)}, f32[51,8,128]{2,1,0:T(8,128)S(1)}, u32[]{:S(2)}, u32[]{:S(2)}) %collective-permute-start) | collective-permute-done | bytes 208928 | tf_op jit(solution)/shard_map/ppermute | solution.py:781
  10.2 0.0 collective-permute-done.1.up_two.row_two
  10.2 0.4 shard_map.87
  10.6 0.0 copy-start.10
  10.6 3.5 %collective-permute-start.2 = (f32[34,2,8,128]{3,2,1,0:T(8,128)S(1)}, f32[34,2,8,128]{3,2,1,0:T(8,128)S(1)}, u32[]{:S(2)}, u32[]{:S(2)}) collective-permute-start(f32[34,2,8,128]{3,2,1,0:T(8,128)S(1)} %get-tuple-element.36), channel_id=1, source_target_pairs={{0,1},{1,0},{2,3},{3,2},{4,5},{5,4},{6,7},{7,6},{8,9},{9,8},{10,11... | collective-permute-start | bytes 835592 | tf_op jit(solution)/shard_map/ppermute | solution.py:781
  14.1 5.1 %collective-permute-start.3 = (f32[34,2,8,128]{3,2,1,0:T(8,128)S(1)}, f32[34,2,8,128]{3,2,1,0:T(8,128)S(1)}, u32[]{:S(2)}, u32[]{:S(2)}) collective-permute-start(f32[34,2,8,128]{3,2,1,0:T(8,128)S(1)} %get-tuple-element.37), channel_id=1, source_target_pairs={{1,2},{2,1},{3,4},{4,3},{5,6},{6,5},{7,8},{8,7},{9,10},{10,9},{11,... | collective-permute-start | bytes 835592 | tf_op jit(solution)/shard_map/ppermute | solution.py:781
  19.2 0.0 collective-permute-done.2.one
  19.2 4.2 %collective-permute-done.3.two = f32[34,2,8,128]{3,2,1,0:T(8,128)S(1)} collective-permute-done((f32[34,2,8,128]{3,2,1,0:T(8,128)S(1)}, f32[34,2,8,128]{3,2,1,0:T(8,128)S(1)}, u32[]{:S(2)}, u32[]{:S(2)}) %collective-permute-start.3) | collective-permute-done | bytes 278560 | tf_op jit(solution)/shard_map/ppermute | solution.py:781
  23.4 6.1 %shard_map.88 = (f32[4,8,4,16,128]{4,3,2,1,0:T(8,128)}, f32[4,8,4,16,128]{4,3,2,1,0:T(8,128)}, f32[8,4,16,128]{3,2,1,0:T(8,128)}, f32[8,4,16,128]{3,2,1,0:T(8,12...) custom-call(f32[4,4]{1,0:T(4,128)S(1)} %copy-done.10, ...), custom_call_target="tpu_custom_call" | custom-call | tf_op jit(solution)/shard_map/pallas_call | solution.py:765
  29.5 14.1 %all-to-all-start = ((f32[32,3,8,128]{3,2,1,0:T(8,128)}), f32[32,3,8,128]{3,2,1,0:T(8,128)S(1)}, u32[]{:S(2)}, u32[]{:S(2)}) async-start(f32[32,3,8,128]{3,2,1,0:T(8,128)} %get-tuple-element.38), calls=%async_computation | async-start | bytes 786432 | tf_op jit(solution)/shard_map/all_to_all | solution.py:829
  43.6 0.0 copy-done.13
  43.6 0.7 collective-permute-start.5
  44.3 5.6 %collective-permute-start.4 = (f32[30,8,128]{2,1,0:T(8,128)S(1)}, f32[30,8,128]{2,1,0:T(8,128)S(1)}, u32[]{:S(2)}, u32[]{:S(2)}) collective-permute-start(f32[30,8,128]{2,1,0:T(8,128)S(1)} %copy-done.13), channel_id=1, source_target_pairs={{0,16},{16,0},{32,48},{48,32},{64,80},{80,64},{96,112},{112,96},{1... | collective-permute-start | bytes 368648 | tf_op jit(solution)/shard_map/ppermute | solution.py:781
  49.9 0.0 collective-permute-done.5.refs_13_
  49.9 5.0 %collective-permute-done.4.refs_12_ = f32[30,8,128]{2,1,0:T(8,128)S(1)} collective-permute-done((f32[30,8,128]{2,1,0:T(8,128)S(1)}, f32[30,8,128]{2,1,0:T(8,128)S(1)}, u32[]{:S(2)}, u32[]{:S(2)}) %collective-permute-start.4) | collective-permute-done | bytes 122912 | tf_op jit(solution)/shard_map/ppermute | solution.py:781
  54.9 3.8 %all-to-all-done.gathered.statics = f32[32,3,8,128]{3,2,1,0:T(8,128)S(1)} async-done(((f32[32,3,8,128]{3,2,1,0:T(8,128)}), f32[32,3,8,128]{3,2,1,0:T(8,128)S(1)}, u32[]{:S(2)}, u32[]{:S(2)}) %all-to-all-start) | async-done | bytes 393248 | tf_op jit(solution)/shard_map/all_to_all | solution.py:829
  58.7 0.0 copy-start.2
  58.7 0.0 copy-start.3
  58.7 0.0 copy-start.4
  58.7 0.0 copy-start.5
  58.7 0.0 copy-start.6
  58.7 8.4 %shard_map.89 = (f32[4,8,4,16,128]{4,3,2,1,0:T(8,128)S(1)}, f32[22,2,8,128]{3,2,1,0:T(8,128)S(1)}, f32[22,2,8,128]{3,2,1,0:T(8,128)S(1)}) custom-call(f32[4,4]{1,0:T(4,128)S(1)} %copy-done.10, f32[32,3,8,128]{3,2,1,0:T(8,128)S(1)} %all-to-all-done.gathered.statics, f32[4,8,4,16,128]{4,3,2,1,0:T(8,128)} %get-tuple-element.39.refs_0_, ...), custom_call_target="tpu_custom_call" | custom-call | tf_op jit(solution)/shard_map/pallas_call | solution.py:765
  67.2 1.9 %collective-permute-start.6 = (f32[22,2,8,128]{3,2,1,0:T(8,128)S(1)}, f32[22,2,8,128]{3,2,1,0:T(8,128)S(1)}, u32[]{:S(2)}, u32[]{:S(2)}) collective-permute-start(f32[22,2,8,128]{3,2,1,0:T(8,128)S(1)} %get-tuple-element.53), channel_id=1, source_target_pairs={{0,1},{1,0},{2,3},{3,2},{4,5},{5,4},{6,7},{7,6},{8,9},{9,8},{10,11... | collective-permute-start | bytes 540680 | tf_op jit(solution)/shard_map/ppermute | solution.py:781
  69.1 6.4 %collective-permute-start.7 = (f32[22,2,8,128]{3,2,1,0:T(8,128)S(1)}, f32[22,2,8,128]{3,2,1,0:T(8,128)S(1)}, u32[]{:S(2)}, u32[]{:S(2)}) collective-permute-start(f32[22,2,8,128]{3,2,1,0:T(8,128)S(1)} %get-tuple-element.54), channel_id=1, source_target_pairs={{1,2},{2,1},{3,4},{4,3},{5,6},{6,5},{7,8},{8,7},{9,10},{10,9},{11,... | collective-permute-start | bytes 540680 | tf_op jit(solution)/shard_map/ppermute | solution.py:781
  75.5 0.0 collective-permute-done.6.one
  75.5 3.0 %collective-permute-done.7.two = f32[22,2,8,128]{3,2,1,0:T(8,128)S(1)} collective-permute-done((f32[22,2,8,128]{3,2,1,0:T(8,128)S(1)}, f32[22,2,8,128]{3,2,1,0:T(8,128)S(1)}, u32[]{:S(2)}, u32[]{:S(2)}) %collective-permute-start.7) | collective-permute-done | bytes 180256 | tf_op jit(solution)/shard_map/ppermute | solution.py:781
  78.6 4.0 %shard_map.90 = (f32[4,8,4,16,128]{4,3,2,1,0:T(8,128)S(1)}, f32[4,4,2,16,128]{4,3,2,1,0:T(8,128)S(1)}, f32[4,4,2,16,128]{4,3,2,1,0:T(8,128)S(1)}, f32[4,2,1,16,1...) custom-call(f32[4,4]{1,0:T(4,128)S(1)} %copy-done.10, ...), custom_call_target="tpu_custom_call" | custom-call | tf_op jit(solution)/shard_map/pallas_call | solution.py:765
  82.6 17.9 %all_to_all.10.gathered = f32[32,2,8,128]{3,2,1,0:T(8,128)S(1)} all-to-all(f32[32,2,8,128]{3,2,1,0:T(8,128)S(1)} %get-tuple-element.58), channel_id=1, replica_groups=mesh['gx'=32,'gy'=16] {'gx'}, dimensions={0} | all-to-all | bytes 524288 | tf_op jit(solution)/shard_map/all_to_all | solution.py:855
  100.5 5.6 %shard_map.91 = (f32[4,64,256]{2,1,0:T(8,128)}, f32[4,64,256]{2,1,0:T(8,128)}) custom-call(f32[4,4]{1,0:T(4,128)S(1)} %copy-done.10, f32[32,2,8,128]{3,2,1,0:T(8,128)S(1)} %all_to_all.10.gathered, f32[32,3,8,128]{3,2,1,0:T(8,128)S(1)} %all-to-all-done.gathered.statics, f32[4,8,4,16,128]{4,3,2,1,0:T(8,128)S(1)} %get-tuple-element.59.x0i, ...), custom_call_target="tpu_custom_call" | custom-call | tf_op jit(solution)/shard_map/pallas_call | solution.py:765
  (21 shorter events, 0.0 us)
Async XLA Ops:
  2.3 7.9 %collective-permute-start = (f32[51,8,128]{2,1,0:T(8,128)S(1)}, f32[51,8,128]{2,1,0:T(8,128)S(1)}, u32[]{:S(2)}, u32[]{:S(2)}) collective-permute-start(f32[51,8,128]{2,1,0:T(8,128)S(1)} %get-tuple-element.34), channel_id=1, source_target_pairs={{0,16},{16,0},{32,48},{48,32},{64,80},{80,64},{96,112},{112,96},{1... | collective-permute-start | bytes 626696 | tf_op jit(solution)/shard_map/ppermute | solution.py:781
  5.4 4.8 %collective-permute-start.1 = (f32[51,8,128]{2,1,0:T(8,128)S(1)}, f32[51,8,128]{2,1,0:T(8,128)S(1)}, u32[]{:S(2)}, u32[]{:S(2)}) collective-permute-start(f32[51,8,128]{2,1,0:T(8,128)S(1)} %get-tuple-element.35), channel_id=1, source_target_pairs={{16,32},{32,16},{48,64},{64,48},{80,96},{96,80},{112,128},{128,112... | collective-permute-start | bytes 626696 | tf_op jit(solution)/shard_map/ppermute | solution.py:781
  10.6 12.8 %copy-start.10 = (f32[4,4]{1,0:T(4,128)S(1)}, f32[4,4]{1,0:T(4,128)}, u32[]{:S(2)}) copy-start(f32[4,4]{1,0:T(4,128)} %K.7) | copy-start | bytes 196
  10.6 8.6 %collective-permute-start.2 = (f32[34,2,8,128]{3,2,1,0:T(8,128)S(1)}, f32[34,2,8,128]{3,2,1,0:T(8,128)S(1)}, u32[]{:S(2)}, u32[]{:S(2)}) collective-permute-start(f32[34,2,8,128]{3,2,1,0:T(8,128)S(1)} %get-tuple-element.36), channel_id=1, source_target_pairs={{0,1},{1,0},{2,3},{3,2},{4,5},{5,4},{6,7},{7,6},{8,9},{9,8},{10,11... | collective-permute-start | bytes 835592 | tf_op jit(solution)/shard_map/ppermute | solution.py:781
  14.1 9.3 %collective-permute-start.3 = (f32[34,2,8,128]{3,2,1,0:T(8,128)S(1)}, f32[34,2,8,128]{3,2,1,0:T(8,128)S(1)}, u32[]{:S(2)}, u32[]{:S(2)}) collective-permute-start(f32[34,2,8,128]{3,2,1,0:T(8,128)S(1)} %get-tuple-element.37), channel_id=1, source_target_pairs={{1,2},{2,1},{3,4},{4,3},{5,6},{6,5},{7,8},{8,7},{9,10},{10,9},{11,... | collective-permute-start | bytes 835592 | tf_op jit(solution)/shard_map/ppermute | solution.py:781
  29.5 14.1 %copy-start.13 = (f32[30,8,128]{2,1,0:T(8,128)S(1)}, f32[30,8,128]{2,1,0:T(8,128)}, u32[]{:S(2)}) copy-start(f32[30,8,128]{2,1,0:T(8,128)} %get-tuple-element.51) | copy-start | bytes 368644
  29.5 29.1 %all-to-all-start = ((f32[32,3,8,128]{3,2,1,0:T(8,128)}), f32[32,3,8,128]{3,2,1,0:T(8,128)S(1)}, u32[]{:S(2)}, u32[]{:S(2)}) async-start(f32[32,3,8,128]{3,2,1,0:T(8,128)} %get-tuple-element.38), calls=%async_computation | async-start | bytes 786432 | tf_op jit(solution)/shard_map/all_to_all | solution.py:829
  43.6 6.2 %collective-permute-start.5 = (f32[30,8,128]{2,1,0:T(8,128)S(1)}, f32[30,8,128]{2,1,0:T(8,128)S(1)}, u32[]{:S(2)}, u32[]{:S(2)}) collective-permute-start(f32[30,8,128]{2,1,0:T(8,128)S(1)} %copy-done.13), channel_id=1, source_target_pairs={{16,32},{32,16},{48,64},{64,48},{80,96},{96,80},{112,128},{128,112... | collective-permute-start | bytes 368648 | tf_op jit(solution)/shard_map/ppermute | solution.py:781
  44.3 10.6 %collective-permute-start.4 = (f32[30,8,128]{2,1,0:T(8,128)S(1)}, f32[30,8,128]{2,1,0:T(8,128)S(1)}, u32[]{:S(2)}, u32[]{:S(2)}) collective-permute-start(f32[30,8,128]{2,1,0:T(8,128)S(1)} %copy-done.13), channel_id=1, source_target_pairs={{0,16},{16,0},{32,48},{48,32},{64,80},{80,64},{96,112},{112,96},{1... | collective-permute-start | bytes 368648 | tf_op jit(solution)/shard_map/ppermute | solution.py:781
  49.9 8.7 %copy-start.11 = (f32[30,8,128]{2,1,0:T(8,128)}, f32[30,8,128]{2,1,0:T(8,128)S(1)}, u32[]{:S(2)}) copy-start(f32[30,8,128]{2,1,0:T(8,128)S(1)} %collective-permute-done.5.refs_13_) | copy-start | bytes 368644
  54.9 3.8 %copy-start.12 = (f32[30,8,128]{2,1,0:T(8,128)}, f32[30,8,128]{2,1,0:T(8,128)S(1)}, u32[]{:S(2)}) copy-start(f32[30,8,128]{2,1,0:T(8,128)S(1)} %collective-permute-done.4.refs_12_) | copy-start | bytes 368644
  58.7 19.8 %copy-start = (f32[4,8,4,16,128]{4,3,2,1,0:T(8,128)S(1)}, f32[4,8,4,16,128]{4,3,2,1,0:T(8,128)}, u32[]{:S(2)}) copy-start(f32[4,8,4,16,128]{4,3,2,1,0:T(8,128)} %get-tuple-element.40.refs_1_.r0) | copy-start | bytes 3145732
  58.7 19.8 %copy-start.1 = (f32[4,8,4,16,128]{4,3,2,1,0:T(8,128)S(1)}, f32[4,8,4,16,128]{4,3,2,1,0:T(8,128)}, u32[]{:S(2)}) copy-start(f32[4,8,4,16,128]{4,3,2,1,0:T(8,128)} %get-tuple-element.42.refs_3_.i0) | copy-start | bytes 3145732
  58.7 19.8 %copy-start.2 = (f32[8,4,16,128]{3,2,1,0:T(8,128)S(1)}, f32[8,4,16,128]{3,2,1,0:T(8,128)}, u32[]{:S(2)}) copy-start(f32[8,4,16,128]{3,2,1,0:T(8,128)} %get-tuple-element.41.refs_2_.m0) | copy-start | bytes 786436
  58.7 19.8 %copy-start.3 = (f32[8,4,16,128]{3,2,1,0:T(8,128)S(1)}, f32[8,4,16,128]{3,2,1,0:T(8,128)}, u32[]{:S(2)}) copy-start(f32[8,4,16,128]{3,2,1,0:T(8,128)} %get-tuple-element.55.s0) | copy-start | bytes 786436
  58.7 19.8 %copy-start.4 = (f32[4,4,2,16,128]{4,3,2,1,0:T(8,128)S(1)}, f32[4,4,2,16,128]{4,3,2,1,0:T(8,128)}, u32[]{:S(2)}) copy-start(f32[4,4,2,16,128]{4,3,2,1,0:T(8,128)} %get-tuple-element.56.i1) | copy-start | bytes 786436
  58.7 19.8 %copy-start.5 = (f32[4,2,16,128]{3,2,1,0:T(8,128)S(1)}, f32[4,2,16,128]{3,2,1,0:T(8,128)}, u32[]{:S(2)}) copy-start(f32[4,2,16,128]{3,2,1,0:T(8,128)} %get-tuple-element.46.refs_7_.m1) | copy-start | bytes 196612
  58.7 19.8 %copy-start.6 = (f32[4,2,1,16,128]{4,3,2,1,0:T(8,128)S(1)}, f32[4,2,1,16,128]{4,3,2,1,0:T(8,128)}, u32[]{:S(2)}) copy-start(f32[4,2,1,16,128]{4,3,2,1,0:T(8,128)} %get-tuple-element.57.i2) | copy-start | bytes 196612
  58.7 19.8 %copy-start.7 = (f32[4,2,16,128]{3,2,1,0:T(8,128)S(1)}, f32[4,2,16,128]{3,2,1,0:T(8,128)}, u32[]{:S(2)}) copy-start(f32[4,2,16,128]{3,2,1,0:T(8,128)} %get-tuple-element.45.refs_6_.s1) | copy-start | bytes 196612
  58.7 19.8 %copy-start.8 = (f32[2,1,16,128]{3,2,1,0:T(8,128)S(1)}, f32[2,1,16,128]{3,2,1,0:T(8,128)}, u32[]{:S(2)}) copy-start(f32[2,1,16,128]{3,2,1,0:T(8,128)} %get-tuple-element.50.refs_11_.m2) | copy-start | bytes 49156
  58.7 19.8 %copy-start.9 = (f32[2,1,16,128]{3,2,1,0:T(8,128)S(1)}, f32[2,1,16,128]{3,2,1,0:T(8,128)}, u32[]{:S(2)}) copy-start(f32[2,1,16,128]{3,2,1,0:T(8,128)} %get-tuple-element.49.refs_10_.s2) | copy-start | bytes 49156
  67.2 8.3 %collective-permute-start.6 = (f32[22,2,8,128]{3,2,1,0:T(8,128)S(1)}, f32[22,2,8,128]{3,2,1,0:T(8,128)S(1)}, u32[]{:S(2)}, u32[]{:S(2)}) collective-permute-start(f32[22,2,8,128]{3,2,1,0:T(8,128)S(1)} %get-tuple-element.53), channel_id=1, source_target_pairs={{0,1},{1,0},{2,3},{3,2},{4,5},{5,4},{6,7},{7,6},{8,9},{9,8},{10,11... | collective-permute-start | bytes 540680 | tf_op jit(solution)/shard_map/ppermute | solution.py:781
  69.1 9.4 %collective-permute-start.7 = (f32[22,2,8,128]{3,2,1,0:T(8,128)S(1)}, f32[22,2,8,128]{3,2,1,0:T(8,128)S(1)}, u32[]{:S(2)}, u32[]{:S(2)}) collective-permute-start(f32[22,2,8,128]{3,2,1,0:T(8,128)S(1)} %get-tuple-element.54), channel_id=1, source_target_pairs={{1,2},{2,1},{3,4},{4,3},{5,6},{6,5},{7,8},{8,7},{9,10},{10,9},{11,... | collective-permute-start | bytes 540680 | tf_op jit(solution)/shard_map/ppermute | solution.py:781

commit v5 on v4

--- a/solution.py
+++ b/solution.py
@@ -17,6 +17,8 @@
 XTILES = 64
 MIDDLE = 30
 STATE = 15
+GIVEN = 17
+KEPT = 11
 F32 = jnp.float32
 BF16 = jnp.bfloat16
 
@@ -445,7 +447,7 @@
 def down_one(K, own, row_one, row_two, one, two, *refs):
     there, payload = refs[: STATE + 1], refs[STATE + 1]
     here = refs[STATE + 2 : 2 * STATE + 3]
-    ma0, mb0, ma1, mb1, ma2, mb2, three_rhs, tile, sent, spread_sent = refs[2 * STATE + 3 :]
+    ma0, mb0, ma1, mb1, ma2, mb2, three_rhs, spread_out, sent, spread_sent = refs[2 * STATE + 3 :]
     x0, r0, s0, m0, i0, x1, r1, s1, m1, i1, x2, r2, s2, m2, i2, middle = here
     moves = []
 
@@ -498,12 +500,13 @@
     s3 = 0.5 * (s2[0, 0, 0:8] + s2[1, 0, 0:8])
     y = exact_dot(jnp.concatenate(rest + [m3[0:8], s3], axis=0), decimate())
     y = [y[8 * n : 8 * n + 8] for n in range(6)]
-    for n in range(3):
-        tile[n] = half_pair(y[2 * n], y[2 * n + 1])
+    tiles = [half_pair(y[2 * n], y[2 * n + 1]) for n in range(3)]
     for d in range(payload.shape[0]):
-        move = pltpu.make_async_copy(tile, payload.at[d], spread_sent.at[d])
-        move.start()
-        moves.append(move)
+        for n in range(3):
+            spread_out[d, n] = tiles[n]
+    move = pltpu.make_async_copy(spread_out, payload, spread_sent)
+    move.start()
+    moves.append(move)
     for move in moves:
         move.wait()
 
@@ -639,17 +642,18 @@
         correct[2 + half, 0, 0] = y[height : 2 * height]
 
 
-def ascend(K, X, M, RHS, SOLID, INV, correct, last):
+def rise(level, K, X, M, RHS, SOLID, INV, source, last):
+    a, b = M[level]
+    prolong(level, X[level], a, SOLID[level], source)
+    sweep(level, K, X[level], a, b, RHS[level], SOLID[level], INV[level])
+    sweep(level, K, X[level], b, a, RHS[level], SOLID[level], INV[level], last=last)
+    return X[level]
+
+
+def ascend(K, X, M, RHS, SOLID, INV, correct):
     source = correct
     for level in (2, 1, 0):
-        a, b = M[level]
-        prolong(level, X[level], a, SOLID[level], source)
-        sweep(level, K, X[level], a, b, RHS[level], SOLID[level], INV[level])
-        sweep(
-            level, K, X[level], b, a, RHS[level], SOLID[level], INV[level],
-            last=level > 0 or not last,
-        )
-        source = X[level]
+        source = rise(level, K, X, M, RHS, SOLID, INV, source, level > 0)
 
 
 def copy_state(sources, targets):
@@ -658,19 +662,20 @@
 
 
 def up_one(K, gathered, *refs):
-    there = refs[:14]
-    x0, one, two = refs[14:17]
-    here = (x0,) + refs[17:30]
-    x1, r1, s1, m1, i1, x2, r2, s2, m2, i2, ma0, mb0, ma1, mb1, ma2, mb2 = refs[30:46]
-    natural, x3, ma3, mb3, r3, m3, s3, i3, wide, correct, arrived = refs[46:]
+    there, refs = refs[:GIVEN], refs[GIVEN:]
+    kept, one, two = refs[:KEPT], refs[KEPT], refs[KEPT + 1]
+    refs = refs[KEPT + 2 :]
+    here, refs = kept + refs[: GIVEN - KEPT], refs[GIVEN - KEPT :]
+    x1, r1, s1, m1, i1, x2, r2, s2, m2, i2, ma0, mb0, ma1, mb1, ma2, mb2 = refs[:16]
+    natural, x3, ma3, mb3, r3, m3, s3, i3, wide, correct, arrived = refs[16:]
     moves = [
-        pltpu.make_async_copy(there[n], here[n], arrived.at[n]) for n in range(len(there))
+        pltpu.make_async_copy(there[n], here[n], arrived.at[n]) for n in range(GIVEN)
     ]
-    for move in moves:
+    for move in moves[::-1]:
         move.start()
-    x0, r0, m0, i0, x1s, r1s, s1s, m1s, x2s, r2s, s2s, m2s, near, far = here
+    r0, m0, i0, s0, x0, i1s, i2s, s1s, m1s, s2s, m2s, x1s, r1s, x2s, r2s, near, far = here
     solve_coarsest(K, gathered, gathered, natural, x3, ma3, mb3, r3, m3, s3, i3, wide, correct)
-    for move in moves:
+    for move in moves[5:]:
         move.wait()
     grow(
         levels_one_two((x1s, r1s, s1s, m1s), (x2s, r2s, s2s, m2s)),
@@ -680,7 +685,12 @@
     invert(1, K, s1, i1)
     invert(2, K, s2, i2)
     M = ((ma0, mb0), (ma1, mb1), (ma2, mb2))
-    ascend(K, (x0, x1, x2), M, (r0, r1, r2), (m0, m1, m2), (i0, i1, i2), correct, False)
+    X, RHS, SOLID, INV = (x0, x1, x2), (r0, r1, r2), (m0, m1, m2), (i0, i1, i2)
+    source = rise(2, K, X, M, RHS, SOLID, INV, correct, True)
+    source = rise(1, K, X, M, RHS, SOLID, INV, source, True)
+    for move in moves[:5]:
+        move.wait()
+    rise(0, K, X, M, RHS, SOLID, INV, source, True)
 
     def pick(index, v):
         f, q, h = index // 16, index // 2 % 8, index % 2
@@ -699,7 +709,7 @@
     copy_state((x0i, x1i, x2i), (x0, x1, x2))
     solve_coarsest(K, gathered, statics, natural, x3, ma3, mb3, r3, m3, s3, i3, wide, correct)
     M = ((ma0, mb0), (ma1, mb1), (ma2, mb2))
-    ascend(K, (x0, x1, x2), M, (r0, r1, r2), (m0, m1, m2), (i0, i1, i2), correct, True)
+    ascend(K, (x0, x1, x2), M, (r0, r1, r2), (m0, m1, m2), (i0, i1, i2), correct)
     mine = slice(0, 8)
     for q in range(8):
         for h in range(2):
@@ -818,9 +828,9 @@
         + masked_scratch()
         + [
             pltpu.VMEM((F, 1, 1, 16, 128), F32),
-            pltpu.VMEM((3, 8, 128), F32),
+            pltpu.VMEM((blocks, 3, 8, 128), F32),
             pltpu.SemaphoreType.DMA((STATE + 1,)),
-            pltpu.SemaphoreType.DMA((blocks,)),
+            pltpu.SemaphoreType.DMA,
         ],
         (coupling,) + halo,
     )
@@ -833,17 +843,18 @@
         tall += [pltpu.VMEM(field(level, 24), F32)] * 2
         tall += [pltpu.VMEM(plane(level, 24), F32)] * 2
         tall += [pltpu.VMEM(field(level, 24), F32)]
-    given = (x0, r0, m0, i0, x1, r1, s1, m1, x2, r2, s2, m2, near, far)
-    x0, one, two = call(
+    given = (r0, m0, i0, s0, x0, i1, i2, s1, m1, s2, m2, x1, r1, x2, r2, near, far)
+    r0, m0, i0, s0, x0, i1, i2, s1, m1, s2, m2, one, two = call(
         up_one,
-        [sds(*field(0))] + [sds(-(-XTILES // 3), 2, 8, 128)] * 2,
-        [pltpu.VMEM(array.shape, F32) for array in given[1:]]
+        [sds(*array.shape) for array in given[:KEPT]]
+        + [sds(-(-XTILES // 3), 2, 8, 128)] * 2,
+        [pltpu.VMEM(array.shape, F32) for array in given[KEPT:]]
         + tall
         + masked_scratch(24)
         + coarsest_scratch(blocks, 24)
-        + [pltpu.SemaphoreType.DMA((len(given),))],
+        + [pltpu.SemaphoreType.DMA((GIVEN,))],
         (coupling, statics) + given,
-        hbm=len(given),
+        hbm=GIVEN,
     )
     x0, x1, r1, x2, r2, payload = call(
         down_two,

time: 107 us -> 105 us (0.981)
  Pallas kernels: 26.2 us -> 25.1 us
    pallas_call x6, Pallas kernels: 26.2 us -> 25.1 us  [call(): pl.pallas_call(body, out_shape=outs, in_specs=specs, out_specs=[pl.BlockS...]
where the time goes in v5:
time: 105 us
  starting transfers between devices  41 us (39%)
  Pallas kernels  25.1 us (24%)
  waiting for transfers between devices  20 us (19%)
  blocking collectives  18 us (17%)
    ppermute x8, starting transfers between devices, swap(): return (lax.ppermute(first, axis, near), lax.ppermute(second, axis, far))  26.9 us
    pallas_call x6, Pallas kernels, call(): pl.pallas_call(body, out_shape=outs, in_specs=specs, out_specs=[pl.BlockS...  25.1 us
    all_to_all x1, blocking collectives, shards(): gathered = lax.all_to_all(payload, 'gx', 0, 0)  18 us
    ppermute x8, waiting for transfers between devices, swap(): return (lax.ppermute(first, axis, near), lax.ppermute(second, axis, far))  16.3 us
    all_to_all x1, starting transfers between devices, shards(): statics = lax.all_to_all(payload, 'gx', 0, 0)  14.1 us
    all_to_all x1, waiting for transfers between devices, shards(): statics = lax.all_to_all(payload, 'gx', 0, 0)  3.77 us
  transfers between devices with their start and end apart: 9, of which 5 were waited for; matrix products, arithmetic and copies ran while one was open for 0% of the time, Pallas kernels for 0%

profile of v5, /device:TPU:193, one launch (start us, length us, event | category | flops | bytes accessed | tf_op | source)
XLA Modules:
  0.0 104.9 jit_solution(9770732535826541884)
XLA Ops:
  0.6 1.7 %shard_map.86 = (f32[102,8,128]{2,1,0:T(8,128)S(1)}, f32[51,8,128]{2,1,0:T(8,128)S(1)}, f32[51,8,128]{2,1,0:T(8,128)S(1)}) custom-call(f32[4,64,256]{2,1,0:T(8,128)} %source_in.1, f32[64,256]{1,0:T(8,128)} %reaction_in.1, s32[64,256]{1,0:T(8,128)} %solid0_in.1, s32[32,128]{1,0:T(8,128)} %solid1_in.1, s32[16,64]{1,0:T(8,128)} %solid2_in.1, s32[8,32]{1,0:T(8,128)} %solid3_in.1), custom_call_target="tpu_custom_call" | custom-call | tf_op jit(solution)/shard_map/pallas_call | solution.py:775
  2.3 3.1 %collective-permute-start = (f32[51,8,128]{2,1,0:T(8,128)S(1)}, f32[51,8,128]{2,1,0:T(8,128)S(1)}, u32[]{:S(2)}, u32[]{:S(2)}) collective-permute-start(f32[51,8,128]{2,1,0:T(8,128)S(1)} %get-tuple-element.44), channel_id=1, source_target_pairs={{0,16},{16,0},{32,48},{48,32},{64,80},{80,64},{96,112},{112,96},{1... | collective-permute-start | bytes 626696 | tf_op jit(solution)/shard_map/ppermute | solution.py:791
  5.4 0.7 collective-permute-start.1
  6.1 4.1 %collective-permute-done.up_one.row_one = f32[51,8,128]{2,1,0:T(8,128)S(1)} collective-permute-done((f32[51,8,128]{2,1,0:T(8,128)S(1)}, f32[51,8,128]{2,1,0:T(8,128)S(1)}, u32[]{:S(2)}, u32[]{:S(2)}) %collective-permute-start) | collective-permute-done | bytes 208928 | tf_op jit(solution)/shard_map/ppermute | solution.py:791
  10.2 0.0 collective-permute-done.1.up_two.row_two
  10.2 0.4 shard_map.87
  10.6 0.0 copy-start
  10.6 3.5 %collective-permute-start.2 = (f32[34,2,8,128]{3,2,1,0:T(8,128)S(1)}, f32[34,2,8,128]{3,2,1,0:T(8,128)S(1)}, u32[]{:S(2)}, u32[]{:S(2)}) collective-permute-start(f32[34,2,8,128]{3,2,1,0:T(8,128)S(1)} %get-tuple-element.46), channel_id=1, source_target_pairs={{0,1},{1,0},{2,3},{3,2},{4,5},{5,4},{6,7},{7,6},{8,9},{9,8},{10,11... | collective-permute-start | bytes 835592 | tf_op jit(solution)/shard_map/ppermute | solution.py:791
  14.1 5.1 %collective-permute-start.3 = (f32[34,2,8,128]{3,2,1,0:T(8,128)S(1)}, f32[34,2,8,128]{3,2,1,0:T(8,128)S(1)}, u32[]{:S(2)}, u32[]{:S(2)}) collective-permute-start(f32[34,2,8,128]{3,2,1,0:T(8,128)S(1)} %get-tuple-element.47), channel_id=1, source_target_pairs={{1,2},{2,1},{3,4},{4,3},{5,6},{6,5},{7,8},{8,7},{9,10},{10,9},{11,... | collective-permute-start | bytes 835592 | tf_op jit(solution)/shard_map/ppermute | solution.py:791
  19.2 0.0 collective-permute-done.2.one
  19.2 4.2 %collective-permute-done.3.two = f32[34,2,8,128]{3,2,1,0:T(8,128)S(1)} collective-permute-done((f32[34,2,8,128]{3,2,1,0:T(8,128)S(1)}, f32[34,2,8,128]{3,2,1,0:T(8,128)S(1)}, u32[]{:S(2)}, u32[]{:S(2)}) %collective-permute-start.3) | collective-permute-done | bytes 278560 | tf_op jit(solution)/shard_map/ppermute | solution.py:791
  23.4 0.0 copy-done
  23.4 5.8 %shard_map.88 = (f32[4,8,4,16,128]{4,3,2,1,0:T(8,128)}, f32[4,8,4,16,128]{4,3,2,1,0:T(8,128)}, f32[8,4,16,128]{3,2,1,0:T(8,128)}, f32[8,4,16,128]{3,2,1,0:T(8,12...) custom-call(f32[4,4]{1,0:T(4,128)S(1)} %copy-done, ...), custom_call_target="tpu_custom_call" | custom-call | tf_op jit(solution)/shard_map/pallas_call | solution.py:775
  29.3 0.0 copy-start.3
  29.3 14.1 %all-to-all-start = ((f32[32,3,8,128]{3,2,1,0:T(8,128)}), f32[32,3,8,128]{3,2,1,0:T(8,128)S(1)}, u32[]{:S(2)}, u32[]{:S(2)}) async-start(f32[32,3,8,128]{3,2,1,0:T(8,128)} %get-tuple-element.48), calls=%async_computation | async-start | bytes 786432 | tf_op jit(solution)/shard_map/all_to_all | solution.py:839
  43.4 0.0 copy-done.3
  43.4 0.7 collective-permute-start.5
  44.1 5.6 %collective-permute-start.4 = (f32[30,8,128]{2,1,0:T(8,128)S(1)}, f32[30,8,128]{2,1,0:T(8,128)S(1)}, u32[]{:S(2)}, u32[]{:S(2)}) collective-permute-start(f32[30,8,128]{2,1,0:T(8,128)S(1)} %copy-done.3), channel_id=1, source_target_pairs={{0,16},{16,0},{32,48},{48,32},{64,80},{80,64},{96,112},{112,96},{1... | collective-permute-start | bytes 368648 | tf_op jit(solution)/shard_map/ppermute | solution.py:791
  49.7 0.0 collective-permute-done.5.refs_16_
  49.7 0.0 copy-start.1
  49.7 5.0 %collective-permute-done.4.refs_15_ = f32[30,8,128]{2,1,0:T(8,128)S(1)} collective-permute-done((f32[30,8,128]{2,1,0:T(8,128)S(1)}, f32[30,8,128]{2,1,0:T(8,128)S(1)}, u32[]{:S(2)}, u32[]{:S(2)}) %collective-permute-start.4) | collective-permute-done | bytes 122912 | tf_op jit(solution)/shard_map/ppermute | solution.py:791
  54.7 3.8 %all-to-all-done.gathered.statics = f32[32,3,8,128]{3,2,1,0:T(8,128)S(1)} async-done(((f32[32,3,8,128]{3,2,1,0:T(8,128)}), f32[32,3,8,128]{3,2,1,0:T(8,128)S(1)}, u32[]{:S(2)}, u32[]{:S(2)}) %all-to-all-start) | async-done | bytes 393248 | tf_op jit(solution)/shard_map/all_to_all | solution.py:839
  58.4 0.0 copy-done.1
  58.4 0.0 copy-done.2
  58.4 8.4 %shard_map.89 = (f32[4,8,4,16,128]{4,3,2,1,0:T(8,128)S(1)}, f32[8,4,16,128]{3,2,1,0:T(8,128)S(1)}, f32[4,8,4,16,128]{4,3,2,1,0:T(8,128)S(1)}, f32[8,4,16,128]{3,...) custom-call(f32[4,4]{1,0:T(4,128)S(1)} %copy-done, ...), custom_call_target="tpu_custom_call" | custom-call | tf_op jit(solution)/shard_map/pallas_call | solution.py:775
  66.9 1.9 %collective-permute-start.6 = (f32[22,2,8,128]{3,2,1,0:T(8,128)S(1)}, f32[22,2,8,128]{3,2,1,0:T(8,128)S(1)}, u32[]{:S(2)}, u32[]{:S(2)}) collective-permute-start(f32[22,2,8,128]{3,2,1,0:T(8,128)S(1)} %get-tuple-element.66), channel_id=1, source_target_pairs={{0,1},{1,0},{2,3},{3,2},{4,5},{5,4},{6,7},{7,6},{8,9},{9,8},{10,11... | collective-permute-start | bytes 540680 | tf_op jit(solution)/shard_map/ppermute | solution.py:791
  68.8 6.4 %collective-permute-start.7 = (f32[22,2,8,128]{3,2,1,0:T(8,128)S(1)}, f32[22,2,8,128]{3,2,1,0:T(8,128)S(1)}, u32[]{:S(2)}, u32[]{:S(2)}) collective-permute-start(f32[22,2,8,128]{3,2,1,0:T(8,128)S(1)} %get-tuple-element.67), channel_id=1, source_target_pairs={{1,2},{2,1},{3,4},{4,3},{5,6},{6,5},{7,8},{8,7},{9,10},{10,9},{11,... | collective-permute-start | bytes 540680 | tf_op jit(solution)/shard_map/ppermute | solution.py:791
  75.2 0.0 collective-permute-done.6.one
  75.2 3.0 %collective-permute-done.7.two = f32[22,2,8,128]{3,2,1,0:T(8,128)S(1)} collective-permute-done((f32[22,2,8,128]{3,2,1,0:T(8,128)S(1)}, f32[22,2,8,128]{3,2,1,0:T(8,128)S(1)}, u32[]{:S(2)}, u32[]{:S(2)}) %collective-permute-start.7) | collective-permute-done | bytes 180256 | tf_op jit(solution)/shard_map/ppermute | solution.py:791
  78.2 3.5 %shard_map.90 = (f32[4,8,4,16,128]{4,3,2,1,0:T(8,128)S(1)}, f32[4,4,2,16,128]{4,3,2,1,0:T(8,128)S(1)}, f32[4,4,2,16,128]{4,3,2,1,0:T(8,128)S(1)}, f32[4,2,1,16,1...) custom-call(f32[4,4]{1,0:T(4,128)S(1)} %copy-done, ...), custom_call_target="tpu_custom_call" | custom-call | tf_op jit(solution)/shard_map/pallas_call | solution.py:775
  81.7 18.0 %all_to_all.10.gathered = f32[32,2,8,128]{3,2,1,0:T(8,128)S(1)} all-to-all(f32[32,2,8,128]{3,2,1,0:T(8,128)S(1)} %get-tuple-element.78), channel_id=1, replica_groups=mesh['gx'=32,'gy'=16] {'gx'}, dimensions={0} | all-to-all | bytes 524288 | tf_op jit(solution)/shard_map/all_to_all | solution.py:866
  99.7 5.3 %shard_map.91 = (f32[4,64,256]{2,1,0:T(8,128)}, f32[4,64,256]{2,1,0:T(8,128)}) custom-call(f32[4,4]{1,0:T(4,128)S(1)} %copy-done, f32[32,2,8,128]{3,2,1,0:T(8,128)S(1)} %all_to_all.10.gathered, f32[32,3,8,128]{3,2,1,0:T(8,128)S(1)} %all-to-all-done.gathered.statics, f32[4,8,4,16,128]{4,3,2,1,0:T(8,128)S(1)} %get-tuple-element.79.x0i, ...), custom_call_target="tpu_custom_call" | custom-call | tf_op jit(solution)/shard_map/pallas_call | solution.py:775
  (1 shorter events, 0.0 us)
Async XLA Ops:
  2.3 7.9 %collective-permute-start = (f32[51,8,128]{2,1,0:T(8,128)S(1)}, f32[51,8,128]{2,1,0:T(8,128)S(1)}, u32[]{:S(2)}, u32[]{:S(2)}) collective-permute-start(f32[51,8,128]{2,1,0:T(8,128)S(1)} %get-tuple-element.44), channel_id=1, source_target_pairs={{0,16},{16,0},{32,48},{48,32},{64,80},{80,64},{96,112},{112,96},{1... | collective-permute-start | bytes 626696 | tf_op jit(solution)/shard_map/ppermute | solution.py:791
  5.4 4.8 %collective-permute-start.1 = (f32[51,8,128]{2,1,0:T(8,128)S(1)}, f32[51,8,128]{2,1,0:T(8,128)S(1)}, u32[]{:S(2)}, u32[]{:S(2)}) collective-permute-start(f32[51,8,128]{2,1,0:T(8,128)S(1)} %get-tuple-element.45), channel_id=1, source_target_pairs={{16,32},{32,16},{48,64},{64,48},{80,96},{96,80},{112,128},{128,112... | collective-permute-start | bytes 626696 | tf_op jit(solution)/shard_map/ppermute | solution.py:791
  10.6 12.8 %copy-start = (f32[4,4]{1,0:T(4,128)S(1)}, f32[4,4]{1,0:T(4,128)}, u32[]{:S(2)}) copy-start(f32[4,4]{1,0:T(4,128)} %K.7) | copy-start | bytes 196
  10.6 8.6 %collective-permute-start.2 = (f32[34,2,8,128]{3,2,1,0:T(8,128)S(1)}, f32[34,2,8,128]{3,2,1,0:T(8,128)S(1)}, u32[]{:S(2)}, u32[]{:S(2)}) collective-permute-start(f32[34,2,8,128]{3,2,1,0:T(8,128)S(1)} %get-tuple-element.46), channel_id=1, source_target_pairs={{0,1},{1,0},{2,3},{3,2},{4,5},{5,4},{6,7},{7,6},{8,9},{9,8},{10,11... | collective-permute-start | bytes 835592 | tf_op jit(solution)/shard_map/ppermute | solution.py:791
  14.1 9.3 %collective-permute-start.3 = (f32[34,2,8,128]{3,2,1,0:T(8,128)S(1)}, f32[34,2,8,128]{3,2,1,0:T(8,128)S(1)}, u32[]{:S(2)}, u32[]{:S(2)}) collective-permute-start(f32[34,2,8,128]{3,2,1,0:T(8,128)S(1)} %get-tuple-element.47), channel_id=1, source_target_pairs={{1,2},{2,1},{3,4},{4,3},{5,6},{6,5},{7,8},{8,7},{9,10},{10,9},{11,... | collective-permute-start | bytes 835592 | tf_op jit(solution)/shard_map/ppermute | solution.py:791
  29.3 14.1 %copy-start.3 = (f32[30,8,128]{2,1,0:T(8,128)S(1)}, f32[30,8,128]{2,1,0:T(8,128)}, u32[]{:S(2)}) copy-start(f32[30,8,128]{2,1,0:T(8,128)} %get-tuple-element.64) | copy-start | bytes 368644
  29.3 29.1 %all-to-all-start = ((f32[32,3,8,128]{3,2,1,0:T(8,128)}), f32[32,3,8,128]{3,2,1,0:T(8,128)S(1)}, u32[]{:S(2)}, u32[]{:S(2)}) async-start(f32[32,3,8,128]{3,2,1,0:T(8,128)} %get-tuple-element.48), calls=%async_computation | async-start | bytes 786432 | tf_op jit(solution)/shard_map/all_to_all | solution.py:839
  43.4 6.2 %collective-permute-start.5 = (f32[30,8,128]{2,1,0:T(8,128)S(1)}, f32[30,8,128]{2,1,0:T(8,128)S(1)}, u32[]{:S(2)}, u32[]{:S(2)}) collective-permute-start(f32[30,8,128]{2,1,0:T(8,128)S(1)} %copy-done.3), channel_id=1, source_target_pairs={{16,32},{32,16},{48,64},{64,48},{80,96},{96,80},{112,128},{128,112... | collective-permute-start | bytes 368648 | tf_op jit(solution)/shard_map/ppermute | solution.py:791
  44.1 10.6 %collective-permute-start.4 = (f32[30,8,128]{2,1,0:T(8,128)S(1)}, f32[30,8,128]{2,1,0:T(8,128)S(1)}, u32[]{:S(2)}, u32[]{:S(2)}) collective-permute-start(f32[30,8,128]{2,1,0:T(8,128)S(1)} %copy-done.3), channel_id=1, source_target_pairs={{0,16},{16,0},{32,48},{48,32},{64,80},{80,64},{96,112},{112,96},{1... | collective-permute-start | bytes 368648 | tf_op jit(solution)/shard_map/ppermute | solution.py:791
  49.7 8.7 %copy-start.1 = (f32[30,8,128]{2,1,0:T(8,128)}, f32[30,8,128]{2,1,0:T(8,128)S(1)}, u32[]{:S(2)}) copy-start(f32[30,8,128]{2,1,0:T(8,128)S(1)} %collective-permute-done.5.refs_16_) | copy-start | bytes 368644
  54.6 3.8 %copy-start.2 = (f32[30,8,128]{2,1,0:T(8,128)}, f32[30,8,128]{2,1,0:T(8,128)S(1)}, u32[]{:S(2)}) copy-start(f32[30,8,128]{2,1,0:T(8,128)S(1)} %collective-permute-done.4.refs_15_) | copy-start | bytes 368644
  66.9 8.3 %collective-permute-start.6 = (f32[22,2,8,128]{3,2,1,0:T(8,128)S(1)}, f32[22,2,8,128]{3,2,1,0:T(8,128)S(1)}, u32[]{:S(2)}, u32[]{:S(2)}) collective-permute-start(f32[22,2,8,128]{3,2,1,0:T(8,128)S(1)} %get-tuple-element.66), channel_id=1, source_target_pairs={{0,1},{1,0},{2,3},{3,2},{4,5},{5,4},{6,7},{7,6},{8,9},{9,8},{10,11... | collective-permute-start | bytes 540680 | tf_op jit(solution)/shard_map/ppermute | solution.py:791
  68.8 9.4 %collective-permute-start.7 = (f32[22,2,8,128]{3,2,1,0:T(8,128)S(1)}, f32[22,2,8,128]{3,2,1,0:T(8,128)S(1)}, u32[]{:S(2)}, u32[]{:S(2)}) collective-permute-start(f32[22,2,8,128]{3,2,1,0:T(8,128)S(1)} %get-tuple-element.67), channel_id=1, source_target_pairs={{1,2},{2,1},{3,4},{4,3},{5,6},{6,5},{7,8},{8,7},{9,10},{10,9},{11,... | collective-permute-start | bytes 540680 | tf_op jit(solution)/shard_map/ppermute | solution.py:791

commit v6 on v5

--- a/solution.py
+++ b/solution.py
@@ -16,9 +16,9 @@
 TILES = 102
 XTILES = 64
 MIDDLE = 30
-STATE = 15
-GIVEN = 17
-KEPT = 11
+STATE = 12
+GIVEN = 14
+KEPT = 8
 F32 = jnp.float32
 BF16 = jnp.bfloat16
 
@@ -447,8 +447,9 @@
 def down_one(K, own, row_one, row_two, one, two, *refs):
     there, payload = refs[: STATE + 1], refs[STATE + 1]
     here = refs[STATE + 2 : 2 * STATE + 3]
-    ma0, mb0, ma1, mb1, ma2, mb2, three_rhs, spread_out, sent, spread_sent = refs[2 * STATE + 3 :]
-    x0, r0, s0, m0, i0, x1, r1, s1, m1, i1, x2, r2, s2, m2, i2, middle = here
+    i0, i1, i2, ma0, mb0, ma1, mb1, ma2, mb2 = refs[2 * STATE + 3 : 2 * STATE + 12]
+    three_rhs, spread_out, sent, spread_sent = refs[2 * STATE + 12 :]
+    x0, r0, s0, m0, x1, r1, s1, m1, x2, r2, s2, m2, middle = here
     moves = []
 
     def send(*which):
@@ -489,13 +490,13 @@
     M = ((ma0, mb0), (ma1, mb1), (ma2, mb2))
     for level in range(3):
         invert(level, K, REACT[level], INV[level])
-    send(4, 7, 8, 9, 12, 13, 14)
+    send(6, 7, 10, 11)
     first(0, x0, ma0, r0, m0, i0)
     sweep(0, K, x0, ma0, mb0, r0, m0, i0)
     send(0)
     descend(K, X, M, RHS, SOLID, REACT, INV)
     pack_middle(levels_one_two((x1, r1, s1, m1), (x2, r2, s2, m2)), middle)
-    send(15, 5, 6, 10, 11)
+    send(12, 4, 5, 8, 9)
     rest = coarse_rhs(K, X, M, RHS, SOLID, REACT, three_rhs)
     s3 = 0.5 * (s2[0, 0, 0:8] + s2[1, 0, 0:8])
     y = exact_dot(jnp.concatenate(rest + [m3[0:8], s3], axis=0), decimate())
@@ -663,8 +664,8 @@
 
 def up_one(K, gathered, *refs):
     there, refs = refs[:GIVEN], refs[GIVEN:]
-    kept, one, two = refs[:KEPT], refs[KEPT], refs[KEPT + 1]
-    refs = refs[KEPT + 2 :]
+    kept, (i0, i1s, i2s, one, two) = refs[:KEPT], refs[KEPT : KEPT + 5]
+    refs = refs[KEPT + 5 :]
     here, refs = kept + refs[: GIVEN - KEPT], refs[GIVEN - KEPT :]
     x1, r1, s1, m1, i1, x2, r2, s2, m2, i2, ma0, mb0, ma1, mb1, ma2, mb2 = refs[:16]
     natural, x3, ma3, mb3, r3, m3, s3, i3, wide, correct, arrived = refs[16:]
@@ -673,9 +674,9 @@
     ]
     for move in moves[::-1]:
         move.start()
-    r0, m0, i0, s0, x0, i1s, i2s, s1s, m1s, s2s, m2s, x1s, r1s, x2s, r2s, near, far = here
+    r0, m0, x0, s0, s1s, m1s, s2s, m2s, x1s, r1s, x2s, r2s, near, far = here
     solve_coarsest(K, gathered, gathered, natural, x3, ma3, mb3, r3, m3, s3, i3, wide, correct)
-    for move in moves[5:]:
+    for move in moves[3:]:
         move.wait()
     grow(
         levels_one_two((x1s, r1s, s1s, m1s), (x2s, r2s, s2s, m2s)),
@@ -684,11 +685,14 @@
     )
     invert(1, K, s1, i1)
     invert(2, K, s2, i2)
+    invert(0, K, s0, i0)
+    invert(1, K, s1s, i1s)
+    invert(2, K, s2s, i2s)
     M = ((ma0, mb0), (ma1, mb1), (ma2, mb2))
     X, RHS, SOLID, INV = (x0, x1, x2), (r0, r1, r2), (m0, m1, m2), (i0, i1, i2)
     source = rise(2, K, X, M, RHS, SOLID, INV, correct, True)
     source = rise(1, K, X, M, RHS, SOLID, INV, source, True)
-    for move in moves[:5]:
+    for move in moves[:3]:
         move.wait()
     rise(0, K, X, M, RHS, SOLID, INV, source, True)
 
@@ -819,12 +823,13 @@
     halo = (own,) + rows + swap("gy", *side)
     shapes = []
     for level in range(3):
-        shapes += [field(level)] * 2 + [plane(level)] * 2 + [field(level)]
+        shapes += [field(level)] * 2 + [plane(level)] * 2
     shapes.append((MIDDLE, 8, 128))
     state = call(
         down_one,
         [pltpu.HBM(shape, F32) for shape in shapes + [(blocks, 3, 8, 128)]],
         [pltpu.VMEM(shape, F32) for shape in shapes]
+        + [pltpu.VMEM(field(level), F32) for level in range(3)]
         + masked_scratch()
         + [
             pltpu.VMEM((F, 1, 1, 16, 128), F32),
@@ -834,7 +839,7 @@
         ],
         (coupling,) + halo,
     )
-    x0, r0, s0, m0, i0, x1, r1, s1, m1, i1, x2, r2, s2, m2, i2, middle, payload = state
+    x0, r0, s0, m0, x1, r1, s1, m1, x2, r2, s2, m2, middle, payload = state
     near, far = swap("gx", middle, middle)
     statics = lax.all_to_all(payload, "gx", 0, 0)
     inner = [pltpu.VMEM(field(level), F32) for level in range(3)]
@@ -843,10 +848,11 @@
         tall += [pltpu.VMEM(field(level, 24), F32)] * 2
         tall += [pltpu.VMEM(plane(level, 24), F32)] * 2
         tall += [pltpu.VMEM(field(level, 24), F32)]
-    given = (r0, m0, i0, s0, x0, i1, i2, s1, m1, s2, m2, x1, r1, x2, r2, near, far)
-    r0, m0, i0, s0, x0, i1, i2, s1, m1, s2, m2, one, two = call(
+    given = (r0, m0, x0, s0, s1, m1, s2, m2, x1, r1, x2, r2, near, far)
+    r0, m0, x0, s0, s1, m1, s2, m2, i0, i1, i2, one, two = call(
         up_one,
         [sds(*array.shape) for array in given[:KEPT]]
+        + [sds(*field(level)) for level in range(3)]
         + [sds(-(-XTILES // 3), 2, 8, 128)] * 2,
         [pltpu.VMEM(array.shape, F32) for array in given[KEPT:]]
         + tall

time: 105 us -> 105 us (level)
  no operation moved by 1% of the time
where the time goes in v6:
time: 105 us; the launch traced here: 104 us
  starting transfers between devices  41 us (39%)
  Pallas kernels  24.5 us (23%)
  waiting for transfers between devices  20 us (19%)
  blocking collectives  18 us (17%)
    ppermute x8, starting transfers between devices, swap(): return (lax.ppermute(first, axis, near), lax.ppermute(second, axis, far))  26.9 us
    pallas_call x6, Pallas kernels, call(): pl.pallas_call(body, out_shape=outs, in_specs=specs, out_specs=[pl.BlockS...  24.5 us
    all_to_all x1, blocking collectives, shards(): gathered = lax.all_to_all(payload, 'gx', 0, 0)  18 us
    ppermute x8, waiting for transfers between devices, swap(): return (lax.ppermute(first, axis, near), lax.ppermute(second, axis, far))  16.3 us
    all_to_all x1, starting transfers between devices, shards(): statics = lax.all_to_all(payload, 'gx', 0, 0)  14.1 us
    all_to_all x1, waiting for transfers between devices, shards(): statics = lax.all_to_all(payload, 'gx', 0, 0)  3.77 us
  transfers between devices with their start and end apart: 9, of which 5 were waited for; matrix products, arithmetic and copies ran while one was open for 0% of the time, Pallas kernels for 0%

profile of v6, /device:TPU:193, one launch (start us, length us, event | category | flops | bytes accessed | tf_op | source)
XLA Modules:
  0.0 104.3 jit_solution(13578055750485012642)
XLA Ops:
  0.6 1.7 %shard_map.86 = (f32[102,8,128]{2,1,0:T(8,128)S(1)}, f32[51,8,128]{2,1,0:T(8,128)S(1)}, f32[51,8,128]{2,1,0:T(8,128)S(1)}) custom-call(f32[4,64,256]{2,1,0:T(8,128)} %source_in.1, f32[64,256]{1,0:T(8,128)} %reaction_in.1, s32[64,256]{1,0:T(8,128)} %solid0_in.1, s32[32,128]{1,0:T(8,128)} %solid1_in.1, s32[16,64]{1,0:T(8,128)} %solid2_in.1, s32[8,32]{1,0:T(8,128)} %solid3_in.1), custom_call_target="tpu_custom_call" | custom-call | tf_op jit(solution)/shard_map/pallas_call | solution.py:779
  2.3 3.1 %collective-permute-start = (f32[51,8,128]{2,1,0:T(8,128)S(1)}, f32[51,8,128]{2,1,0:T(8,128)S(1)}, u32[]{:S(2)}, u32[]{:S(2)}) collective-permute-start(f32[51,8,128]{2,1,0:T(8,128)S(1)} %get-tuple-element.41), channel_id=1, source_target_pairs={{0,16},{16,0},{32,48},{48,32},{64,80},{80,64},{96,112},{112,96},{1... | collective-permute-start | bytes 626696 | tf_op jit(solution)/shard_map/ppermute | solution.py:795
  5.4 0.7 collective-permute-start.1
  6.1 4.1 %collective-permute-done.up_one.row_one = f32[51,8,128]{2,1,0:T(8,128)S(1)} collective-permute-done((f32[51,8,128]{2,1,0:T(8,128)S(1)}, f32[51,8,128]{2,1,0:T(8,128)S(1)}, u32[]{:S(2)}, u32[]{:S(2)}) %collective-permute-start) | collective-permute-done | bytes 208928 | tf_op jit(solution)/shard_map/ppermute | solution.py:795
  10.2 0.0 collective-permute-done.1.up_two.row_two
  10.2 0.4 shard_map.87
  10.6 0.0 copy-start
  10.6 3.5 %collective-permute-start.2 = (f32[34,2,8,128]{3,2,1,0:T(8,128)S(1)}, f32[34,2,8,128]{3,2,1,0:T(8,128)S(1)}, u32[]{:S(2)}, u32[]{:S(2)}) collective-permute-start(f32[34,2,8,128]{3,2,1,0:T(8,128)S(1)} %get-tuple-element.43), channel_id=1, source_target_pairs={{0,1},{1,0},{2,3},{3,2},{4,5},{5,4},{6,7},{7,6},{8,9},{9,8},{10,11... | collective-permute-start | bytes 835592 | tf_op jit(solution)/shard_map/ppermute | solution.py:795
  14.1 5.1 %collective-permute-start.3 = (f32[34,2,8,128]{3,2,1,0:T(8,128)S(1)}, f32[34,2,8,128]{3,2,1,0:T(8,128)S(1)}, u32[]{:S(2)}, u32[]{:S(2)}) collective-permute-start(f32[34,2,8,128]{3,2,1,0:T(8,128)S(1)} %get-tuple-element.44), channel_id=1, source_target_pairs={{1,2},{2,1},{3,4},{4,3},{5,6},{6,5},{7,8},{8,7},{9,10},{10,9},{11,... | collective-permute-start | bytes 835592 | tf_op jit(solution)/shard_map/ppermute | solution.py:795
  19.2 0.0 collective-permute-done.2.one
  19.2 4.2 %collective-permute-done.3.two = f32[34,2,8,128]{3,2,1,0:T(8,128)S(1)} collective-permute-done((f32[34,2,8,128]{3,2,1,0:T(8,128)S(1)}, f32[34,2,8,128]{3,2,1,0:T(8,128)S(1)}, u32[]{:S(2)}, u32[]{:S(2)}) %collective-permute-start.3) | collective-permute-done | bytes 278560 | tf_op jit(solution)/shard_map/ppermute | solution.py:795
  23.4 0.0 copy-done
  23.4 5.4 %shard_map.88 = (f32[4,8,4,16,128]{4,3,2,1,0:T(8,128)}, f32[4,8,4,16,128]{4,3,2,1,0:T(8,128)}, f32[8,4,16,128]{3,2,1,0:T(8,128)}, f32[8,4,16,128]{3,2,1,0:T(8,12...) custom-call(f32[4,4]{1,0:T(4,128)S(1)} %copy-done, ...), custom_call_target="tpu_custom_call" | custom-call | tf_op jit(solution)/shard_map/pallas_call | solution.py:779
  28.8 0.0 copy-start.3
  28.8 14.1 %all-to-all-start = ((f32[32,3,8,128]{3,2,1,0:T(8,128)}), f32[32,3,8,128]{3,2,1,0:T(8,128)S(1)}, u32[]{:S(2)}, u32[]{:S(2)}) async-start(f32[32,3,8,128]{3,2,1,0:T(8,128)} %get-tuple-element.45), calls=%async_computation | async-start | bytes 786432 | tf_op jit(solution)/shard_map/all_to_all | solution.py:844
  43.0 0.0 copy-done.3
  43.0 0.7 collective-permute-start.5
  43.6 5.6 %collective-permute-start.4 = (f32[30,8,128]{2,1,0:T(8,128)S(1)}, f32[30,8,128]{2,1,0:T(8,128)S(1)}, u32[]{:S(2)}, u32[]{:S(2)}) collective-permute-start(f32[30,8,128]{2,1,0:T(8,128)S(1)} %copy-done.3), channel_id=1, source_target_pairs={{0,16},{16,0},{32,48},{48,32},{64,80},{80,64},{96,112},{112,96},{1... | collective-permute-start | bytes 368648 | tf_op jit(solution)/shard_map/ppermute | solution.py:795
  49.2 0.0 collective-permute-done.5.refs_13_
  49.2 0.0 copy-start.1
  49.2 5.0 %collective-permute-done.4.refs_12_ = f32[30,8,128]{2,1,0:T(8,128)S(1)} collective-permute-done((f32[30,8,128]{2,1,0:T(8,128)S(1)}, f32[30,8,128]{2,1,0:T(8,128)S(1)}, u32[]{:S(2)}, u32[]{:S(2)}) %collective-permute-start.4) | collective-permute-done | bytes 122912 | tf_op jit(solution)/shard_map/ppermute | solution.py:795
  54.2 3.8 %all-to-all-done.gathered.statics = f32[32,3,8,128]{3,2,1,0:T(8,128)S(1)} async-done(((f32[32,3,8,128]{3,2,1,0:T(8,128)}), f32[32,3,8,128]{3,2,1,0:T(8,128)S(1)}, u32[]{:S(2)}, u32[]{:S(2)}) %all-to-all-start) | async-done | bytes 393248 | tf_op jit(solution)/shard_map/all_to_all | solution.py:844
  58.0 0.0 copy-done.1
  58.0 0.0 copy-done.2
  58.0 8.3 %shard_map.89 = (f32[4,8,4,16,128]{4,3,2,1,0:T(8,128)S(1)}, f32[8,4,16,128]{3,2,1,0:T(8,128)S(1)}, f32[4,8,4,16,128]{4,3,2,1,0:T(8,128)S(1)}, f32[8,4,16,128]{3,...) custom-call(f32[4,4]{1,0:T(4,128)S(1)} %copy-done, ...), custom_call_target="tpu_custom_call" | custom-call | tf_op jit(solution)/shard_map/pallas_call | solution.py:779
  66.2 1.9 %collective-permute-start.6 = (f32[22,2,8,128]{3,2,1,0:T(8,128)S(1)}, f32[22,2,8,128]{3,2,1,0:T(8,128)S(1)}, u32[]{:S(2)}, u32[]{:S(2)}) collective-permute-start(f32[22,2,8,128]{3,2,1,0:T(8,128)S(1)} %get-tuple-element.60), channel_id=1, source_target_pairs={{0,1},{1,0},{2,3},{3,2},{4,5},{5,4},{6,7},{7,6},{8,9},{9,8},{10,11... | collective-permute-start | bytes 540680 | tf_op jit(solution)/shard_map/ppermute | solution.py:795
  68.2 6.4 %collective-permute-start.7 = (f32[22,2,8,128]{3,2,1,0:T(8,128)S(1)}, f32[22,2,8,128]{3,2,1,0:T(8,128)S(1)}, u32[]{:S(2)}, u32[]{:S(2)}) collective-permute-start(f32[22,2,8,128]{3,2,1,0:T(8,128)S(1)} %get-tuple-element.61), channel_id=1, source_target_pairs={{1,2},{2,1},{3,4},{4,3},{5,6},{6,5},{7,8},{8,7},{9,10},{10,9},{11,... | collective-permute-start | bytes 540680 | tf_op jit(solution)/shard_map/ppermute | solution.py:795
  74.6 0.0 collective-permute-done.6.one
  74.6 3.0 %collective-permute-done.7.two = f32[22,2,8,128]{3,2,1,0:T(8,128)S(1)} collective-permute-done((f32[22,2,8,128]{3,2,1,0:T(8,128)S(1)}, f32[22,2,8,128]{3,2,1,0:T(8,128)S(1)}, u32[]{:S(2)}, u32[]{:S(2)}) %collective-permute-start.7) | collective-permute-done | bytes 180256 | tf_op jit(solution)/shard_map/ppermute | solution.py:795
  77.5 3.5 %shard_map.90 = (f32[4,8,4,16,128]{4,3,2,1,0:T(8,128)S(1)}, f32[4,4,2,16,128]{4,3,2,1,0:T(8,128)S(1)}, f32[4,4,2,16,128]{4,3,2,1,0:T(8,128)S(1)}, f32[4,2,1,16,1...) custom-call(f32[4,4]{1,0:T(4,128)S(1)} %copy-done, ...), custom_call_target="tpu_custom_call" | custom-call | tf_op jit(solution)/shard_map/pallas_call | solution.py:779
  81.1 18.0 %all_to_all.10.gathered = f32[32,2,8,128]{3,2,1,0:T(8,128)S(1)} all-to-all(f32[32,2,8,128]{3,2,1,0:T(8,128)S(1)} %get-tuple-element.72), channel_id=1, replica_groups=mesh['gx'=32,'gy'=16] {'gx'}, dimensions={0} | all-to-all | bytes 524288 | tf_op jit(solution)/shard_map/all_to_all | solution.py:872
  99.0 5.3 %shard_map.91 = (f32[4,64,256]{2,1,0:T(8,128)}, f32[4,64,256]{2,1,0:T(8,128)}) custom-call(f32[4,4]{1,0:T(4,128)S(1)} %copy-done, f32[32,2,8,128]{3,2,1,0:T(8,128)S(1)} %all_to_all.10.gathered, f32[32,3,8,128]{3,2,1,0:T(8,128)S(1)} %all-to-all-done.gathered.statics, f32[4,8,4,16,128]{4,3,2,1,0:T(8,128)S(1)} %get-tuple-element.73.x0i, ...), custom_call_target="tpu_custom_call" | custom-call | tf_op jit(solution)/shard_map/pallas_call | solution.py:779
  (1 shorter events, 0.0 us)
Async XLA Ops:
  2.3 7.9 %collective-permute-start = (f32[51,8,128]{2,1,0:T(8,128)S(1)}, f32[51,8,128]{2,1,0:T(8,128)S(1)}, u32[]{:S(2)}, u32[]{:S(2)}) collective-permute-start(f32[51,8,128]{2,1,0:T(8,128)S(1)} %get-tuple-element.41), channel_id=1, source_target_pairs={{0,16},{16,0},{32,48},{48,32},{64,80},{80,64},{96,112},{112,96},{1... | collective-permute-start | bytes 626696 | tf_op jit(solution)/shard_map/ppermute | solution.py:795
  5.4 4.8 %collective-permute-start.1 = (f32[51,8,128]{2,1,0:T(8,128)S(1)}, f32[51,8,128]{2,1,0:T(8,128)S(1)}, u32[]{:S(2)}, u32[]{:S(2)}) collective-permute-start(f32[51,8,128]{2,1,0:T(8,128)S(1)} %get-tuple-element.42), channel_id=1, source_target_pairs={{16,32},{32,16},{48,64},{64,48},{80,96},{96,80},{112,128},{128,112... | collective-permute-start | bytes 626696 | tf_op jit(solution)/shard_map/ppermute | solution.py:795
  10.6 12.8 %copy-start = (f32[4,4]{1,0:T(4,128)S(1)}, f32[4,4]{1,0:T(4,128)}, u32[]{:S(2)}) copy-start(f32[4,4]{1,0:T(4,128)} %K.7) | copy-start | bytes 196
  10.6 8.6 %collective-permute-start.2 = (f32[34,2,8,128]{3,2,1,0:T(8,128)S(1)}, f32[34,2,8,128]{3,2,1,0:T(8,128)S(1)}, u32[]{:S(2)}, u32[]{:S(2)}) collective-permute-start(f32[34,2,8,128]{3,2,1,0:T(8,128)S(1)} %get-tuple-element.43), channel_id=1, source_target_pairs={{0,1},{1,0},{2,3},{3,2},{4,5},{5,4},{6,7},{7,6},{8,9},{9,8},{10,11... | collective-permute-start | bytes 835592 | tf_op jit(solution)/shard_map/ppermute | solution.py:795
  14.1 9.3 %collective-permute-start.3 = (f32[34,2,8,128]{3,2,1,0:T(8,128)S(1)}, f32[34,2,8,128]{3,2,1,0:T(8,128)S(1)}, u32[]{:S(2)}, u32[]{:S(2)}) collective-permute-start(f32[34,2,8,128]{3,2,1,0:T(8,128)S(1)} %get-tuple-element.44), channel_id=1, source_target_pairs={{1,2},{2,1},{3,4},{4,3},{5,6},{6,5},{7,8},{8,7},{9,10},{10,9},{11,... | collective-permute-start | bytes 835592 | tf_op jit(solution)/shard_map/ppermute | solution.py:795
  28.8 14.1 %copy-start.3 = (f32[30,8,128]{2,1,0:T(8,128)S(1)}, f32[30,8,128]{2,1,0:T(8,128)}, u32[]{:S(2)}) copy-start(f32[30,8,128]{2,1,0:T(8,128)} %get-tuple-element.58) | copy-start | bytes 368644
  28.8 29.1 %all-to-all-start = ((f32[32,3,8,128]{3,2,1,0:T(8,128)}), f32[32,3,8,128]{3,2,1,0:T(8,128)S(1)}, u32[]{:S(2)}, u32[]{:S(2)}) async-start(f32[32,3,8,128]{3,2,1,0:T(8,128)} %get-tuple-element.45), calls=%async_computation | async-start | bytes 786432 | tf_op jit(solution)/shard_map/all_to_all | solution.py:844
  43.0 6.2 %collective-permute-start.5 = (f32[30,8,128]{2,1,0:T(8,128)S(1)}, f32[30,8,128]{2,1,0:T(8,128)S(1)}, u32[]{:S(2)}, u32[]{:S(2)}) collective-permute-start(f32[30,8,128]{2,1,0:T(8,128)S(1)} %copy-done.3), channel_id=1, source_target_pairs={{16,32},{32,16},{48,64},{64,48},{80,96},{96,80},{112,128},{128,112... | collective-permute-start | bytes 368648 | tf_op jit(solution)/shard_map/ppermute | solution.py:795
  43.6 10.6 %collective-permute-start.4 = (f32[30,8,128]{2,1,0:T(8,128)S(1)}, f32[30,8,128]{2,1,0:T(8,128)S(1)}, u32[]{:S(2)}, u32[]{:S(2)}) collective-permute-start(f32[30,8,128]{2,1,0:T(8,128)S(1)} %copy-done.3), channel_id=1, source_target_pairs={{0,16},{16,0},{32,48},{48,32},{64,80},{80,64},{96,112},{112,96},{1... | collective-permute-start | bytes 368648 | tf_op jit(solution)/shard_map/ppermute | solution.py:795
  49.2 8.7 %copy-start.1 = (f32[30,8,128]{2,1,0:T(8,128)}, f32[30,8,128]{2,1,0:T(8,128)S(1)}, u32[]{:S(2)}) copy-start(f32[30,8,128]{2,1,0:T(8,128)S(1)} %collective-permute-done.5.refs_13_) | copy-start | bytes 368644
  54.2 3.8 %copy-start.2 = (f32[30,8,128]{2,1,0:T(8,128)}, f32[30,8,128]{2,1,0:T(8,128)S(1)}, u32[]{:S(2)}) copy-start(f32[30,8,128]{2,1,0:T(8,128)S(1)} %collective-permute-done.4.refs_12_) | copy-start | bytes 368644
  66.2 8.3 %collective-permute-start.6 = (f32[22,2,8,128]{3,2,1,0:T(8,128)S(1)}, f32[22,2,8,128]{3,2,1,0:T(8,128)S(1)}, u32[]{:S(2)}, u32[]{:S(2)}) collective-permute-start(f32[22,2,8,128]{3,2,1,0:T(8,128)S(1)} %get-tuple-element.60), channel_id=1, source_target_pairs={{0,1},{1,0},{2,3},{3,2},{4,5},{5,4},{6,7},{7,6},{8,9},{9,8},{10,11... | collective-permute-start | bytes 540680 | tf_op jit(solution)/shard_map/ppermute | solution.py:795
  68.2 9.4 %collective-permute-start.7 = (f32[22,2,8,128]{3,2,1,0:T(8,128)S(1)}, f32[22,2,8,128]{3,2,1,0:T(8,128)S(1)}, u32[]{:S(2)}, u32[]{:S(2)}) collective-permute-start(f32[22,2,8,128]{3,2,1,0:T(8,128)S(1)} %get-tuple-element.61), channel_id=1, source_target_pairs={{1,2},{2,1},{3,4},{4,3},{5,6},{6,5},{7,8},{8,7},{9,10},{10,9},{11,... | collective-permute-start | bytes 540680 | tf_op jit(solution)/shard_map/ppermute | solution.py:795

commit v7 on v6

--- a/solution.py
+++ b/solution.py
@@ -668,7 +668,7 @@
     refs = refs[KEPT + 5 :]
     here, refs = kept + refs[: GIVEN - KEPT], refs[GIVEN - KEPT :]
     x1, r1, s1, m1, i1, x2, r2, s2, m2, i2, ma0, mb0, ma1, mb1, ma2, mb2 = refs[:16]
-    natural, x3, ma3, mb3, r3, m3, s3, i3, wide, correct, arrived = refs[16:]
+    natural, x3, ma3, mb3, r3, m3, s3, i3, wide, correct, pairs, arrived = refs[16:]
     moves = [
         pltpu.make_async_copy(there[n], here[n], arrived.at[n]) for n in range(GIVEN)
     ]
@@ -696,19 +696,22 @@
         move.wait()
     rise(0, K, X, M, RHS, SOLID, INV, source, True)
 
-    def pick(index, v):
-        f, q, h = index // 16, index // 2 % 8, index % 2
-        part = slice(8 * v, 8 * v + 8)
-        return half_pair(x0[f, q, 2 * h, part], x0[f, q, 2 * h + 1, part])
-
-    pack_sides(pick, XTILES, one, two, is_even("gy"))
+    for f in range(F):
+        for q in range(8):
+            for h in range(2):
+                for v in range(2):
+                    part = slice(8 * v, 8 * v + 8)
+                    pairs[f * 16 + q * 2 + h, v] = half_pair(
+                        x0[f, q, 2 * h, part], x0[f, q, 2 * h + 1, part]
+                    )
+    pack_sides(lambda index, v: pairs[index, v], XTILES, one, two, is_even("gy"))
 
 
 def up_two(
     K, gathered, statics, x0i, r0, s0, m0, i0, x1i, r1, m1, i1, x2i, r2, m2, i2,
     displacement, residual,
     x0, x1, x2, ma0, mb0, ma1, mb1, ma2, mb2,
-    natural, x3, ma3, mb3, r3, m3, s3, i3, wide, correct, stage,
+    natural, x3, ma3, mb3, r3, m3, s3, i3, wide, correct, stage, rest,
 ):
     copy_state((x0i, x1i, x2i), (x0, x1, x2))
     solve_coarsest(K, gathered, statics, natural, x3, ma3, mb3, r3, m3, s3, i3, wide, correct)
@@ -716,15 +719,18 @@
     ascend(K, (x0, x1, x2), M, (r0, r1, r2), (m0, m1, m2), (i0, i1, i2), correct)
     mine = slice(0, 8)
     for q in range(8):
-        for h in range(2):
-            outs = []
-            for p in (2 * h, 2 * h + 1):
-                drives, xs = drive(0, K, x0, ma0, r0, m0, q, p, mine)
-                s = s0[q, p, mine]
-                rest = [drives[f] - (s + (4.0 + K[f, f])) * xs[f] for f in range(F)]
-                outs.append(xs + rest)
-            for a in range(2 * F):
-                stage[a, h, pl.ds(q, 8, stride=8), :] = half_pair(outs[0][a], outs[1][a])
+        for p in range(4):
+            drives, xs = drive(0, K, x0, ma0, r0, m0, q, p, mine)
+            s = s0[q, p, mine]
+            for f in range(F):
+                rest[f, q, p] = drives[f] - (s + (4.0 + K[f, f])) * xs[f]
+    for f in range(F):
+        for q in range(8):
+            for h in range(2):
+                for a, v in ((f, x0), (F + f, rest)):
+                    stage[a, h, pl.ds(q, 8, stride=8), :] = half_pair(
+                        v[f, q, 2 * h, mine], v[f, q, 2 * h + 1, mine]
+                    )
     matrix = join_matrix(256, 4)
     for f in range(F):
         for out, a in ((displacement, f), (residual, F + f)):
@@ -858,7 +864,7 @@
         + tall
         + masked_scratch(24)
         + coarsest_scratch(blocks, 24)
-        + [pltpu.SemaphoreType.DMA((GIVEN,))],
+        + [pltpu.VMEM((XTILES, 2, 8, 128), F32), pltpu.SemaphoreType.DMA((GIVEN,))],
         (coupling, statics) + given,
         hbm=GIVEN,
     )
@@ -874,7 +880,7 @@
         up_two,
         [sds(F, 64, 256), sds(F, 64, 256)],
         inner + masked_scratch() + coarsest_scratch(blocks)
-        + [pltpu.VMEM((2 * F, 2, 64, 128), F32)],
+        + [pltpu.VMEM((2 * F, 2, 64, 128), F32), pltpu.VMEM((F, 8, 4, 8, 128), F32)],
         (coupling, gathered, statics, x0, r0, s0, m0, i0, x1, r1, m1, i1, x2, r2, m2, i2),
     )
     return displacement, residual

time: 105 us -> 103 us (0.981)
  Pallas kernels: 24.5 us -> 22.3 us
    pallas_call x6, Pallas kernels: 24.5 us -> 22.3 us  [call(): pl.pallas_call(body, out_shape=outs, in_specs=specs, out_specs=[pl.BlockS...]
where the time goes in v7:
time: 103 us; the launch traced here: 102 us
  starting transfers between devices  41 us (40%)
  Pallas kernels  22.3 us (22%)
  waiting for transfers between devices  20 us (19%)
  blocking collectives  18 us (17%)
    ppermute x8, starting transfers between devices, swap(): return (lax.ppermute(first, axis, near), lax.ppermute(second, axis, far))  26.9 us
    pallas_call x6, Pallas kernels, call(): pl.pallas_call(body, out_shape=outs, in_specs=specs, out_specs=[pl.BlockS...  22.3 us
    all_to_all x1, blocking collectives, shards(): gathered = lax.all_to_all(payload, 'gx', 0, 0)  18 us
    ppermute x8, waiting for transfers between devices, swap(): return (lax.ppermute(first, axis, near), lax.ppermute(second, axis, far))  16.3 us
    all_to_all x1, starting transfers between devices, shards(): statics = lax.all_to_all(payload, 'gx', 0, 0)  14.1 us
    all_to_all x1, waiting for transfers between devices, shards(): statics = lax.all_to_all(payload, 'gx', 0, 0)  3.77 us
  transfers between devices with their start and end apart: 9, of which 5 were waited for; matrix products, arithmetic and copies ran while one was open for 0% of the time, Pallas kernels for 0%

profile of v7, /device:TPU:193, one launch (start us, length us, event | category | flops | bytes accessed | tf_op | source)
XLA Modules:
  0.0 102.1 jit_solution(6266425720330547660)
XLA Ops:
  0.6 1.7 %shard_map.86 = (f32[102,8,128]{2,1,0:T(8,128)S(1)}, f32[51,8,128]{2,1,0:T(8,128)S(1)}, f32[51,8,128]{2,1,0:T(8,128)S(1)}) custom-call(f32[4,64,256]{2,1,0:T(8,128)} %source_in.1, f32[64,256]{1,0:T(8,128)} %reaction_in.1, s32[64,256]{1,0:T(8,128)} %solid0_in.1, s32[32,128]{1,0:T(8,128)} %solid1_in.1, s32[16,64]{1,0:T(8,128)} %solid2_in.1, s32[8,32]{1,0:T(8,128)} %solid3_in.1), custom_call_target="tpu_custom_call" | custom-call | tf_op jit(solution)/shard_map/pallas_call | solution.py:785
  2.3 3.1 %collective-permute-start = (f32[51,8,128]{2,1,0:T(8,128)S(1)}, f32[51,8,128]{2,1,0:T(8,128)S(1)}, u32[]{:S(2)}, u32[]{:S(2)}) collective-permute-start(f32[51,8,128]{2,1,0:T(8,128)S(1)} %get-tuple-element.41), channel_id=1, source_target_pairs={{0,16},{16,0},{32,48},{48,32},{64,80},{80,64},{96,112},{112,96},{1... | collective-permute-start | bytes 626696 | tf_op jit(solution)/shard_map/ppermute | solution.py:801
  5.4 0.7 collective-permute-start.1
  6.1 4.1 %collective-permute-done.up_one.row_one = f32[51,8,128]{2,1,0:T(8,128)S(1)} collective-permute-done((f32[51,8,128]{2,1,0:T(8,128)S(1)}, f32[51,8,128]{2,1,0:T(8,128)S(1)}, u32[]{:S(2)}, u32[]{:S(2)}) %collective-permute-start) | collective-permute-done | bytes 208928 | tf_op jit(solution)/shard_map/ppermute | solution.py:801
  10.2 0.0 collective-permute-done.1.up_two.row_two
  10.2 0.4 shard_map.87
  10.6 0.0 copy-start
  10.6 3.5 %collective-permute-start.2 = (f32[34,2,8,128]{3,2,1,0:T(8,128)S(1)}, f32[34,2,8,128]{3,2,1,0:T(8,128)S(1)}, u32[]{:S(2)}, u32[]{:S(2)}) collective-permute-start(f32[34,2,8,128]{3,2,1,0:T(8,128)S(1)} %get-tuple-element.43), channel_id=1, source_target_pairs={{0,1},{1,0},{2,3},{3,2},{4,5},{5,4},{6,7},{7,6},{8,9},{9,8},{10,11... | collective-permute-start | bytes 835592 | tf_op jit(solution)/shard_map/ppermute | solution.py:801
  14.1 5.1 %collective-permute-start.3 = (f32[34,2,8,128]{3,2,1,0:T(8,128)S(1)}, f32[34,2,8,128]{3,2,1,0:T(8,128)S(1)}, u32[]{:S(2)}, u32[]{:S(2)}) collective-permute-start(f32[34,2,8,128]{3,2,1,0:T(8,128)S(1)} %get-tuple-element.44), channel_id=1, source_target_pairs={{1,2},{2,1},{3,4},{4,3},{5,6},{6,5},{7,8},{8,7},{9,10},{10,9},{11,... | collective-permute-start | bytes 835592 | tf_op jit(solution)/shard_map/ppermute | solution.py:801
  19.2 0.0 collective-permute-done.2.one
  19.2 4.2 %collective-permute-done.3.two = f32[34,2,8,128]{3,2,1,0:T(8,128)S(1)} collective-permute-done((f32[34,2,8,128]{3,2,1,0:T(8,128)S(1)}, f32[34,2,8,128]{3,2,1,0:T(8,128)S(1)}, u32[]{:S(2)}, u32[]{:S(2)}) %collective-permute-start.3) | collective-permute-done | bytes 278560 | tf_op jit(solution)/shard_map/ppermute | solution.py:801
  23.4 0.0 copy-done
  23.4 5.4 %shard_map.88 = (f32[4,8,4,16,128]{4,3,2,1,0:T(8,128)}, f32[4,8,4,16,128]{4,3,2,1,0:T(8,128)}, f32[8,4,16,128]{3,2,1,0:T(8,128)}, f32[8,4,16,128]{3,2,1,0:T(8,12...) custom-call(f32[4,4]{1,0:T(4,128)S(1)} %copy-done, ...), custom_call_target="tpu_custom_call" | custom-call | tf_op jit(solution)/shard_map/pallas_call | solution.py:785
  28.8 0.0 copy-start.3
  28.8 14.1 %all-to-all-start = ((f32[32,3,8,128]{3,2,1,0:T(8,128)}), f32[32,3,8,128]{3,2,1,0:T(8,128)S(1)}, u32[]{:S(2)}, u32[]{:S(2)}) async-start(f32[32,3,8,128]{3,2,1,0:T(8,128)} %get-tuple-element.45), calls=%async_computation | async-start | bytes 786432 | tf_op jit(solution)/shard_map/all_to_all | solution.py:850
  43.0 0.0 copy-done.3
  43.0 0.7 collective-permute-start.5
  43.6 5.6 %collective-permute-start.4 = (f32[30,8,128]{2,1,0:T(8,128)S(1)}, f32[30,8,128]{2,1,0:T(8,128)S(1)}, u32[]{:S(2)}, u32[]{:S(2)}) collective-permute-start(f32[30,8,128]{2,1,0:T(8,128)S(1)} %copy-done.3), channel_id=1, source_target_pairs={{0,16},{16,0},{32,48},{48,32},{64,80},{80,64},{96,112},{112,96},{1... | collective-permute-start | bytes 368648 | tf_op jit(solution)/shard_map/ppermute | solution.py:801
  49.2 0.0 collective-permute-done.5.refs_13_
  49.2 0.0 copy-start.1
  49.2 5.0 %collective-permute-done.4.refs_12_ = f32[30,8,128]{2,1,0:T(8,128)S(1)} collective-permute-done((f32[30,8,128]{2,1,0:T(8,128)S(1)}, f32[30,8,128]{2,1,0:T(8,128)S(1)}, u32[]{:S(2)}, u32[]{:S(2)}) %collective-permute-start.4) | collective-permute-done | bytes 122912 | tf_op jit(solution)/shard_map/ppermute | solution.py:801
  54.2 3.8 %all-to-all-done.gathered.statics = f32[32,3,8,128]{3,2,1,0:T(8,128)S(1)} async-done(((f32[32,3,8,128]{3,2,1,0:T(8,128)}), f32[32,3,8,128]{3,2,1,0:T(8,128)S(1)}, u32[]{:S(2)}, u32[]{:S(2)}) %all-to-all-start) | async-done | bytes 393248 | tf_op jit(solution)/shard_map/all_to_all | solution.py:850
  58.0 0.0 copy-done.1
  58.0 0.0 copy-done.2
  58.0 6.1 %shard_map.89 = (f32[4,8,4,16,128]{4,3,2,1,0:T(8,128)S(1)}, f32[8,4,16,128]{3,2,1,0:T(8,128)S(1)}, f32[4,8,4,16,128]{4,3,2,1,0:T(8,128)S(1)}, f32[8,4,16,128]{3,...) custom-call(f32[4,4]{1,0:T(4,128)S(1)} %copy-done, ...), custom_call_target="tpu_custom_call" | custom-call | tf_op jit(solution)/shard_map/pallas_call | solution.py:785
  64.1 1.9 %collective-permute-start.6 = (f32[22,2,8,128]{3,2,1,0:T(8,128)S(1)}, f32[22,2,8,128]{3,2,1,0:T(8,128)S(1)}, u32[]{:S(2)}, u32[]{:S(2)}) collective-permute-start(f32[22,2,8,128]{3,2,1,0:T(8,128)S(1)} %get-tuple-element.60), channel_id=1, source_target_pairs={{0,1},{1,0},{2,3},{3,2},{4,5},{5,4},{6,7},{7,6},{8,9},{9,8},{10,11... | collective-permute-start | bytes 540680 | tf_op jit(solution)/shard_map/ppermute | solution.py:801
  66.0 6.4 %collective-permute-start.7 = (f32[22,2,8,128]{3,2,1,0:T(8,128)S(1)}, f32[22,2,8,128]{3,2,1,0:T(8,128)S(1)}, u32[]{:S(2)}, u32[]{:S(2)}) collective-permute-start(f32[22,2,8,128]{3,2,1,0:T(8,128)S(1)} %get-tuple-element.61), channel_id=1, source_target_pairs={{1,2},{2,1},{3,4},{4,3},{5,6},{6,5},{7,8},{8,7},{9,10},{10,9},{11,... | collective-permute-start | bytes 540680 | tf_op jit(solution)/shard_map/ppermute | solution.py:801
  72.4 0.0 collective-permute-done.6.one
  72.4 3.0 %collective-permute-done.7.two = f32[22,2,8,128]{3,2,1,0:T(8,128)S(1)} collective-permute-done((f32[22,2,8,128]{3,2,1,0:T(8,128)S(1)}, f32[22,2,8,128]{3,2,1,0:T(8,128)S(1)}, u32[]{:S(2)}, u32[]{:S(2)}) %collective-permute-start.7) | collective-permute-done | bytes 180256 | tf_op jit(solution)/shard_map/ppermute | solution.py:801
  75.4 3.5 %shard_map.90 = (f32[4,8,4,16,128]{4,3,2,1,0:T(8,128)S(1)}, f32[4,4,2,16,128]{4,3,2,1,0:T(8,128)S(1)}, f32[4,4,2,16,128]{4,3,2,1,0:T(8,128)S(1)}, f32[4,2,1,16,1...) custom-call(f32[4,4]{1,0:T(4,128)S(1)} %copy-done, ...), custom_call_target="tpu_custom_call" | custom-call | tf_op jit(solution)/shard_map/pallas_call | solution.py:785
  78.9 18.0 %all_to_all.10.gathered = f32[32,2,8,128]{3,2,1,0:T(8,128)S(1)} all-to-all(f32[32,2,8,128]{3,2,1,0:T(8,128)S(1)} %get-tuple-element.72), channel_id=1, replica_groups=mesh['gx'=32,'gy'=16] {'gx'}, dimensions={0} | all-to-all | bytes 524288 | tf_op jit(solution)/shard_map/all_to_all | solution.py:878
  96.9 5.2 %shard_map.91 = (f32[4,64,256]{2,1,0:T(8,128)}, f32[4,64,256]{2,1,0:T(8,128)}) custom-call(f32[4,4]{1,0:T(4,128)S(1)} %copy-done, f32[32,2,8,128]{3,2,1,0:T(8,128)S(1)} %all_to_all.10.gathered, f32[32,3,8,128]{3,2,1,0:T(8,128)S(1)} %all-to-all-done.gathered.statics, f32[4,8,4,16,128]{4,3,2,1,0:T(8,128)S(1)} %get-tuple-element.73.x0i, ...), custom_call_target="tpu_custom_call" | custom-call | tf_op jit(solution)/shard_map/pallas_call | solution.py:785
  (1 shorter events, 0.0 us)
Async XLA Ops:
  2.3 7.9 %collective-permute-start = (f32[51,8,128]{2,1,0:T(8,128)S(1)}, f32[51,8,128]{2,1,0:T(8,128)S(1)}, u32[]{:S(2)}, u32[]{:S(2)}) collective-permute-start(f32[51,8,128]{2,1,0:T(8,128)S(1)} %get-tuple-element.41), channel_id=1, source_target_pairs={{0,16},{16,0},{32,48},{48,32},{64,80},{80,64},{96,112},{112,96},{1... | collective-permute-start | bytes 626696 | tf_op jit(solution)/shard_map/ppermute | solution.py:801
  5.4 4.8 %collective-permute-start.1 = (f32[51,8,128]{2,1,0:T(8,128)S(1)}, f32[51,8,128]{2,1,0:T(8,128)S(1)}, u32[]{:S(2)}, u32[]{:S(2)}) collective-permute-start(f32[51,8,128]{2,1,0:T(8,128)S(1)} %get-tuple-element.42), channel_id=1, source_target_pairs={{16,32},{32,16},{48,64},{64,48},{80,96},{96,80},{112,128},{128,112... | collective-permute-start | bytes 626696 | tf_op jit(solution)/shard_map/ppermute | solution.py:801
  10.6 12.8 %copy-start = (f32[4,4]{1,0:T(4,128)S(1)}, f32[4,4]{1,0:T(4,128)}, u32[]{:S(2)}) copy-start(f32[4,4]{1,0:T(4,128)} %K.7) | copy-start | bytes 196
  10.6 8.6 %collective-permute-start.2 = (f32[34,2,8,128]{3,2,1,0:T(8,128)S(1)}, f32[34,2,8,128]{3,2,1,0:T(8,128)S(1)}, u32[]{:S(2)}, u32[]{:S(2)}) collective-permute-start(f32[34,2,8,128]{3,2,1,0:T(8,128)S(1)} %get-tuple-element.43), channel_id=1, source_target_pairs={{0,1},{1,0},{2,3},{3,2},{4,5},{5,4},{6,7},{7,6},{8,9},{9,8},{10,11... | collective-permute-start | bytes 835592 | tf_op jit(solution)/shard_map/ppermute | solution.py:801
  14.1 9.3 %collective-permute-start.3 = (f32[34,2,8,128]{3,2,1,0:T(8,128)S(1)}, f32[34,2,8,128]{3,2,1,0:T(8,128)S(1)}, u32[]{:S(2)}, u32[]{:S(2)}) collective-permute-start(f32[34,2,8,128]{3,2,1,0:T(8,128)S(1)} %get-tuple-element.44), channel_id=1, source_target_pairs={{1,2},{2,1},{3,4},{4,3},{5,6},{6,5},{7,8},{8,7},{9,10},{10,9},{11,... | collective-permute-start | bytes 835592 | tf_op jit(solution)/shard_map/ppermute | solution.py:801
  28.8 14.1 %copy-start.3 = (f32[30,8,128]{2,1,0:T(8,128)S(1)}, f32[30,8,128]{2,1,0:T(8,128)}, u32[]{:S(2)}) copy-start(f32[30,8,128]{2,1,0:T(8,128)} %get-tuple-element.58) | copy-start | bytes 368644
  28.8 29.1 %all-to-all-start = ((f32[32,3,8,128]{3,2,1,0:T(8,128)}), f32[32,3,8,128]{3,2,1,0:T(8,128)S(1)}, u32[]{:S(2)}, u32[]{:S(2)}) async-start(f32[32,3,8,128]{3,2,1,0:T(8,128)} %get-tuple-element.45), calls=%async_computation | async-start | bytes 786432 | tf_op jit(solution)/shard_map/all_to_all | solution.py:850
  43.0 6.2 %collective-permute-start.5 = (f32[30,8,128]{2,1,0:T(8,128)S(1)}, f32[30,8,128]{2,1,0:T(8,128)S(1)}, u32[]{:S(2)}, u32[]{:S(2)}) collective-permute-start(f32[30,8,128]{2,1,0:T(8,128)S(1)} %copy-done.3), channel_id=1, source_target_pairs={{16,32},{32,16},{48,64},{64,48},{80,96},{96,80},{112,128},{128,112... | collective-permute-start | bytes 368648 | tf_op jit(solution)/shard_map/ppermute | solution.py:801
  43.6 10.6 %collective-permute-start.4 = (f32[30,8,128]{2,1,0:T(8,128)S(1)}, f32[30,8,128]{2,1,0:T(8,128)S(1)}, u32[]{:S(2)}, u32[]{:S(2)}) collective-permute-start(f32[30,8,128]{2,1,0:T(8,128)S(1)} %copy-done.3), channel_id=1, source_target_pairs={{0,16},{16,0},{32,48},{48,32},{64,80},{80,64},{96,112},{112,96},{1... | collective-permute-start | bytes 368648 | tf_op jit(solution)/shard_map/ppermute | solution.py:801
  49.2 8.7 %copy-start.1 = (f32[30,8,128]{2,1,0:T(8,128)}, f32[30,8,128]{2,1,0:T(8,128)S(1)}, u32[]{:S(2)}) copy-start(f32[30,8,128]{2,1,0:T(8,128)S(1)} %collective-permute-done.5.refs_13_) | copy-start | bytes 368644
  54.2 3.8 %copy-start.2 = (f32[30,8,128]{2,1,0:T(8,128)}, f32[30,8,128]{2,1,0:T(8,128)S(1)}, u32[]{:S(2)}) copy-start(f32[30,8,128]{2,1,0:T(8,128)S(1)} %collective-permute-done.4.refs_12_) | copy-start | bytes 368644
  64.1 8.3 %collective-permute-start.6 = (f32[22,2,8,128]{3,2,1,0:T(8,128)S(1)}, f32[22,2,8,128]{3,2,1,0:T(8,128)S(1)}, u32[]{:S(2)}, u32[]{:S(2)}) collective-permute-start(f32[22,2,8,128]{3,2,1,0:T(8,128)S(1)} %get-tuple-element.60), channel_id=1, source_target_pairs={{0,1},{1,0},{2,3},{3,2},{4,5},{5,4},{6,7},{7,6},{8,9},{9,8},{10,11... | collective-permute-start | bytes 540680 | tf_op jit(solution)/shard_map/ppermute | solution.py:801
  66.0 9.4 %collective-permute-start.7 = (f32[22,2,8,128]{3,2,1,0:T(8,128)S(1)}, f32[22,2,8,128]{3,2,1,0:T(8,128)S(1)}, u32[]{:S(2)}, u32[]{:S(2)}) collective-permute-start(f32[22,2,8,128]{3,2,1,0:T(8,128)S(1)} %get-tuple-element.61), channel_id=1, source_target_pairs={{1,2},{2,1},{3,4},{4,3},{5,6},{6,5},{7,8},{8,7},{9,10},{10,9},{11,... | collective-permute-start | bytes 540680 | tf_op jit(solution)/shard_map/ppermute | solution.py:801
